TPU v7x, 32 devices: a whole 2x2x4 slice. The times are simulated.
32 devices in a mesh: kgrp: 4 (over x, core), band: 8 (over z, y).
Axes of the slice: x: 2, y: 2, z: 4, core: 2. Of those that a mesh axis runs over, the one named last changes fastest.
Arguments:
- orbitals: bfloat16 [4, 128, 2, 32768], P('kgrp', 'band'), may hold values from -6 to 6
- points: int32 [512], replicated, may hold values from 0 to 32767, as said below
- partner: int32 [4], replicated, may hold values from 0 to 3, each once
- coulomb: bfloat16 [512, 32768], P(None, 'band'), may hold values from -0.01171875 to 0.01171875
Outputs:
- exchange_term: bfloat16 [4, 128, 2, 32768], P('kgrp', 'band')
Inputs may be any that keep to these rules, and one draw needn't show every extreme that they name: `points`: 512 distinct grid cells; cells 0 and 32767 are always among them.
All inputs are finite; a program needn't handle non-finite values.
Results may differ from a plain program's by a relative error of at most 0.0057.
Values may be sent and summed in bfloat16 or wider, within the bound.
No kernel may reach another device: no remote copies, remote signals or barrier semaphores. Data moves between devices by JAX's collectives and lax.ppermute only.
A program may use at most 128 MiB of HBM per device.

v0:
```python
import math

import jax
import jax.numpy as jnp
import numpy as np
from jax import lax
from jax.experimental import pallas as pl
from jax.experimental.pallas import tpu as pltpu
from jax.sharding import PartitionSpec as P

GX = 32
GY = 32
GZ = 32
LANES = 128
BF16 = jnp.bfloat16
F32 = jnp.float32
VMEM_BYTES = 56 * 1024 * 1024


def round_bf16(values):
    return values.astype(BF16).astype(np.float64)


def table_scale(length):
    cosines = np.cos(2.0 * np.pi * np.arange(length // 4) / length)
    best = (np.inf, 1.0)
    for scale in np.linspace(1.0, 2.0, 8193)[:-1]:
        exact = scale * cosines
        error = float(np.max(np.abs(round_bf16(exact) / exact - 1.0)))
        best = min(best, (error, float(scale)))
    return best[1]


def plane_table(scale):
    cell = np.arange(GY * GZ)
    y, z = cell // GZ, cell % GZ
    turns = (y[:, None] * y[None, :] % GY) / GY + (z[:, None] * z[None, :] % GZ) / GZ
    angle = 2.0 * np.pi * (turns % 1.0)
    return (scale * np.stack([np.cos(angle), np.sin(angle)])).astype(BF16)


def line_table(scale, order, planes, bands):
    count = len(order)
    device = np.arange(count)[:, None, None]
    plane = np.arange(planes)[None, :, None]
    x = planes * (device ^ np.array(order)[None, None, :]) + plane
    kx = np.arange(GX)[None, :, None, None]
    angle = 2.0 * np.pi * (kx * x[:, None] % GX) / GX
    cos_t, sin_t = np.cos(angle), np.sin(angle)
    pair = np.stack([np.stack([cos_t, sin_t], -1), np.stack([-sin_t, cos_t], -1)], 2)
    table = np.zeros((count, bands, GX, 2, planes, count, bands, 2), np.float64)
    for band in range(bands):
        table[:, band, :, :, :, :, band, :] = pair
    return (scale * table).reshape(count, bands * GX * 2, planes * count * bands * 2).astype(BF16)


def turn_table(rows):
    table = np.zeros((rows, rows), np.float32)
    even = np.arange(0, rows, 2)
    table[even, even + 1] = -1.0
    table[even + 1, even] = 1.0
    return table.astype(BF16)


def dot(a, b):
    return jnp.dot(a, b, preferred_element_type=F32)


def pick_kernel(points_ref, tiles_ref, out_ref):
    rows = tiles_ref.shape[1]
    lane = lax.broadcasted_iota(jnp.int32, (rows, LANES), 1)

    @pl.loop(0, out_ref.shape[0])
    def _(group):
        def step(m, total):
            point = points_ref[group * LANES + m]
            tile = tiles_ref[point // LANES].astype(F32)
            shift = (m - point % LANES + LANES) % LANES
            return jnp.where(lane == m, pltpu.roll(tile, shift, 1), total)

        total = lax.fori_loop(0, LANES, step, jnp.zeros((rows, LANES), F32), unroll=8)
        out_ref[group] = total.astype(BF16)


def pick(tiles, points):
    groups = points.shape[0] // LANES
    rows = tiles.shape[1]
    out = pl.pallas_call(
        pick_kernel,
        in_specs=[pl.BlockSpec(memory_space=pltpu.SMEM), pl.BlockSpec(memory_space=pltpu.VMEM)],
        out_specs=pl.BlockSpec(memory_space=pltpu.VMEM),
        out_shape=jax.ShapeDtypeStruct((groups, rows, LANES), BF16),
        compiler_params=pltpu.CompilerParams(vmem_limit_bytes=VMEM_BYTES),
        name="pick_points",
    )(points, tiles)
    return out.transpose(1, 0, 2).reshape(rows, groups * LANES)


def coef_kernel(both_ref, turn_ref, own_ref, src_ref):
    count, _, rows, nu = both_ref.shape
    own = jnp.concatenate([both_ref[k, 0] for k in range(count)], axis=0)
    src = jnp.concatenate([both_ref[k, 1] for k in range(count)], axis=0)
    turn = turn_ref[...]
    own_ref[:nu] = own.astype(F32).T.astype(BF16)
    own_ref[nu:] = dot(turn, own).T.astype(BF16)
    src_ref[:, :nu] = -src
    src_ref[:, nu:] = (-dot(turn, src)).astype(BF16)


def coefficients(both, turn):
    count, _, rows, nu = both.shape
    return pl.pallas_call(
        coef_kernel,
        out_shape=(
            jax.ShapeDtypeStruct((2 * nu, count * rows), BF16),
            jax.ShapeDtypeStruct((count * rows, 2 * nu), BF16),
        ),
        compiler_params=pltpu.CompilerParams(vmem_limit_bytes=VMEM_BYTES),
        name="coefficients",
    )(both, turn)


def exchange_kernel(count, *refs):
    cells = refs[:count]
    own_ref, src_ref, coulomb_ref, table_ref, turn_ref = refs[count : count + 5]
    outs = refs[count + 5 : 2 * count + 5]
    grid_ref = refs[2 * count + 5]
    nu = coulomb_ref.shape[0]
    rows = cells[0].shape[1]
    wide = 2 * LANES
    for part in range(GY * GZ // wide):
        columns = slice(part * wide, (part + 1) * wide)
        tiles = [
            jnp.concatenate([c[2 * part + t] for c in cells], axis=0) for t in range(2)
        ]
        density = dot(own_ref[...], jnp.concatenate(tiles, axis=1))
        coulomb = coulomb_ref[:, columns].astype(F32)
        weighted = jnp.concatenate(
            [(coulomb * density[:nu]).astype(BF16), (coulomb * density[nu:]).astype(BF16)], axis=0
        )
        grid_ref[:, columns] = dot(src_ref[...], weighted).astype(BF16)
    field = grid_ref[...]
    turned = (-dot(turn_ref[...], field)).astype(BF16)
    plane = (dot(field, table_ref[0]) + dot(turned, table_ref[1])).astype(BF16)
    for k in range(count):
        outs[k][0] = plane[k * rows : (k + 1) * rows]


def exchange(cells, own, src, coulomb, table, turn, first_plane, planes):
    count = len(cells)
    rows = cells[0].shape[1]
    nu = coulomb.shape[0]
    area = GY * GZ
    tiles = area // LANES
    macs = planes * area * (2 * own.size + 2 * count * rows * area)

    def whole(array):
        return pl.BlockSpec(array.shape, lambda p: (0,) * array.ndim)

    return pl.pallas_call(
        lambda *refs: exchange_kernel(count, *refs),
        grid=(planes,),
        in_specs=[pl.BlockSpec((tiles, rows, LANES), lambda p: (p, 0, 0))] * count
        + [whole(own), whole(src), pl.BlockSpec((nu, area), lambda p: (0, first_plane + p)), whole(table), whole(turn)],
        out_specs=[pl.BlockSpec((1, rows, area), lambda p: (p, 0, 0))] * count,
        out_shape=[jax.ShapeDtypeStruct((planes, rows, area), BF16)] * count,
        scratch_shapes=[pltpu.VMEM((count * rows, area), BF16)],
        compiler_params=pltpu.CompilerParams(vmem_limit_bytes=VMEM_BYTES),
        cost_estimate=pl.CostEstimate(flops=2 * macs, bytes_accessed=12 * 2**20, transcendentals=0),
        name="exchange_planes",
    )(*cells, own, src, coulomb, table, turn)


def line_kernel(factor, group_rows, count, *refs):
    fields, table_ref, out_ref = refs[1:-2], refs[-2], refs[-1]
    start = pl.multiple_of(pl.program_id(0) * group_rows, group_rows)
    picked = [
        f[p, pl.ds(start, group_rows)]
        for c in range(0, len(fields), count)
        for p in range(fields[c].shape[0])
        for f in fields[c : c + count]
    ]
    lines = dot(table_ref[0], jnp.concatenate(picked, axis=0)) * factor
    lines = lines.astype(BF16)
    for t in range(out_ref.shape[1]):
        tile = lines[:, t * LANES : (t + 1) * LANES]
        out_ref[:, t] = tile.reshape(tile.shape[0] // 2, 2, LANES)


def line_pass(fields, table, device, factor, rows, groups, count):
    area = GY * GZ
    group_rows = rows // groups
    tiles = area // LANES
    height = rows // 2 * GX
    macs = rows * GX * area * table.shape[2]
    spec = pltpu.PrefetchScalarGridSpec(
        num_scalar_prefetch=1,
        grid=(groups,),
        in_specs=[pl.BlockSpec(f.shape, lambda g, d: (0, 0, 0)) for f in fields]
        + [pl.BlockSpec((1,) + table.shape[1:], lambda g, d: (d[0], 0, 0))],
        out_specs=pl.BlockSpec((height // groups, tiles, 2, LANES), lambda g, d: (g, 0, 0, 0)),
    )
    return pl.pallas_call(
        lambda *refs: line_kernel(factor, group_rows, count, *refs),
        grid_spec=spec,
        out_shape=jax.ShapeDtypeStruct((height, tiles, 2, LANES), BF16),
        compiler_params=pltpu.CompilerParams(vmem_limit_bytes=VMEM_BYTES),
        cost_estimate=pl.CostEstimate(flops=2 * macs, bytes_accessed=5 * 2**20, transcendentals=0),
        name="line_pass",
    )(device, *fields, table)


def hop(array, distance, count):
    return lax.ppermute(array, "band", [(i, i ^ distance) for i in range(count)])


def body(orbitals, points, partner, coulomb):
    resident = orbitals[0]
    bands, _, all_cells = resident.shape
    rows = 2 * bands
    count = lax.axis_size("band")
    me = lax.axis_index("band")
    planes = GX // count
    chunks = 2 if planes % 2 == 0 else 1
    chunk_planes = planes // chunks
    plane_tiles = GY * GZ // LANES
    chunk_tiles = chunk_planes * plane_tiles

    order = [0]
    bit = count // 2
    while bit:
        order = order + [k ^ bit for k in order]
        bit //= 2

    tiled = resident.reshape(bands, 2, all_cells // LANES, LANES).transpose(0, 2, 1, 3)

    def block(k, c):
        first = (me ^ k) * (planes * plane_tiles) + c * chunk_tiles
        part = lax.dynamic_slice_in_dim(tiled, first, chunk_tiles, 1)
        return part.transpose(1, 0, 2, 3).reshape(chunk_tiles, rows, LANES)

    received = []
    for c in range(chunks):
        arrivals = {}
        for k in sorted(order, reverse=True):
            arrivals[k] = hop(block(k, c), k, count) if k else block(0, c)
        received.append([arrivals[k] for k in order])

    tiles = tiled.transpose(1, 0, 2, 3).reshape(all_cells // LANES, rows, LANES)
    own_values = pick(tiles, points)
    everyone = lax.all_gather(own_values, "kgrp", axis=0, tiled=False)
    chosen = partner == lax.axis_index("kgrp")
    src_values = jnp.sum(jnp.where(chosen[:, None, None], everyone, jnp.zeros_like(everyone)), axis=0)
    both = jnp.stack([own_values, src_values])[None]
    bit = count // 2
    while bit:
        both = jnp.concatenate([both, hop(both, bit, count)], axis=0)
        bit //= 2

    scale = table_scale(GX)
    turn = jnp.asarray(turn_table(count * rows))
    own_coef, src_coef = coefficients(both, turn)
    plane_t = jnp.asarray(plane_table(scale))
    groups = 2 if bands % 16 == 0 else 1
    line_t = jnp.asarray(line_table(scale, order, planes, bands // groups))

    fields = []
    for c in range(chunks):
        sent = exchange(
            received[c], own_coef, src_coef, coulomb, plane_t, turn, c * chunk_planes, chunk_planes
        )
        back = {}
        for k in sorted(order, reverse=True):
            at = order.index(k)
            back[k] = hop(sent[at], k, count) if k else sent[at]
        fields += [back[k] for k in order]

    factor = 1.0 / (scale * scale * math.sqrt(GX * GY * GZ))
    device = jnp.reshape(me, (1,)).astype(jnp.int32)
    out = line_pass(fields, line_t, device, factor, rows, groups, count)
    out = out.reshape(bands, all_cells // LANES, 2, LANES).transpose(0, 2, 1, 3)
    return out.reshape(1, bands, 2, all_cells)


def solution(mesh):
    return jax.shard_map(
        body,
        mesh=mesh,
        in_specs=(P("kgrp", "band", None, None), P(), P(), P(None, "band")),
        out_specs=P("kgrp", "band", None, None),
        check_vma=False,
    )
```

profile of v0, /device:TPU:0, one launch (start us, length us, event | category | flops | bytes accessed | tf_op | source)
XLA Modules:
  0.0 142.8 jit_solution(10622187063150680529)
XLA Ops:
  0.0 3.3 %reshape_squeeze.3 = bf16[16,2,256,128]{3,2,1,0:T(8,128)(2,1)S(1)} reshape(bf16[1,16,2,32768]{3,2,1,0:T(2,128)(2,1)} %param.7) | data formatting | bytes 4194304 | tf_op jit(solution)/shard_map/reshape;squeeze | solution.py:235
  3.3 3.5 %copy.27 = bf16[16,2,256,128]{3,1,0,2:T(2,128)(2,1)} copy(bf16[16,2,256,128]{3,2,1,0:T(8,128)(2,1)S(1)} %reshape_squeeze.3) | data formatting | bytes 4194304 | tf_op jit(solution)/shard_map/reshape;squeeze | solution.py:235
  6.8 10.2 %pick_points.1 = bf16[4,32,128]{2,1,0:T(8,128)(2,1)} custom-call(s32[512]{0:T(512)} %points_ref.1, bf16[256,32,128]{2,1,0:T(8,128)(2,1)} %bitcast.61), custom_call_target="tpu_custom_call" | custom-call | tf_op jit(solution)/shard_map/pick_points/pallas_call | solution.py:88
  17.0 0.8 copy.36
  17.8 6.7 %all_gather.3 = bf16[4,32,512]{2,1,0:T(8,128)(2,1)S(1)} all-gather(bf16[1,32,512]{2,1,0:T(8,128)(2,1)S(1)} %stack_reshape.3), channel_id=1, replica_groups=mesh['kgrp'=4,'band'=8] {'kgrp'}, dimensions={0}, use_global_device_ids=true | all-gather | bytes 163840 | tf_op jit(solution)/shard_map/all_gather | solution.py:251
  24.4 0.1 select_reduce_fusion
  24.6 3.0 %collective-permute-start.7 = (bf16[1,2,32,512]{3,2,1,0:T(8,128)(2,1)S(1)}, bf16[1,2,32,512]{3,2,1,0:T(8,128)(2,1)S(1)}, u32[]{:S(2)}, u32[]{:S(2)}) collective-permute-start(bf16[1,2,32,512]{3,2,1,0:T(8,128)(2,1)S(1)} %maximum_bitcast_fusion), channel_id=1, source_target_pairs={{0,4},{1,5},{2,6},{3,7},{4,0},{5,1},{6,2},{7,3},{8,12},{9,13},{10,... | collective-permute-start | bytes 196616 | tf_op jit(solution)/shard_map/ppermute | solution.py:214
  27.6 4.0 %collective-permute-done.7 = bf16[1,2,32,512]{3,2,1,0:T(8,128)(2,1)S(1)} collective-permute-done((bf16[1,2,32,512]{3,2,1,0:T(8,128)(2,1)S(1)}, bf16[1,2,32,512]{3,2,1,0:T(8,128)(2,1)S(1)}, u32[]{:S(2)}, u32[]{:S(2)}) %collective-permute-start.7) | collective-permute-done | bytes 65568 | tf_op jit(solution)/shard_map/ppermute | solution.py:214
  31.6 0.8 collective-permute-start.8
  32.4 4.2 %collective-permute-done.8 = bf16[2,2,32,512]{3,2,1,0:T(8,128)(2,1)S(1)} collective-permute-done((bf16[2,2,32,512]{3,2,1,0:T(8,128)(2,1)S(1)}, bf16[2,2,32,512]{3,2,1,0:T(8,128)(2,1)S(1)}, u32[]{:S(2)}, u32[]{:S(2)}) %collective-permute-start.8) | collective-permute-done | bytes 131104 | tf_op jit(solution)/shard_map/ppermute | solution.py:214
  36.7 1.6 %collective-permute-start.9 = (bf16[4,2,32,512]{3,2,1,0:T(8,128)(2,1)S(1)}, bf16[4,2,32,512]{3,2,1,0:T(8,128)(2,1)S(1)}, u32[]{:S(2)}, u32[]{:S(2)}) collective-permute-start(bf16[4,2,32,512]{3,2,1,0:T(8,128)(2,1)S(1)} %pad_maximum_fusion.1), channel_id=1, source_target_pairs={{0,1},{1,0},{2,3},{3,2},{4,5},{5,4},{6,7},{7,6},{8,9},{9,8},{10,11... | collective-permute-start | bytes 786440 | tf_op jit(solution)/shard_map/ppermute | solution.py:214
  38.3 2.9 %constant_dynamic-slice_fusion = (bf16[16,2,16,128]{3,1,0,2:T(2,128)(2,1)S(1)}, bf16[16,2,16,128]{3,1,0,2:T(2,128)(2,1)S(1)}, bf16[16,2,16,128]{3,1,0,2:T(2,128)...) fusion(bf16[16,2,256,128]{3,1,0,2:T(2,128)(2,1)S(1)} %copy-done, ...), kind=kLoop, calls=%fused_computation.5 | loop fusion | bytes 4194368 | tf_op jit(solution)/shard_map/dynamic-slice.15
  41.2 2.8 %collective-permute-start.17 = (bf16[16,32,128]{2,1,0:T(8,128)(2,1)S(1)}, bf16[16,32,128]{2,1,0:T(8,128)(2,1)S(1)}, u32[]{:S(2)}, u32[]{:S(2)}) collective-permute-start(bf16[16,32,128]{2,1,0:T(8,128)(2,1)S(1)} %bitcast.78), channel_id=1, source_target_pairs={{0,4},{1,5},{2,6},{3,7},{4,0},{5,1},{6,2},{7,3},{8,12},{9,13},{10,... | collective-permute-start | bytes 393224 | tf_op jit(solution)/shard_map/ppermute | solution.py:214
  44.0 1.7 %collective-permute-start.18 = (bf16[16,32,128]{2,1,0:T(8,128)(2,1)S(1)}, bf16[16,32,128]{2,1,0:T(8,128)(2,1)S(1)}, u32[]{:S(2)}, u32[]{:S(2)}) collective-permute-start(bf16[16,32,128]{2,1,0:T(8,128)(2,1)S(1)} %bitcast.77), channel_id=1, source_target_pairs={{0,2},{1,3},{2,0},{3,1},{4,6},{5,7},{6,4},{7,5},{8,10},{9,11},{10,... | collective-permute-start | bytes 393224 | tf_op jit(solution)/shard_map/ppermute | solution.py:214
  45.8 0.5 collective-permute-start.20
  46.3 7.3 %collective-permute-done.17.refs_1_ = bf16[16,32,128]{2,1,0:T(8,128)(2,1)S(1)} collective-permute-done((bf16[16,32,128]{2,1,0:T(8,128)(2,1)S(1)}, bf16[16,32,128]{2,1,0:T(8,128)(2,1)S(1)}, u32[]{:S(2)}, u32[]{:S(2)}) %collective-permute-start.17) | collective-permute-done | bytes 131104 | tf_op jit(solution)/shard_map/ppermute | solution.py:214
  53.6 5.9 %collective-permute-start.22 = (bf16[16,32,128]{2,1,0:T(8,128)(2,1)S(1)}, bf16[16,32,128]{2,1,0:T(8,128)(2,1)S(1)}, u32[]{:S(2)}, u32[]{:S(2)}) collective-permute-start(bf16[16,32,128]{2,1,0:T(8,128)(2,1)S(1)} %bitcast.73), channel_id=1, source_target_pairs={{0,3},{1,2},{2,1},{3,0},{4,7},{5,6},{6,5},{7,4},{8,11},{9,10},{10,... | collective-permute-start | bytes 393224 | tf_op jit(solution)/shard_map/ppermute | solution.py:214
  59.6 3.3 %collective-permute-start = (bf16[16,32,128]{2,1,0:T(8,128)(2,1)S(1)}, bf16[16,32,128]{2,1,0:T(8,128)(2,1)S(1)}, u32[]{:S(2)}, u32[]{:S(2)}) collective-permute-start(bf16[16,32,128]{2,1,0:T(8,128)(2,1)S(1)} %bitcast.71), channel_id=1, source_target_pairs={{0,4},{1,5},{2,6},{3,7},{4,0},{5,1},{6,2},{7,3},{8,12},{9,13},{10,... | collective-permute-start | bytes 393224 | tf_op jit(solution)/shard_map/ppermute | solution.py:214
  62.9 1.0 collective-permute-start.1
  63.9 0.8 pad_maximum_fusion.both_ref
  64.7 2.4 %coefficients.1 = (bf16[1024,256]{1,0:T(8,128)(2,1)}, bf16[256,1024]{1,0:T(8,128)(2,1)}) custom-call(bf16[8,2,32,512]{3,2,1,0:T(8,128)(2,1)} %pad_maximum_fusion.both_ref, bf16[256,256]{1,0:T(8,128)(2,1)} %constant.49.clone.turn_ref.refs_12_), custom_call_target="tpu_custom_call" | custom-call | tf_op jit(solution)/shard_map/coefficients/pallas_call | solution.py:112
  67.1 1.8 %collective-permute-start.2 = (bf16[16,32,128]{2,1,0:T(8,128)(2,1)S(1)}, bf16[16,32,128]{2,1,0:T(8,128)(2,1)S(1)}, u32[]{:S(2)}, u32[]{:S(2)}) collective-permute-start(bf16[16,32,128]{2,1,0:T(8,128)(2,1)S(1)} %bitcast.68), channel_id=1, source_target_pairs={{0,6},{1,7},{2,4},{3,5},{4,2},{5,3},{6,0},{7,1},{8,14},{9,15},{10,... | collective-permute-start | bytes 393224 | tf_op jit(solution)/shard_map/ppermute | solution.py:214
  69.0 1.5 %collective-permute-start.3 = (bf16[16,32,128]{2,1,0:T(8,128)(2,1)S(1)}, bf16[16,32,128]{2,1,0:T(8,128)(2,1)S(1)}, u32[]{:S(2)}, u32[]{:S(2)}) collective-permute-start(bf16[16,32,128]{2,1,0:T(8,128)(2,1)S(1)} %bitcast.67), channel_id=1, source_target_pairs={{0,1},{1,0},{2,3},{3,2},{4,5},{5,4},{6,7},{7,6},{8,9},{9,8},{10,11... | collective-permute-start | bytes 393224 | tf_op jit(solution)/shard_map/ppermute | solution.py:214
  70.5 5.8 %collective-permute-start.4 = (bf16[16,32,128]{2,1,0:T(8,128)(2,1)S(1)}, bf16[16,32,128]{2,1,0:T(8,128)(2,1)S(1)}, u32[]{:S(2)}, u32[]{:S(2)}) collective-permute-start(bf16[16,32,128]{2,1,0:T(8,128)(2,1)S(1)} %bitcast.66), channel_id=1, source_target_pairs={{0,5},{1,4},{2,7},{3,6},{4,1},{5,0},{6,3},{7,2},{8,13},{9,12},{10,... | collective-permute-start | bytes 393224 | tf_op jit(solution)/shard_map/ppermute | solution.py:214
  76.3 2.6 %collective-permute-done.refs_1_ = bf16[16,32,128]{2,1,0:T(8,128)(2,1)S(1)} collective-permute-done((bf16[16,32,128]{2,1,0:T(8,128)(2,1)S(1)}, bf16[16,32,128]{2,1,0:T(8,128)(2,1)S(1)}, u32[]{:S(2)}, u32[]{:S(2)}) %collective-permute-start) | collective-permute-done | bytes 131104 | tf_op jit(solution)/shard_map/ppermute | solution.py:214
  79.0 2.1 %collective-permute-start.6 = (bf16[16,32,128]{2,1,0:T(8,128)(2,1)S(1)}, bf16[16,32,128]{2,1,0:T(8,128)(2,1)S(1)}, u32[]{:S(2)}, u32[]{:S(2)}) collective-permute-start(bf16[16,32,128]{2,1,0:T(8,128)(2,1)S(1)} %bitcast.64), channel_id=1, source_target_pairs={{0,7},{1,6},{2,5},{3,4},{4,3},{5,2},{6,1},{7,0},{8,15},{9,14},{10,... | collective-permute-start | bytes 393224 | tf_op jit(solution)/shard_map/ppermute | solution.py:214
  81.2 9.6 %exchange_planes.3 = (bf16[2,32,1024]{2,1,0:T(8,128)(2,1)}, bf16[2,32,1024]{2,1,0:T(8,128)(2,1)}, bf16[2,32,1024]{2,1,0:T(8,128)(2,1)}, bf16[2,32,1024]{2,1,0:T(...) custom-call(bf16[16,32,128]{2,1,0:T(8,128)(2,1)} %bitcast.69, ...), custom_call_target="tpu_custom_call" | custom-call | flops 4294967296 | bytes 12582912 | tf_op jit(solution)/shard_map/exchange_planes/pallas_call | solution.py:160
  90.8 2.3 %collective-permute-start.24 = (bf16[2,32,1024]{2,1,0:T(8,128)(2,1)}, bf16[2,32,1024]{2,1,0:T(8,128)(2,1)S(1)}, u32[]{:S(2)}, u32[]{:S(2)}) collective-permute-start(bf16[2,32,1024]{2,1,0:T(8,128)(2,1)} %get-tuple-element.34), channel_id=1, source_target_pairs={{0,4},{1,5},{2,6},{3,7},{4,0},{5,1},{6,2},{7,3},{8,12},{9,13},{10,... | collective-permute-start | bytes 393224 | tf_op jit(solution)/shard_map/ppermute | solution.py:214
  93.1 0.8 collective-permute-start.25
  93.9 1.3 collective-permute-start.26
  95.2 1.0 collective-permute-start.27
  96.2 1.8 %collective-permute-start.28 = (bf16[2,32,1024]{2,1,0:T(8,128)(2,1)}, bf16[2,32,1024]{2,1,0:T(8,128)(2,1)S(1)}, u32[]{:S(2)}, u32[]{:S(2)}) collective-permute-start(bf16[2,32,1024]{2,1,0:T(8,128)(2,1)} %get-tuple-element.38), channel_id=1, source_target_pairs={{0,5},{1,4},{2,7},{3,6},{4,1},{5,0},{6,3},{7,2},{8,13},{9,12},{10,... | collective-permute-start | bytes 393224 | tf_op jit(solution)/shard_map/ppermute | solution.py:214
  98.1 9.6 %exchange_planes.2 = (bf16[2,32,1024]{2,1,0:T(8,128)(2,1)}, bf16[2,32,1024]{2,1,0:T(8,128)(2,1)}, bf16[2,32,1024]{2,1,0:T(8,128)(2,1)}, bf16[2,32,1024]{2,1,0:T(...) custom-call(bf16[16,32,128]{2,1,0:T(8,128)(2,1)} %bitcast.63, ...), custom_call_target="tpu_custom_call" | custom-call | flops 4294967296 | bytes 12582912 | tf_op jit(solution)/shard_map/exchange_planes/pallas_call | solution.py:160
  107.7 1.9 %collective-permute-start.29 = (bf16[2,32,1024]{2,1,0:T(8,128)(2,1)S(1)}, bf16[2,32,1024]{2,1,0:T(8,128)(2,1)S(1)}, u32[]{:S(2)}, u32[]{:S(2)}) collective-permute-start(bf16[2,32,1024]{2,1,0:T(8,128)(2,1)S(1)} %copy-done.18), channel_id=1, source_target_pairs={{0,3},{1,2},{2,1},{3,0},{4,7},{5,6},{6,5},{7,4},{8,11},{9,10},{10,... | collective-permute-start | bytes 393224 | tf_op jit(solution)/shard_map/ppermute | solution.py:214
  109.6 2.1 %collective-permute-start.30 = (bf16[2,32,1024]{2,1,0:T(8,128)(2,1)S(1)}, bf16[2,32,1024]{2,1,0:T(8,128)(2,1)S(1)}, u32[]{:S(2)}, u32[]{:S(2)}) collective-permute-start(bf16[2,32,1024]{2,1,0:T(8,128)(2,1)S(1)} %copy-done.17), channel_id=1, source_target_pairs={{0,7},{1,6},{2,5},{3,4},{4,3},{5,2},{6,1},{7,0},{8,15},{9,14},{10,... | collective-permute-start | bytes 393224 | tf_op jit(solution)/shard_map/ppermute | solution.py:214
  111.8 0.4 collective-permute-start.10
  112.2 2.6 %collective-permute-start.11 = (bf16[2,32,1024]{2,1,0:T(8,128)(2,1)}, bf16[2,32,1024]{2,1,0:T(8,128)(2,1)S(1)}, u32[]{:S(2)}, u32[]{:S(2)}) collective-permute-start(bf16[2,32,1024]{2,1,0:T(8,128)(2,1)} %get-tuple-element.27), channel_id=1, source_target_pairs={{0,2},{1,3},{2,0},{3,1},{4,6},{5,7},{6,4},{7,5},{8,10},{9,11},{10,... | collective-permute-start | bytes 393224 | tf_op jit(solution)/shard_map/ppermute | solution.py:214
  114.8 1.3 collective-permute-start.12
  116.2 1.0 collective-permute-start.13
  117.1 1.9 %collective-permute-done.30.refs_16_ = bf16[2,32,1024]{2,1,0:T(8,128)(2,1)S(1)} collective-permute-done((bf16[2,32,1024]{2,1,0:T(8,128)(2,1)S(1)}, bf16[2,32,1024]{2,1,0:T(8,128)(2,1)S(1)}, u32[]{:S(2)}, u32[]{:S(2)}) %collective-permute-start.30) | collective-permute-done | bytes 131104 | tf_op jit(solution)/shard_map/ppermute | solution.py:214
  119.0 5.0 %collective-permute-start.14 = (bf16[2,32,1024]{2,1,0:T(8,128)(2,1)}, bf16[2,32,1024]{2,1,0:T(8,128)(2,1)S(1)}, u32[]{:S(2)}, u32[]{:S(2)}) collective-permute-start(bf16[2,32,1024]{2,1,0:T(8,128)(2,1)} %get-tuple-element.30), channel_id=1, source_target_pairs={{0,5},{1,4},{2,7},{3,6},{4,1},{5,0},{6,3},{7,2},{8,13},{9,12},{10,... | collective-permute-start | bytes 393224 | tf_op jit(solution)/shard_map/ppermute | solution.py:214
  124.0 3.9 %collective-permute-done.10.refs_2_ = bf16[2,32,1024]{2,1,0:T(8,128)(2,1)S(1)} collective-permute-done((bf16[2,32,1024]{2,1,0:T(8,128)(2,1)}, bf16[2,32,1024]{2,1,0:T(8,128)(2,1)S(1)}, u32[]{:S(2)}, u32[]{:S(2)}) %collective-permute-start.10) | collective-permute-done | bytes 131104 | tf_op jit(solution)/shard_map/ppermute | solution.py:214
  127.9 3.5 %collective-permute-start.16 = (bf16[2,32,1024]{2,1,0:T(8,128)(2,1)}, bf16[2,32,1024]{2,1,0:T(8,128)(2,1)S(1)}, u32[]{:S(2)}, u32[]{:S(2)}) collective-permute-start(bf16[2,32,1024]{2,1,0:T(8,128)(2,1)} %get-tuple-element.32), channel_id=1, source_target_pairs={{0,7},{1,6},{2,5},{3,4},{4,3},{5,2},{6,1},{7,0},{8,15},{9,14},{10,... | collective-permute-start | bytes 393224 | tf_op jit(solution)/shard_map/ppermute | solution.py:214
  131.4 3.2 %collective-permute-done.14.refs_6_ = bf16[2,32,1024]{2,1,0:T(8,128)(2,1)S(1)} collective-permute-done((bf16[2,32,1024]{2,1,0:T(8,128)(2,1)}, bf16[2,32,1024]{2,1,0:T(8,128)(2,1)S(1)}, u32[]{:S(2)}, u32[]{:S(2)}) %collective-permute-start.14) | collective-permute-done | bytes 131104 | tf_op jit(solution)/shard_map/ppermute | solution.py:214
  134.6 2.1 %collective-permute-done.15.refs_7_ = bf16[2,32,1024]{2,1,0:T(8,128)(2,1)S(1)} collective-permute-done((bf16[2,32,1024]{2,1,0:T(8,128)(2,1)}, bf16[2,32,1024]{2,1,0:T(8,128)(2,1)S(1)}, u32[]{:S(2)}, u32[]{:S(2)}) %collective-permute-start.15) | collective-permute-done | bytes 131104 | tf_op jit(solution)/shard_map/ppermute | solution.py:214
  136.9 0.5 copy-done.13
  137.4 0.1 copy-done.14
  137.5 5.3 %line_pass.1 = bf16[512,8,2,128]{3,2,1,0:T(2,128)(2,1)} custom-call(s32[1]{0:T(128)} %bitcast.refs_0_, bf16[2,32,1024]{2,1,0:T(8,128)(2,1)} %get-tuple-element.25.refs_1_, bf16[2,32,1024]{2,1,0:T(8,128)(2,1)} %copy-done.8, bf16[2,32,1024]{2,1,0:T(8,128)(2,1)} %copy-done.9, bf16[2,32,1024]{2,1,0:T(8,128)(2,1)} %copy-done.10, bf16[2,32,1024]{2,1,0:T(8,128)(2,1)} %copy-done.11, ...), custom_call_target="tpu_custom_call" | custom-call | flops 1073741824 | bytes 5242880 | tf_op jit(solution)/shard_map/line_pass/pallas_call | solution.py:203
  (95 shorter events, 0.3 us)
Async XLA Ops:
  6.8 17.6 %copy-start.31 = (s32[4]{0:T(128)S(1)}, s32[4]{0:T(128)}, u32[]{:S(2)}) copy-start(s32[4]{0:T(128)} %param.9) | copy-start | bytes 52
  6.8 31.5 %copy-start = (bf16[16,2,256,128]{3,1,0,2:T(2,128)(2,1)S(1)}, bf16[16,2,256,128]{3,1,0,2:T(2,128)(2,1)}, u32[]{:S(2)}) copy-start(bf16[16,2,256,128]{3,1,0,2:T(2,128)(2,1)} %copy.27) | copy-start | bytes 6291460
  24.6 7.1 %collective-permute-start.7 = (bf16[1,2,32,512]{3,2,1,0:T(8,128)(2,1)S(1)}, bf16[1,2,32,512]{3,2,1,0:T(8,128)(2,1)S(1)}, u32[]{:S(2)}, u32[]{:S(2)}) collective-permute-start(bf16[1,2,32,512]{3,2,1,0:T(8,128)(2,1)S(1)} %maximum_bitcast_fusion), channel_id=1, source_target_pairs={{0,4},{1,5},{2,6},{3,7},{4,0},{5,1},{6,2},{7,3},{8,12},{9,13},{10,... | collective-permute-start | bytes 196616 | tf_op jit(solution)/shard_map/ppermute | solution.py:214
  31.6 5.0 %collective-permute-start.8 = (bf16[2,2,32,512]{3,2,1,0:T(8,128)(2,1)S(1)}, bf16[2,2,32,512]{3,2,1,0:T(8,128)(2,1)S(1)}, u32[]{:S(2)}, u32[]{:S(2)}) collective-permute-start(bf16[2,2,32,512]{3,2,1,0:T(8,128)(2,1)S(1)} %pad_maximum_fusion.2), channel_id=1, source_target_pairs={{0,2},{1,3},{2,0},{3,1},{4,6},{5,7},{6,4},{7,5},{8,10},{9,11},{10,... | collective-permute-start | bytes 393224 | tf_op jit(solution)/shard_map/ppermute | solution.py:214
  36.7 26.2 %collective-permute-start.9 = (bf16[4,2,32,512]{3,2,1,0:T(8,128)(2,1)S(1)}, bf16[4,2,32,512]{3,2,1,0:T(8,128)(2,1)S(1)}, u32[]{:S(2)}, u32[]{:S(2)}) collective-permute-start(bf16[4,2,32,512]{3,2,1,0:T(8,128)(2,1)S(1)} %pad_maximum_fusion.1), channel_id=1, source_target_pairs={{0,1},{1,0},{2,3},{3,2},{4,5},{5,4},{6,7},{7,6},{8,9},{9,8},{10,11... | collective-permute-start | bytes 786440 | tf_op jit(solution)/shard_map/ppermute | solution.py:214
  41.2 12.4 %collective-permute-start.17 = (bf16[16,32,128]{2,1,0:T(8,128)(2,1)S(1)}, bf16[16,32,128]{2,1,0:T(8,128)(2,1)S(1)}, u32[]{:S(2)}, u32[]{:S(2)}) collective-permute-start(bf16[16,32,128]{2,1,0:T(8,128)(2,1)S(1)} %bitcast.78), channel_id=1, source_target_pairs={{0,4},{1,5},{2,6},{3,7},{4,0},{5,1},{6,2},{7,3},{8,12},{9,13},{10,... | collective-permute-start | bytes 393224 | tf_op jit(solution)/shard_map/ppermute | solution.py:214
  44.0 9.6 %collective-permute-start.18 = (bf16[16,32,128]{2,1,0:T(8,128)(2,1)S(1)}, bf16[16,32,128]{2,1,0:T(8,128)(2,1)S(1)}, u32[]{:S(2)}, u32[]{:S(2)}) collective-permute-start(bf16[16,32,128]{2,1,0:T(8,128)(2,1)S(1)} %bitcast.77), channel_id=1, source_target_pairs={{0,2},{1,3},{2,0},{3,1},{4,6},{5,7},{6,4},{7,5},{8,10},{9,11},{10,... | collective-permute-start | bytes 393224 | tf_op jit(solution)/shard_map/ppermute | solution.py:214
  45.8 13.8 %collective-permute-start.19 = (bf16[16,32,128]{2,1,0:T(8,128)(2,1)S(1)}, bf16[16,32,128]{2,1,0:T(8,128)(2,1)S(1)}, u32[]{:S(2)}, u32[]{:S(2)}) collective-permute-start(bf16[16,32,128]{2,1,0:T(8,128)(2,1)S(1)} %bitcast.76), channel_id=1, source_target_pairs={{0,6},{1,7},{2,4},{3,5},{4,2},{5,3},{6,0},{7,1},{8,14},{9,15},{10,... | collective-permute-start | bytes 393224 | tf_op jit(solution)/shard_map/ppermute | solution.py:214
  45.8 13.8 %collective-permute-start.20 = (bf16[16,32,128]{2,1,0:T(8,128)(2,1)S(1)}, bf16[16,32,128]{2,1,0:T(8,128)(2,1)S(1)}, u32[]{:S(2)}, u32[]{:S(2)}) collective-permute-start(bf16[16,32,128]{2,1,0:T(8,128)(2,1)S(1)} %bitcast.75), channel_id=1, source_target_pairs={{0,1},{1,0},{2,3},{3,2},{4,5},{5,4},{6,7},{7,6},{8,9},{9,8},{10,11... | collective-permute-start | bytes 393224 | tf_op jit(solution)/shard_map/ppermute | solution.py:214
  53.6 27.5 %copy-start.19 = (bf16[16,32,128]{2,1,0:T(8,128)(2,1)}, bf16[16,32,128]{2,1,0:T(8,128)(2,1)S(1)}, u32[]{:S(2)}) copy-start(bf16[16,32,128]{2,1,0:T(8,128)(2,1)S(1)} %collective-permute-done.17.refs_1_) | copy-start | bytes 393220
  53.6 13.5 %collective-permute-start.21 = (bf16[16,32,128]{2,1,0:T(8,128)(2,1)S(1)}, bf16[16,32,128]{2,1,0:T(8,128)(2,1)S(1)}, u32[]{:S(2)}, u32[]{:S(2)}) collective-permute-start(bf16[16,32,128]{2,1,0:T(8,128)(2,1)S(1)} %bitcast.74), channel_id=1, source_target_pairs={{0,5},{1,4},{2,7},{3,6},{4,1},{5,0},{6,3},{7,2},{8,13},{9,12},{10,... | collective-permute-start | bytes 393224 | tf_op jit(solution)/shard_map/ppermute | solution.py:214
  53.6 27.5 %copy-start.20 = (bf16[16,32,128]{2,1,0:T(8,128)(2,1)}, bf16[16,32,128]{2,1,0:T(8,128)(2,1)S(1)}, u32[]{:S(2)}) copy-start(bf16[16,32,128]{2,1,0:T(8,128)(2,1)S(1)} %collective-permute-done.18.refs_2_) | copy-start | bytes 393220
  53.6 15.4 %collective-permute-start.22 = (bf16[16,32,128]{2,1,0:T(8,128)(2,1)S(1)}, bf16[16,32,128]{2,1,0:T(8,128)(2,1)S(1)}, u32[]{:S(2)}, u32[]{:S(2)}) collective-permute-start(bf16[16,32,128]{2,1,0:T(8,128)(2,1)S(1)} %bitcast.73), channel_id=1, source_target_pairs={{0,3},{1,2},{2,1},{3,0},{4,7},{5,6},{6,5},{7,4},{8,11},{9,10},{10,... | collective-permute-start | bytes 393224 | tf_op jit(solution)/shard_map/ppermute | solution.py:214
  59.5 21.6 %copy-start.22 = (bf16[16,32,128]{2,1,0:T(8,128)(2,1)}, bf16[16,32,128]{2,1,0:T(8,128)(2,1)S(1)}, u32[]{:S(2)}) copy-start(bf16[16,32,128]{2,1,0:T(8,128)(2,1)S(1)} %collective-permute-done.19.refs_3_) | copy-start | bytes 393220
  59.5 11.0 %collective-permute-start.23 = (bf16[16,32,128]{2,1,0:T(8,128)(2,1)S(1)}, bf16[16,32,128]{2,1,0:T(8,128)(2,1)S(1)}, u32[]{:S(2)}, u32[]{:S(2)}) collective-permute-start(bf16[16,32,128]{2,1,0:T(8,128)(2,1)S(1)} %bitcast.72), channel_id=1, source_target_pairs={{0,7},{1,6},{2,5},{3,4},{4,3},{5,2},{6,1},{7,0},{8,15},{9,14},{10,... | collective-permute-start | bytes 393224 | tf_op jit(solution)/shard_map/ppermute | solution.py:214
  59.5 21.6 %copy-start.23 = (bf16[16,32,128]{2,1,0:T(8,128)(2,1)}, bf16[16,32,128]{2,1,0:T(8,128)(2,1)S(1)}, u32[]{:S(2)}) copy-start(bf16[16,32,128]{2,1,0:T(8,128)(2,1)S(1)} %collective-permute-done.20.refs_4_) | copy-start | bytes 393220
  59.6 19.4 %collective-permute-start = (bf16[16,32,128]{2,1,0:T(8,128)(2,1)S(1)}, bf16[16,32,128]{2,1,0:T(8,128)(2,1)S(1)}, u32[]{:S(2)}, u32[]{:S(2)}) collective-permute-start(bf16[16,32,128]{2,1,0:T(8,128)(2,1)S(1)} %bitcast.71), channel_id=1, source_target_pairs={{0,4},{1,5},{2,6},{3,7},{4,0},{5,1},{6,2},{7,3},{8,12},{9,13},{10,... | collective-permute-start | bytes 393224 | tf_op jit(solution)/shard_map/ppermute | solution.py:214
  62.9 16.1 %collective-permute-start.1 = (bf16[16,32,128]{2,1,0:T(8,128)(2,1)S(1)}, bf16[16,32,128]{2,1,0:T(8,128)(2,1)S(1)}, u32[]{:S(2)}, u32[]{:S(2)}) collective-permute-start(bf16[16,32,128]{2,1,0:T(8,128)(2,1)S(1)} %bitcast.70), channel_id=1, source_target_pairs={{0,2},{1,3},{2,0},{3,1},{4,6},{5,7},{6,4},{7,5},{8,10},{9,11},{10,... | collective-permute-start | bytes 393224 | tf_op jit(solution)/shard_map/ppermute | solution.py:214
  67.1 14.0 %copy-start.25 = (bf16[16,32,128]{2,1,0:T(8,128)(2,1)}, bf16[16,32,128]{2,1,0:T(8,128)(2,1)S(1)}, u32[]{:S(2)}) copy-start(bf16[16,32,128]{2,1,0:T(8,128)(2,1)S(1)} %collective-permute-done.21.refs_5_) | copy-start | bytes 393220
  67.1 23.6 %collective-permute-start.2 = (bf16[16,32,128]{2,1,0:T(8,128)(2,1)S(1)}, bf16[16,32,128]{2,1,0:T(8,128)(2,1)S(1)}, u32[]{:S(2)}, u32[]{:S(2)}) collective-permute-start(bf16[16,32,128]{2,1,0:T(8,128)(2,1)S(1)} %bitcast.68), channel_id=1, source_target_pairs={{0,6},{1,7},{2,4},{3,5},{4,2},{5,3},{6,0},{7,1},{8,14},{9,15},{10,... | collective-permute-start | bytes 393224 | tf_op jit(solution)/shard_map/ppermute | solution.py:214
  69.0 12.2 %copy-start.27 = (bf16[16,32,128]{2,1,0:T(8,128)(2,1)}, bf16[16,32,128]{2,1,0:T(8,128)(2,1)S(1)}, u32[]{:S(2)}) copy-start(bf16[16,32,128]{2,1,0:T(8,128)(2,1)S(1)} %collective-permute-done.22.refs_6_) | copy-start | bytes 393220
  69.0 24.1 %collective-permute-start.3 = (bf16[16,32,128]{2,1,0:T(8,128)(2,1)S(1)}, bf16[16,32,128]{2,1,0:T(8,128)(2,1)S(1)}, u32[]{:S(2)}, u32[]{:S(2)}) collective-permute-start(bf16[16,32,128]{2,1,0:T(8,128)(2,1)S(1)} %bitcast.67), channel_id=1, source_target_pairs={{0,1},{1,0},{2,3},{3,2},{4,5},{5,4},{6,7},{7,6},{8,9},{9,8},{10,11... | collective-permute-start | bytes 393224 | tf_op jit(solution)/shard_map/ppermute | solution.py:214
  70.5 23.4 %collective-permute-start.4 = (bf16[16,32,128]{2,1,0:T(8,128)(2,1)S(1)}, bf16[16,32,128]{2,1,0:T(8,128)(2,1)S(1)}, u32[]{:S(2)}, u32[]{:S(2)}) collective-permute-start(bf16[16,32,128]{2,1,0:T(8,128)(2,1)S(1)} %bitcast.66), channel_id=1, source_target_pairs={{0,5},{1,4},{2,7},{3,6},{4,1},{5,0},{6,3},{7,2},{8,13},{9,12},{10,... | collective-permute-start | bytes 393224 | tf_op jit(solution)/shard_map/ppermute | solution.py:214
  79.0 11.8 %copy-start.15 = (bf16[16,32,128]{2,1,0:T(8,128)(2,1)}, bf16[16,32,128]{2,1,0:T(8,128)(2,1)S(1)}, u32[]{:S(2)}) copy-start(bf16[16,32,128]{2,1,0:T(8,128)(2,1)S(1)} %collective-permute-done.refs_1_) | copy-start | bytes 393220
  79.0 16.3 %collective-permute-start.5 = (bf16[16,32,128]{2,1,0:T(8,128)(2,1)S(1)}, bf16[16,32,128]{2,1,0:T(8,128)(2,1)S(1)}, u32[]{:S(2)}, u32[]{:S(2)}) collective-permute-start(bf16[16,32,128]{2,1,0:T(8,128)(2,1)S(1)} %bitcast.65), channel_id=1, source_target_pairs={{0,3},{1,2},{2,1},{3,0},{4,7},{5,6},{6,5},{7,4},{8,11},{9,10},{10,... | collective-permute-start | bytes 393224 | tf_op jit(solution)/shard_map/ppermute | solution.py:214
  79.0 11.8 %copy-start.16 = (bf16[16,32,128]{2,1,0:T(8,128)(2,1)}, bf16[16,32,128]{2,1,0:T(8,128)(2,1)S(1)}, u32[]{:S(2)}) copy-start(bf16[16,32,128]{2,1,0:T(8,128)(2,1)S(1)} %collective-permute-done.1.refs_2_) | copy-start | bytes 393220
  79.0 17.2 %collective-permute-start.6 = (bf16[16,32,128]{2,1,0:T(8,128)(2,1)S(1)}, bf16[16,32,128]{2,1,0:T(8,128)(2,1)S(1)}, u32[]{:S(2)}, u32[]{:S(2)}) collective-permute-start(bf16[16,32,128]{2,1,0:T(8,128)(2,1)S(1)} %bitcast.64), channel_id=1, source_target_pairs={{0,7},{1,6},{2,5},{3,4},{4,3},{5,2},{6,1},{7,0},{8,15},{9,14},{10,... | collective-permute-start | bytes 393224 | tf_op jit(solution)/shard_map/ppermute | solution.py:214
  90.8 16.9 %collective-permute-start.24 = (bf16[2,32,1024]{2,1,0:T(8,128)(2,1)}, bf16[2,32,1024]{2,1,0:T(8,128)(2,1)S(1)}, u32[]{:S(2)}, u32[]{:S(2)}) collective-permute-start(bf16[2,32,1024]{2,1,0:T(8,128)(2,1)} %get-tuple-element.34), channel_id=1, source_target_pairs={{0,4},{1,5},{2,6},{3,7},{4,0},{5,1},{6,2},{7,3},{8,12},{9,13},{10,... | collective-permute-start | bytes 393224 | tf_op jit(solution)/shard_map/ppermute | solution.py:214
  93.1 16.6 %collective-permute-start.25 = (bf16[2,32,1024]{2,1,0:T(8,128)(2,1)}, bf16[2,32,1024]{2,1,0:T(8,128)(2,1)S(1)}, u32[]{:S(2)}, u32[]{:S(2)}) collective-permute-start(bf16[2,32,1024]{2,1,0:T(8,128)(2,1)} %get-tuple-element.35), channel_id=1, source_target_pairs={{0,2},{1,3},{2,0},{3,1},{4,6},{5,7},{6,4},{7,5},{8,10},{9,11},{10,... | collective-permute-start | bytes 393224 | tf_op jit(solution)/shard_map/ppermute | solution.py:214
  93.9 17.9 %collective-permute-start.26 = (bf16[2,32,1024]{2,1,0:T(8,128)(2,1)}, bf16[2,32,1024]{2,1,0:T(8,128)(2,1)S(1)}, u32[]{:S(2)}, u32[]{:S(2)}) collective-permute-start(bf16[2,32,1024]{2,1,0:T(8,128)(2,1)} %get-tuple-element.36), channel_id=1, source_target_pairs={{0,6},{1,7},{2,4},{3,5},{4,2},{5,3},{6,0},{7,1},{8,14},{9,15},{10,... | collective-permute-start | bytes 393224 | tf_op jit(solution)/shard_map/ppermute | solution.py:214
  95.2 17.0 %collective-permute-start.27 = (bf16[2,32,1024]{2,1,0:T(8,128)(2,1)}, bf16[2,32,1024]{2,1,0:T(8,128)(2,1)S(1)}, u32[]{:S(2)}, u32[]{:S(2)}) collective-permute-start(bf16[2,32,1024]{2,1,0:T(8,128)(2,1)} %get-tuple-element.37), channel_id=1, source_target_pairs={{0,1},{1,0},{2,3},{3,2},{4,5},{5,4},{6,7},{7,6},{8,9},{9,8},{10,11... | collective-permute-start | bytes 393224 | tf_op jit(solution)/shard_map/ppermute | solution.py:214
  96.2 18.6 %collective-permute-start.28 = (bf16[2,32,1024]{2,1,0:T(8,128)(2,1)}, bf16[2,32,1024]{2,1,0:T(8,128)(2,1)S(1)}, u32[]{:S(2)}, u32[]{:S(2)}) collective-permute-start(bf16[2,32,1024]{2,1,0:T(8,128)(2,1)} %get-tuple-element.38), channel_id=1, source_target_pairs={{0,5},{1,4},{2,7},{3,6},{4,1},{5,0},{6,3},{7,2},{8,13},{9,12},{10,... | collective-permute-start | bytes 393224 | tf_op jit(solution)/shard_map/ppermute | solution.py:214
  107.7 29.1 %copy-start.1 = (bf16[2,32,1024]{2,1,0:T(8,128)(2,1)}, bf16[2,32,1024]{2,1,0:T(8,128)(2,1)S(1)}, u32[]{:S(2)}) copy-start(bf16[2,32,1024]{2,1,0:T(8,128)(2,1)S(1)} %collective-permute-done.24.refs_10_) | copy-start | bytes 393220
  107.7 8.5 %collective-permute-start.29 = (bf16[2,32,1024]{2,1,0:T(8,128)(2,1)S(1)}, bf16[2,32,1024]{2,1,0:T(8,128)(2,1)S(1)}, u32[]{:S(2)}, u32[]{:S(2)}) collective-permute-start(bf16[2,32,1024]{2,1,0:T(8,128)(2,1)S(1)} %copy-done.18), channel_id=1, source_target_pairs={{0,3},{1,2},{2,1},{3,0},{4,7},{5,6},{6,5},{7,4},{8,11},{9,10},{10,... | collective-permute-start | bytes 393224 | tf_op jit(solution)/shard_map/ppermute | solution.py:214
  109.6 27.1 %copy-start.2 = (bf16[2,32,1024]{2,1,0:T(8,128)(2,1)}, bf16[2,32,1024]{2,1,0:T(8,128)(2,1)S(1)}, u32[]{:S(2)}) copy-start(bf16[2,32,1024]{2,1,0:T(8,128)(2,1)S(1)} %collective-permute-done.25.refs_11_) | copy-start | bytes 393220
  109.6 9.4 %collective-permute-start.30 = (bf16[2,32,1024]{2,1,0:T(8,128)(2,1)S(1)}, bf16[2,32,1024]{2,1,0:T(8,128)(2,1)S(1)}, u32[]{:S(2)}, u32[]{:S(2)}) collective-permute-start(bf16[2,32,1024]{2,1,0:T(8,128)(2,1)S(1)} %copy-done.17), channel_id=1, source_target_pairs={{0,7},{1,6},{2,5},{3,4},{4,3},{5,2},{6,1},{7,0},{8,15},{9,14},{10,... | collective-permute-start | bytes 393224 | tf_op jit(solution)/shard_map/ppermute | solution.py:214
  111.8 25.0 %copy-start.3 = (bf16[2,32,1024]{2,1,0:T(8,128)(2,1)}, bf16[2,32,1024]{2,1,0:T(8,128)(2,1)S(1)}, u32[]{:S(2)}) copy-start(bf16[2,32,1024]{2,1,0:T(8,128)(2,1)S(1)} %collective-permute-done.26.refs_12_) | copy-start | bytes 393220
  111.8 16.1 %collective-permute-start.10 = (bf16[2,32,1024]{2,1,0:T(8,128)(2,1)}, bf16[2,32,1024]{2,1,0:T(8,128)(2,1)S(1)}, u32[]{:S(2)}, u32[]{:S(2)}) collective-permute-start(bf16[2,32,1024]{2,1,0:T(8,128)(2,1)} %get-tuple-element.26), channel_id=1, source_target_pairs={{0,4},{1,5},{2,6},{3,7},{4,0},{5,1},{6,2},{7,3},{8,12},{9,13},{10,... | collective-permute-start | bytes 393224 | tf_op jit(solution)/shard_map/ppermute | solution.py:214
  112.2 24.6 %copy-start.4 = (bf16[2,32,1024]{2,1,0:T(8,128)(2,1)}, bf16[2,32,1024]{2,1,0:T(8,128)(2,1)S(1)}, u32[]{:S(2)}) copy-start(bf16[2,32,1024]{2,1,0:T(8,128)(2,1)S(1)} %collective-permute-done.27.refs_13_) | copy-start | bytes 393220
  112.2 15.7 %collective-permute-start.11 = (bf16[2,32,1024]{2,1,0:T(8,128)(2,1)}, bf16[2,32,1024]{2,1,0:T(8,128)(2,1)S(1)}, u32[]{:S(2)}, u32[]{:S(2)}) collective-permute-start(bf16[2,32,1024]{2,1,0:T(8,128)(2,1)} %get-tuple-element.27), channel_id=1, source_target_pairs={{0,2},{1,3},{2,0},{3,1},{4,6},{5,7},{6,4},{7,5},{8,10},{9,11},{10,... | collective-permute-start | bytes 393224 | tf_op jit(solution)/shard_map/ppermute | solution.py:214
  114.8 22.0 %copy-start.5 = (bf16[2,32,1024]{2,1,0:T(8,128)(2,1)}, bf16[2,32,1024]{2,1,0:T(8,128)(2,1)S(1)}, u32[]{:S(2)}) copy-start(bf16[2,32,1024]{2,1,0:T(8,128)(2,1)S(1)} %collective-permute-done.28.refs_14_) | copy-start | bytes 393220
  114.8 16.6 %collective-permute-start.12 = (bf16[2,32,1024]{2,1,0:T(8,128)(2,1)}, bf16[2,32,1024]{2,1,0:T(8,128)(2,1)S(1)}, u32[]{:S(2)}, u32[]{:S(2)}) collective-permute-start(bf16[2,32,1024]{2,1,0:T(8,128)(2,1)} %get-tuple-element.28), channel_id=1, source_target_pairs={{0,6},{1,7},{2,4},{3,5},{4,2},{5,3},{6,0},{7,1},{8,14},{9,15},{10,... | collective-permute-start | bytes 393224 | tf_op jit(solution)/shard_map/ppermute | solution.py:214
  116.2 20.6 %copy-start.6 = (bf16[2,32,1024]{2,1,0:T(8,128)(2,1)}, bf16[2,32,1024]{2,1,0:T(8,128)(2,1)S(1)}, u32[]{:S(2)}) copy-start(bf16[2,32,1024]{2,1,0:T(8,128)(2,1)S(1)} %collective-permute-done.29.refs_15_) | copy-start | bytes 393220
  116.2 15.2 %collective-permute-start.13 = (bf16[2,32,1024]{2,1,0:T(8,128)(2,1)}, bf16[2,32,1024]{2,1,0:T(8,128)(2,1)S(1)}, u32[]{:S(2)}, u32[]{:S(2)}) collective-permute-start(bf16[2,32,1024]{2,1,0:T(8,128)(2,1)} %get-tuple-element.29), channel_id=1, source_target_pairs={{0,1},{1,0},{2,3},{3,2},{4,5},{5,4},{6,7},{7,6},{8,9},{9,8},{10,11... | collective-permute-start | bytes 393224 | tf_op jit(solution)/shard_map/ppermute | solution.py:214
  119.0 17.8 %copy-start.7 = (bf16[2,32,1024]{2,1,0:T(8,128)(2,1)}, bf16[2,32,1024]{2,1,0:T(8,128)(2,1)S(1)}, u32[]{:S(2)}) copy-start(bf16[2,32,1024]{2,1,0:T(8,128)(2,1)S(1)} %collective-permute-done.30.refs_16_) | copy-start | bytes 393220
  119.0 15.6 %collective-permute-start.14 = (bf16[2,32,1024]{2,1,0:T(8,128)(2,1)}, bf16[2,32,1024]{2,1,0:T(8,128)(2,1)S(1)}, u32[]{:S(2)}, u32[]{:S(2)}) collective-permute-start(bf16[2,32,1024]{2,1,0:T(8,128)(2,1)} %get-tuple-element.30), channel_id=1, source_target_pairs={{0,5},{1,4},{2,7},{3,6},{4,1},{5,0},{6,3},{7,2},{8,13},{9,12},{10,... | collective-permute-start | bytes 393224 | tf_op jit(solution)/shard_map/ppermute | solution.py:214
  127.9 8.9 %collective-permute-start.15 = (bf16[2,32,1024]{2,1,0:T(8,128)(2,1)}, bf16[2,32,1024]{2,1,0:T(8,128)(2,1)S(1)}, u32[]{:S(2)}, u32[]{:S(2)}) collective-permute-start(bf16[2,32,1024]{2,1,0:T(8,128)(2,1)} %get-tuple-element.31), channel_id=1, source_target_pairs={{0,3},{1,2},{2,1},{3,0},{4,7},{5,6},{6,5},{7,4},{8,11},{9,10},{10,... | collective-permute-start | bytes 393224 | tf_op jit(solution)/shard_map/ppermute | solution.py:214
  127.9 8.9 %collective-permute-start.16 = (bf16[2,32,1024]{2,1,0:T(8,128)(2,1)}, bf16[2,32,1024]{2,1,0:T(8,128)(2,1)S(1)}, u32[]{:S(2)}, u32[]{:S(2)}) collective-permute-start(bf16[2,32,1024]{2,1,0:T(8,128)(2,1)} %get-tuple-element.32), channel_id=1, source_target_pairs={{0,7},{1,6},{2,5},{3,4},{4,3},{5,2},{6,1},{7,0},{8,15},{9,14},{10,... | collective-permute-start | bytes 393224 | tf_op jit(solution)/shard_map/ppermute | solution.py:214
  (15 other events, 85.4 us)
where the time goes:
time: 143 us
  starting transfers between devices  57.3 us (40%)
  Pallas kernels  37 us (26%)
  waiting for transfers between devices  29.3 us (20%)
  local copies, waits for them, and re-layouts  11.2 us (8%)
  blocking collectives  6.66 us (5%)
    ppermute x31, starting transfers between devices, hop(): lax.ppermute(array, 'band', [(i, i ^ distance) for i in range(count)])  57.3 us
    ppermute x31, waiting for transfers between devices, hop(): lax.ppermute(array, 'band', [(i, i ^ distance) for i in range(count)])  29.3 us
    pallas_call x2, Pallas kernels, exchange(): pl.pallas_call(lambda *refs: exchange_kernel(count, *refs), grid=(planes,...  19.1 us
    pallas_call x1, Pallas kernels, pick(): pl.pallas_call(pick_kernel, in_specs=[pl.BlockSpec(memory_space=pltpu.SME...  10.2 us
    another operation x2, local copies, waits for them, and re-layouts, body(): resident.reshape(bands, 2, all_cells // LANES, LANES).transpose(0, 2, 1, 3)  6.8 us
    all_gather x1, blocking collectives, body(): everyone = lax.all_gather(own_values, 'kgrp', axis=0, tiled=False)  6.66 us
    pallas_call x1, Pallas kernels, line_pass(): pl.pallas_call(lambda *refs: line_kernel(factor, group_rows, count, *refs...  5.3 us
    another operation x1, local copies, waits for them, and re-layouts  2.91 us
  transfers between devices with their start and end apart: 31, of which 8 were waited for; matrix products, arithmetic and copies ran while one was open for 3% of the time, Pallas kernels for 15%

commit v1 on v0

v1 whole, which is shorter than its diff:
```python
import math

import jax
import jax.numpy as jnp
import numpy as np
from jax import lax
from jax.experimental import pallas as pl
from jax.experimental.pallas import tpu as pltpu
from jax.sharding import PartitionSpec as P

GX = 32
GY = 32
GZ = 32
LANES = 128
BF16 = jnp.bfloat16
F32 = jnp.float32
VMEM_BYTES = 24 * 1024 * 1024


def round_bf16(values):
    return values.astype(BF16).astype(np.float64)


def table_scale(length):
    cosines = np.cos(2.0 * np.pi * np.arange(length // 4) / length)
    best = (np.inf, 1.0)
    for scale in np.linspace(1.0, 2.0, 8193)[:-1]:
        exact = scale * cosines
        error = float(np.max(np.abs(round_bf16(exact) / exact - 1.0)))
        best = min(best, (error, float(scale)))
    return best[1]


def plane_table(scale):
    cell = np.arange(GY * GZ)
    y, z = cell // GZ, cell % GZ
    turns = (y[:, None] * y[None, :] % GY) / GY + (z[:, None] * z[None, :] % GZ) / GZ
    angle = 2.0 * np.pi * (turns % 1.0)
    return (scale * np.stack([np.cos(angle), np.sin(angle)])).astype(BF16)


def line_table(scale, order, planes, bands):
    count = len(order)
    device = np.arange(count)[:, None, None]
    plane = np.arange(planes)[None, :, None]
    x = planes * (device ^ np.array(order)[None, None, :]) + plane
    kx = np.arange(GX)[None, :, None, None]
    angle = 2.0 * np.pi * (kx * x[:, None] % GX) / GX
    cos_t, sin_t = np.cos(angle), np.sin(angle)
    pair = np.stack([np.stack([cos_t, sin_t], -1), np.stack([-sin_t, cos_t], -1)], 2)
    table = np.zeros((count, bands, GX, 2, planes, count, bands, 2), np.float64)
    for band in range(bands):
        table[:, band, :, :, :, :, band, :] = pair
    return (scale * table).reshape(count, bands * GX * 2, planes * count * bands * 2).astype(BF16)


def turn_table(rows):
    table = np.zeros((rows, rows), np.float32)
    even = np.arange(0, rows, 2)
    table[even, even + 1] = -1.0
    table[even + 1, even] = 1.0
    return table.astype(BF16)


def dot(a, b):
    return jnp.dot(a, b, preferred_element_type=F32)


def pick_kernel(points_ref, tiles_ref, out_ref):
    rows = tiles_ref.shape[1]
    lane = lax.broadcasted_iota(jnp.int32, (rows, LANES), 1)

    @pl.loop(0, out_ref.shape[0])
    def _(group):
        def step(m, total):
            point = points_ref[group * LANES + m]
            tile = tiles_ref[lax.shift_right_logical(point, 7)].astype(F32)
            return jnp.where(lane == m, pltpu.roll(tile, (m - point) & (LANES - 1), 1), total)

        total = lax.fori_loop(0, LANES, step, jnp.zeros((rows, LANES), F32), unroll=32)
        out_ref[group] = total.astype(BF16)


def pick(tiles, points):
    groups = points.shape[0] // LANES
    rows = tiles.shape[1]
    out = pl.pallas_call(
        pick_kernel,
        in_specs=[pl.BlockSpec(memory_space=pltpu.SMEM), pl.BlockSpec(memory_space=pltpu.VMEM)],
        out_specs=pl.BlockSpec(memory_space=pltpu.VMEM),
        out_shape=jax.ShapeDtypeStruct((groups, rows, LANES), BF16),
        compiler_params=pltpu.CompilerParams(vmem_limit_bytes=VMEM_BYTES),
        name="pick_points",
    )(points, tiles)
    return out.transpose(1, 0, 2).reshape(rows, groups * LANES)


def coef_kernel(*refs):
    groups, turn_ref, own_ref, src_ref = refs[:-3], refs[-3], refs[-2], refs[-1]
    nu = groups[0].shape[3]
    own = jnp.concatenate([g[k, 0] for g in groups for k in range(g.shape[0])], axis=0)
    src = jnp.concatenate([g[k, 1] for g in groups for k in range(g.shape[0])], axis=0)
    turn = turn_ref[...]
    own_ref[:nu] = own.astype(F32).T.astype(BF16)
    own_ref[nu:] = dot(turn, own).T.astype(BF16)
    src_ref[:, :nu] = -src
    src_ref[:, nu:] = (-dot(turn, src)).astype(BF16)


def coefficients(groups, turn):
    _, _, rows, nu = groups[0].shape
    high = sum(g.shape[0] for g in groups) * rows
    return pl.pallas_call(
        coef_kernel,
        out_shape=(
            jax.ShapeDtypeStruct((2 * nu, high), BF16),
            jax.ShapeDtypeStruct((high, 2 * nu), BF16),
        ),
        compiler_params=pltpu.CompilerParams(vmem_limit_bytes=VMEM_BYTES),
        cost_estimate=pl.CostEstimate(flops=1, bytes_accessed=1, transcendentals=0),
        name="coefficients",
    )(*groups, turn)


def exchange_kernel(first_plane, planes, cells, pairs, inputs, me_ref, *refs):
    arrays = refs[:inputs]
    own_ref, src_ref, coulomb_ref, table_ref, turn_ref = refs[inputs : inputs + 5]
    outs, after_ref, grid_ref, turned_ref = refs[inputs + 5 : -3], refs[-3], refs[-2], refs[-1]
    me = me_ref[0]
    after_ref[0] = me
    nu = coulomb_ref.shape[0]
    rows = arrays[0].shape[2]
    high = len(cells) * rows
    wide = 2 * LANES
    parts = GY * GZ // wide

    @pl.loop(0, planes)
    def _(p):
        down = pl.ds(pl.multiple_of(p * high, high), high)
        for part in range(parts):
            columns = slice(part * wide, (part + 1) * wide)
            tile = (p * parts + part) * 2
            wave = jnp.concatenate(
                [jnp.concatenate([arrays[a][lead(me), tile + t] for a, lead in cells], axis=0) for t in range(2)],
                axis=1,
            )
            density = dot(own_ref[...], wave)
            here = pl.ds(pl.multiple_of((first_plane + p) * GY * GZ + part * wide, wide), wide)
            coulomb = coulomb_ref[:, here].astype(F32)
            weighted = jnp.concatenate(
                [(coulomb * density[:nu]).astype(BF16), (coulomb * density[nu:]).astype(BF16)], axis=0
            )
            field = dot(src_ref[...], weighted).astype(BF16)
            grid_ref[down, columns] = field
            turned_ref[down, columns] = (-dot(turn_ref[...], field)).astype(BF16)

    waves = (dot(grid_ref[...], table_ref[0]) + dot(turned_ref[...], table_ref[1])).astype(BF16)
    side = me % 2
    for p in range(planes):
        for at, (out, half) in enumerate(pairs):
            block = waves[p * high + at * rows : p * high + (at + 1) * rows]
            if half is None:
                outs[out][p] = block
            else:
                outs[out][side ^ half, p] = block


def exchange(me, cells, own, src, coulomb, table, turn, first_plane, planes, pairs):
    arrays, places = distinct(cells)
    rows = arrays[0].shape[2]
    high = len(cells) * rows
    area = GY * GZ
    outs = 1 + max(out for out, _ in pairs)
    halves = () if pairs[0][1] is None else (2,)
    vmem = pl.BlockSpec(memory_space=pltpu.VMEM)
    smem = pl.BlockSpec(memory_space=pltpu.SMEM)
    *sent, after = pl.pallas_call(
        lambda *refs: exchange_kernel(first_plane, planes, places, pairs, len(arrays), *refs),
        in_specs=[smem] + [vmem] * (len(arrays) + 5),
        out_specs=[vmem] * outs + [smem],
        out_shape=[jax.ShapeDtypeStruct(halves + (planes, rows, area), BF16)] * outs
        + [jax.ShapeDtypeStruct((1,), jnp.int32)],
        scratch_shapes=[pltpu.VMEM((planes * high, area), BF16)] * 2,
        compiler_params=pltpu.CompilerParams(vmem_limit_bytes=VMEM_BYTES),
        cost_estimate=pl.CostEstimate(flops=1, bytes_accessed=1, transcendentals=0),
        name="exchange_planes",
    )(me, *arrays, own, src, coulomb, table, turn)
    return sent, after


def collect_kernel(plan, inputs, me_ref, *refs):
    arrays, outs = refs[:inputs], refs[inputs : inputs + len(plan)]
    buffer, in_sems, out_sems = refs[-3:]
    me = me_ref[0]
    ins, backs = [], []
    for out, picks in enumerate(plan):
        for at, (array, lead) in enumerate(picks):
            n = len(ins)
            ins.append(pltpu.make_async_copy(arrays[array].at[lead(me)], buffer.at[n], in_sems.at[n]))
            backs.append(pltpu.make_async_copy(buffer.at[n], outs[out].at[at], out_sems.at[n]))
    for copy in ins:
        copy.start()
    for copy, back in zip(ins, backs):
        copy.wait()
        back.start()
    for back in backs:
        back.wait()


def distinct(picks):
    arrays, places = [], []
    for array, lead in picks:
        at = next((i for i, a in enumerate(arrays) if a is array), len(arrays))
        if at == len(arrays):
            arrays.append(array)
        places.append((at, lead))
    return arrays, places


def collect(me, wanted):
    arrays, places = distinct([pick for picks in wanted for pick in picks])
    plan, at = [], 0
    for picks in wanted:
        plan.append(places[at : at + len(picks)])
        at += len(picks)
    hbm = pl.BlockSpec(memory_space=pltpu.HBM)
    return pl.pallas_call(
        lambda *refs: collect_kernel(plan, len(arrays), *refs),
        in_specs=[pl.BlockSpec(memory_space=pltpu.SMEM)] + [hbm] * len(arrays),
        out_specs=[hbm] * len(wanted),
        out_shape=[
            jax.ShapeDtypeStruct((len(picks),) + picks[0][0].shape[1:], picks[0][0].dtype) for picks in wanted
        ],
        scratch_shapes=[
            pltpu.VMEM((len(places),) + arrays[0].shape[1:], arrays[0].dtype),
            pltpu.SemaphoreType.DMA((len(places),)),
            pltpu.SemaphoreType.DMA((len(places),)),
        ],
        compiler_params=pltpu.CompilerParams(vmem_limit_bytes=VMEM_BYTES),
        cost_estimate=pl.CostEstimate(flops=1, bytes_accessed=1, transcendentals=0),
        name="collect_blocks",
    )(me, *arrays)


def line_kernel(factor, group_rows, count, *refs):
    fields, table_ref, out_ref = refs[1:-2], refs[-2], refs[-1]
    start = pl.multiple_of(pl.program_id(0) * group_rows, group_rows)
    picked = [
        f[p, pl.ds(start, group_rows)]
        for c in range(0, len(fields), count)
        for p in range(fields[c].shape[0])
        for f in fields[c : c + count]
    ]
    lines = dot(table_ref[0], jnp.concatenate(picked, axis=0)) * factor
    lines = lines.astype(BF16)
    for t in range(out_ref.shape[1]):
        tile = lines[:, t * LANES : (t + 1) * LANES]
        out_ref[:, t] = tile.reshape(tile.shape[0] // 2, 2, LANES)


def line_pass(me, fields, table, factor, rows, groups, count):
    area = GY * GZ
    group_rows = rows // groups
    tiles = area // LANES
    height = rows // 2 * GX

    def picked(array, lead):
        return pl.BlockSpec((None,) + array.shape[1:], lambda g, me: (lead(me[0]), 0, 0, 0))

    spec = pltpu.PrefetchScalarGridSpec(
        num_scalar_prefetch=1,
        grid=(groups,),
        in_specs=[picked(*f) for f in fields]
        + [pl.BlockSpec((1,) + table.shape[1:], lambda g, me: (me[0], 0, 0))],
        out_specs=pl.BlockSpec((height // groups, tiles, 2, LANES), lambda g, me: (g, 0, 0, 0)),
    )
    return pl.pallas_call(
        lambda *refs: line_kernel(factor, group_rows, count, *refs),
        grid_spec=spec,
        out_shape=jax.ShapeDtypeStruct((height, tiles, 2, LANES), BF16),
        compiler_params=pltpu.CompilerParams(vmem_limit_bytes=VMEM_BYTES),
        cost_estimate=pl.CostEstimate(flops=1, bytes_accessed=1, transcendentals=0),
        name="line_pass",
    )(me, *[array for array, _ in fields], table)


def hop(array, distance, count):
    return lax.ppermute(array, "band", [(i, i ^ distance) for i in range(count)])


def body(orbitals, points, partner, coulomb):
    _, bands, _, all_cells = orbitals.shape
    rows = 2 * bands
    count = lax.axis_size("band")
    me = lax.axis_index("band")
    planes = GX // count
    chunks = 2 if planes % 2 == 0 else 1
    chunk_planes = planes // chunks
    plane_tiles = GY * GZ // LANES
    chunk_tiles = chunk_planes * plane_tiles

    order = list(range(0, count, 2)) + list(range(1, count, 2))

    tiles = orbitals.reshape(1, bands, 2, all_cells // LANES, LANES).transpose(0, 3, 1, 2, 4)
    tiles = lax.optimization_barrier(tiles.reshape(all_cells // LANES, rows, LANES))
    blocks = tiles.reshape(count * chunks, chunk_tiles, rows, LANES)
    scale = table_scale(GX)
    turn = jnp.asarray(turn_table(count * rows))
    device = jnp.reshape(me, (1,)).astype(jnp.int32)

    def first(me):
        return 0

    def swap_pairs(pairs, me):
        (other,) = collect(me, [[(pairs[d], lambda me: 1 - me % 2) for d in sorted(pairs)]])
        swapped = hop(other, 1, count)
        return [
            (swapped, lambda me, k=k: k // 2) if k % 2 else (pairs[k], lambda me: me % 2)
            for k in order
        ]

    def cross(c, me):
        wanted = [
            [(blocks, lambda me, d=d, y=y: ((me ^ d) // 2 * 2 + y) * chunks + c) for y in range(2)]
            for d in range(0, count, 2)
        ]
        pairs = dict(zip(range(0, count, 2), collect(me, wanted)))
        return {d: hop(pair, d, count) if d else pair for d, pair in pairs.items()}

    own_values = pick(tiles, points)
    everyone = lax.all_gather(own_values, "kgrp", axis=0, tiled=False)
    chosen = partner == lax.axis_index("kgrp")
    src_values = jnp.sum(jnp.where(chosen[:, None, None], everyone, jnp.zeros_like(everyone)), axis=0)
    both = jnp.stack([own_values, src_values])[None]
    over_z = [both] + [hop(both, d, count) for d in range(2, count, 2)]
    crossing = [cross(c, device) for c in range(chunks)]
    (here,) = collect(device, [[(part, first) for part in over_z]])
    own_coef, src_coef = coefficients([here, hop(here, 1, count)], turn)

    plane_t = jnp.asarray(plane_table(scale))
    groups = 2 if bands % 16 == 0 else 1
    line_t = jnp.asarray(line_table(scale, order, planes, bands // groups))

    received = swap_pairs(crossing[0], device)
    fields = []
    waiting = None
    for c in range(chunks):
        last = c == chunks - 1
        pairs = [(at, None) if last else (k // 2, k % 2) for at, k in enumerate(order)]
        sent, after = exchange(
            device, received, own_coef, src_coef, coulomb, plane_t, turn, c * chunk_planes, chunk_planes, pairs
        )
        if waiting is not None:
            fields += swap_pairs(waiting, after)
        if last:
            back = {}
            for k in sorted(order, reverse=True):
                at = order.index(k)
                back[k] = hop(sent[at], k, count) if k else sent[at]
            fields += [(back[k][None], first) for k in order]
        else:
            waiting = {d: hop(sent[d // 2], d, count) if d else sent[0] for d in range(0, count, 2)}
            received = swap_pairs(crossing[c + 1], after)

    factor = 1.0 / (scale * scale * math.sqrt(GX * GY * GZ))
    out = line_pass(device, fields, line_t, factor, rows, groups, count)
    out = out.reshape(bands, all_cells // LANES, 2, LANES).transpose(0, 2, 1, 3)
    return out.reshape(1, bands, 2, all_cells)


def solution(mesh):
    return jax.shard_map(
        body,
        mesh=mesh,
        in_specs=(P("kgrp", "band", None, None), P(), P(), P(None, "band")),
        out_specs=P("kgrp", "band", None, None),
        check_vma=False,
    )
```

time: 143 us -> 132 us (0.923)
  starting transfers between devices: 57.3 us -> 41.6 us
  waiting for transfers between devices: 29.3 us -> 41.4 us
  Pallas kernels: 37 us -> 32.2 us
    ppermute x31 -> x23, starting transfers between devices: 57.3 us -> 41.6 us  [hop(): lax.ppermute(array, 'band', [(i, i ^ distance) for i in range(count)])]
    ppermute x31 -> x23, waiting for transfers between devices: 29.3 us -> 41.4 us  [hop(): lax.ppermute(array, 'band', [(i, i ^ distance) for i in range(count)])]
    another operation x3 -> x0, local copies, waits for them, and re-layouts: 9.71 us -> none  [the longest x2 6.8 us: body(): resident.reshape(bands, 2, all_cells // LANES, LANES).transpose(0, 2, 1, 3)]
    unnamed x64 -> x24, local copies, waits for them, and re-layouts: 0.7 us -> 8.9 us
    pallas_call x1, Pallas kernels: 10.2 us -> 2.93 us  [pick(): pl.pallas_call(pick_kernel, in_specs=[pl.BlockSpec(memory_space=pltpu.SME...]
    pallas_call x3 -> x9, Pallas kernels: 21.5 us -> 25.7 us  [the longest x2 13.6 us: exchange(): pl.pallas_call(lambda *refs: exchange_kernel(first_plane, planes, places,...]
    pallas_call x1, Pallas kernels: 5.3 us -> 3.55 us  [line_pass(): pl.pallas_call(lambda *refs: line_kernel(factor, group_rows, count, *refs...]
    reshape x0 -> x1, local copies, waits for them, and re-layouts: none -> 1.44 us  [body(): orbitals.reshape(1, bands, 2, all_cells // LANES, LANES)]
  transfers between devices with their start and end apart: 31 -> 23, of which waited for: 8 -> 8; matrix products, arithmetic and copies ran while one was open for 3% -> 0% of each run, Pallas kernels for 15% -> 16%
where the time goes in v1:
time: 132 us; the launch traced here: 131 us
  starting transfers between devices  41.6 us (32%)
  waiting for transfers between devices  41.4 us (31%)
  Pallas kernels  32.2 us (24%)
  local copies, waits for them, and re-layouts  10.4 us (8%)
  blocking collectives  5.56 us (4%)
    ppermute x23, starting transfers between devices, hop(): lax.ppermute(array, 'band', [(i, i ^ distance) for i in range(count)])  41.6 us
    ppermute x23, waiting for transfers between devices, hop(): lax.ppermute(array, 'band', [(i, i ^ distance) for i in range(count)])  41.4 us
    pallas_call x2, Pallas kernels, exchange(): pl.pallas_call(lambda *refs: exchange_kernel(first_plane, planes, places,...  13.6 us
    pallas_call x6, Pallas kernels, collect(): pl.pallas_call(lambda *refs: collect_kernel(plan, len(arrays), *refs), in...  11.8 us
    unnamed x24, local copies, waits for them, and re-layouts  8.9 us
    all_gather x1, blocking collectives, body(): everyone = lax.all_gather(own_values, 'kgrp', axis=0, tiled=False)  5.56 us
    pallas_call x1, Pallas kernels, line_pass(): pl.pallas_call(lambda *refs: line_kernel(factor, group_rows, count, *refs...  3.55 us
    pallas_call x1, Pallas kernels, pick(): pl.pallas_call(pick_kernel, in_specs=[pl.BlockSpec(memory_space=pltpu.SME...  2.93 us
  transfers between devices with their start and end apart: 23, of which 8 were waited for; matrix products, arithmetic and copies ran while one was open for 0% of the time, Pallas kernels for 16%

profile of v1, /device:TPU:0, one launch (start us, length us, event | category | flops | bytes accessed | tf_op | source)
XLA Modules:
  0.0 131.5 jit_solution(3806383559195887561)
XLA Ops:
  0.0 1.6 %copy-done = bf16[1,16,2,32768]{3,2,1,0:T(2,128)(2,1)S(1)} copy-done((bf16[1,16,2,32768]{3,2,1,0:T(2,128)(2,1)S(1)}, bf16[1,16,2,32768]{3,2,1,0:T(2,128)(2,1)}, u32[]{:S(2)}) %copy-start) | copy-done | bytes 2097176
  1.6 1.4 %copy_bitcast_fusion = bf16[1,16,2,256,128]{4,2,1,3,0:T(2,128)(2,1)S(1)} fusion(bf16[1,16,2,32768]{3,2,1,0:T(2,128)(2,1)S(1)} %copy-done), kind=kLoop, calls=%fused_computation | loop fusion | bytes 4194304 | tf_op jit(solution)/shard_map/reshape | solution.py:304
  3.1 2.7 %collect_blocks.6 = (bf16[2,16,32,128]{3,2,1,0:T(8,128)(2,1)S(1)}, bf16[2,16,32,128]{3,2,1,0:T(8,128)(2,1)}, bf16[2,16,32,128]{3,2,1,0:T(8,128)(2,1)}, bf16[2,16,32,128]{3,2,1,0:T(8,128)(2,1)S(1)}) custom-call(s32[1]{0:T(128)} %bitcast.refs_0_, bf16[16,16,32,128]{3,2,1,0:T(8,128)(2,1)S(1)} %bitcast.27), custom_call_target="tpu_custom_call" | custom-call | flops 1 | bytes 1 | tf_op jit(solution)/shard_map/collect_blocks/pallas_call | solution.py:227
  5.7 1.3 copy-done.1
  7.0 3.0 %collective-permute-start = (bf16[2,16,32,128]{3,2,1,0:T(8,128)(2,1)}, bf16[2,16,32,128]{3,2,1,0:T(8,128)(2,1)S(1)}, u32[]{:S(2)}, u32[]{:S(2)}) collective-permute-start(bf16[2,16,32,128]{3,2,1,0:T(8,128)(2,1)} %get-tuple-element.30), channel_id=1, source_target_pairs={{0,2},{1,3},{2,0},{3,1},{4,6},{5,7},{6,4},{7,5},{8,10},{9,11},{10,... | collective-permute-start | bytes 786440 | tf_op jit(solution)/shard_map/ppermute | solution.py:288
  10.1 2.6 %collective-permute-start.1 = (bf16[2,16,32,128]{3,2,1,0:T(8,128)(2,1)}, bf16[2,16,32,128]{3,2,1,0:T(8,128)(2,1)S(1)}, u32[]{:S(2)}, u32[]{:S(2)}) collective-permute-start(bf16[2,16,32,128]{3,2,1,0:T(8,128)(2,1)} %get-tuple-element.31), channel_id=1, source_target_pairs={{0,4},{1,5},{2,6},{3,7},{4,0},{5,1},{6,2},{7,3},{8,12},{9,13},{10,... | collective-permute-start | bytes 786440 | tf_op jit(solution)/shard_map/ppermute | solution.py:288
  12.7 1.6 %copy-done.2 = bf16[1,16,2,256,128]{4,2,1,3,0:T(2,128)(2,1)S(1)} copy-done((bf16[1,16,2,256,128]{4,2,1,3,0:T(2,128)(2,1)S(1)}, bf16[1,16,2,256,128]{4,2,1,3,0:T(2,128)(2,1)}, u32[]{:S(2)}) %copy-start.2) | copy-done | bytes 2097176
  14.3 2.9 %pick_points.1 = bf16[4,32,128]{2,1,0:T(8,128)(2,1)S(1)} custom-call(s32[512]{0:T(512)S(1)} %copy-done.10, bf16[256,32,128]{2,1,0:T(8,128)(2,1)S(1)} %bitcast.28), custom_call_target="tpu_custom_call" | custom-call | tf_op jit(solution)/shard_map/pick_points/pallas_call | solution.py:87
  17.3 5.6 %all_gather.3 = bf16[4,32,512]{2,1,0:T(8,128)(2,1)S(1)} all-gather(bf16[1,32,512]{2,1,0:T(8,128)(2,1)S(1)} %stack_reshape.3), channel_id=1, replica_groups=mesh['kgrp'=4,'band'=8] {'kgrp'}, dimensions={0}, use_global_device_ids=true | all-gather | bytes 163840 | tf_op jit(solution)/shard_map/all_gather | solution.py:331
  22.8 8.8 %collective-permute-done.1.refs_3_ = bf16[2,16,32,128]{3,2,1,0:T(8,128)(2,1)S(1)} collective-permute-done((bf16[2,16,32,128]{3,2,1,0:T(8,128)(2,1)}, bf16[2,16,32,128]{3,2,1,0:T(8,128)(2,1)S(1)}, u32[]{:S(2)}, u32[]{:S(2)}) %collective-permute-start.1) | collective-permute-done | bytes 262176 | tf_op jit(solution)/shard_map/ppermute | solution.py:288
  31.6 1.4 %collect_blocks.7 = bf16[4,16,32,128]{3,2,1,0:T(8,128)(2,1)S(1)} custom-call(s32[1]{0:T(128)} %bitcast.refs_0_, bf16[2,16,32,128]{3,2,1,0:T(8,128)(2,1)S(1)} %get-tuple-element.29.refs_1_, bf16[2,16,32,128]{3,2,1,0:T(8,128)(2,1)S(1)} %collective-permute-done.refs_2_, bf16[2,16,32,128]{3,2,1,0:T(8,128)(2,1)S(1)} %collective-permute-done.1.refs_3_, ...), custom_call_target="tpu_custom_call" | custom-call | flops 1 | bytes 1 | tf_op jit(solution)/shard_map/collect_blocks/pallas_call | solution.py:227
  33.1 1.6 %collective-permute-start.3 = (bf16[4,16,32,128]{3,2,1,0:T(8,128)(2,1)S(1)}, bf16[4,16,32,128]{3,2,1,0:T(8,128)(2,1)S(1)}, u32[]{:S(2)}, u32[]{:S(2)}) collective-permute-start(bf16[4,16,32,128]{3,2,1,0:T(8,128)(2,1)S(1)} %collect_blocks.7), channel_id=1, source_target_pairs={{0,1},{1,0},{2,3},{3,2},{4,5},{5,4},{6,7},{7,6},{8,9},{9,8},{10,11... | collective-permute-start | bytes 1572872 | tf_op jit(solution)/shard_map/ppermute | solution.py:288
  34.7 0.1 select_reduce_fusion
  34.8 2.5 %collective-permute-start.6 = (bf16[1,2,32,512]{3,2,1,0:T(8,128)(2,1)S(1)}, bf16[1,2,32,512]{3,2,1,0:T(8,128)(2,1)S(1)}, u32[]{:S(2)}, u32[]{:S(2)}) collective-permute-start(bf16[1,2,32,512]{3,2,1,0:T(8,128)(2,1)S(1)} %maximum_bitcast_fusion.refs_1_), channel_id=1, source_target_pairs={{0,6},{1,7},{2,4},{3,5},{4,2},{5,3},{6,0},{7,1},{8,14},{9,15},{10,... | collective-permute-start | bytes 196616 | tf_op jit(solution)/shard_map/ppermute | solution.py:288
  37.3 4.4 %collective-permute-start.5 = (bf16[1,2,32,512]{3,2,1,0:T(8,128)(2,1)S(1)}, bf16[1,2,32,512]{3,2,1,0:T(8,128)(2,1)S(1)}, u32[]{:S(2)}, u32[]{:S(2)}) collective-permute-start(bf16[1,2,32,512]{3,2,1,0:T(8,128)(2,1)S(1)} %maximum_bitcast_fusion.refs_1_), channel_id=1, source_target_pairs={{0,4},{1,5},{2,6},{3,7},{4,0},{5,1},{6,2},{7,3},{8,12},{9,13},{10,... | collective-permute-start | bytes 196616 | tf_op jit(solution)/shard_map/ppermute | solution.py:288
  41.7 0.1 collective-permute-start.4
  41.9 3.2 %collective-permute-done.5.refs_3_ = bf16[1,2,32,512]{3,2,1,0:T(8,128)(2,1)S(1)} collective-permute-done((bf16[1,2,32,512]{3,2,1,0:T(8,128)(2,1)S(1)}, bf16[1,2,32,512]{3,2,1,0:T(8,128)(2,1)S(1)}, u32[]{:S(2)}, u32[]{:S(2)}) %collective-permute-start.5) | collective-permute-done | bytes 65568 | tf_op jit(solution)/shard_map/ppermute | solution.py:288
  45.0 1.0 collective-permute-done.4.refs_2_
  46.0 0.7 collect_blocks.8.refs_0_
  46.7 0.2 collective-permute-start.7
  46.9 2.8 %collect_blocks.9 = (bf16[2,16,32,128]{3,2,1,0:T(8,128)(2,1)S(1)}, bf16[2,16,32,128]{3,2,1,0:T(8,128)(2,1)S(1)}, bf16[2,16,32,128]{3,2,1,0:T(8,128)(2,1)S(1)}, bf16[2,16,32,128]{3,2,1,0:T(8,128)(2,1)S(1)}) custom-call(s32[1]{0:T(128)} %bitcast.refs_0_, bf16[16,16,32,128]{3,2,1,0:T(8,128)(2,1)S(1)} %bitcast.29), custom_call_target="tpu_custom_call" | custom-call | flops 1 | bytes 1 | tf_op jit(solution)/shard_map/collect_blocks/pallas_call | solution.py:227
  49.8 1.5 %collective-permute-start.11 = (bf16[2,16,32,128]{3,2,1,0:T(8,128)(2,1)S(1)}, bf16[2,16,32,128]{3,2,1,0:T(8,128)(2,1)S(1)}, u32[]{:S(2)}, u32[]{:S(2)}) collective-permute-start(bf16[2,16,32,128]{3,2,1,0:T(8,128)(2,1)S(1)} %get-tuple-element.40), channel_id=1, source_target_pairs={{0,2},{1,3},{2,0},{3,1},{4,6},{5,7},{6,4},{7,5},{8,10},{9,11},{10,... | collective-permute-start | bytes 786440 | tf_op jit(solution)/shard_map/ppermute | solution.py:288
  51.3 2.1 %collective-permute-start.12 = (bf16[2,16,32,128]{3,2,1,0:T(8,128)(2,1)S(1)}, bf16[2,16,32,128]{3,2,1,0:T(8,128)(2,1)S(1)}, u32[]{:S(2)}, u32[]{:S(2)}) collective-permute-start(bf16[2,16,32,128]{3,2,1,0:T(8,128)(2,1)S(1)} %get-tuple-element.41), channel_id=1, source_target_pairs={{0,4},{1,5},{2,6},{3,7},{4,0},{5,1},{6,2},{7,3},{8,12},{9,13},{10,... | collective-permute-start | bytes 786440 | tf_op jit(solution)/shard_map/ppermute | solution.py:288
  53.4 0.9 collective-permute-start.13
  54.3 0.3 coefficients.1
  54.6 2.2 %copy-done.4 = bf16[512,4096]{1,0:T(8,128)(2,1)S(1)} copy-done((bf16[512,4096]{1,0:T(8,128)(2,1)S(1)}, bf16[512,4096]{1,0:T(8,128)(2,1)}, u32[]{:S(2)}) %copy-start.4) | copy-done | bytes 4194328
  56.8 2.2 %copy-done.6 = bf16[2,1024,1024]{2,1,0:T(8,128)(2,1)S(1)} copy-done((bf16[2,1024,1024]{2,1,0:T(8,128)(2,1)S(1)}, bf16[2,1024,1024]{2,1,0:T(8,128)(2,1)}, u32[]{:S(2)}) %copy-start.6) | copy-done | bytes 4194328
  59.0 6.9 %exchange_planes.2 = (bf16[2,2,32,1024]{3,2,1,0:T(8,128)(2,1)S(1)}, bf16[2,2,32,1024]{3,2,1,0:T(8,128)(2,1)S(1)}, bf16[2,2,32,1024]{3,2,1,0:T(8,128)(2,1)S(1)}, bf16[2,2,32,1024]{3,2,1,0:T(8,128)(2,1)S(1)}, s32[1]{0:T(128)}) custom-call(s32[1]{0:T(128)} %bitcast.refs_0_, bf16[2,16,32,128]{3,2,1,0:T(8,128)(2,1)S(1)} %get-tuple-element.29.refs_1_, ...), custom_call_target="tpu_custom_call" | custom-call | flops 1 | bytes 1 | tf_op jit(solution)/shard_map/exchange_planes/pallas_call | solution.py:177
  65.9 4.9 %collective-permute-done.12.refs_3_ = bf16[2,16,32,128]{3,2,1,0:T(8,128)(2,1)S(1)} collective-permute-done((bf16[2,16,32,128]{3,2,1,0:T(8,128)(2,1)S(1)}, bf16[2,16,32,128]{3,2,1,0:T(8,128)(2,1)S(1)}, u32[]{:S(2)}, u32[]{:S(2)}) %collective-permute-start.12) | collective-permute-done | bytes 262176 | tf_op jit(solution)/shard_map/ppermute | solution.py:288
  70.8 2.1 %collect_blocks.10 = bf16[4,16,32,128]{3,2,1,0:T(8,128)(2,1)S(1)} custom-call(s32[1]{0:T(128)} %get-tuple-element.43.refs_0_, bf16[2,16,32,128]{3,2,1,0:T(8,128)(2,1)S(1)} %get-tuple-element.39.refs_1_, bf16[2,16,32,128]{3,2,1,0:T(8,128)(2,1)S(1)} %collective-permute-done.11.refs_2_, bf16[2,16,32,128]{3,2,1,0:T(8,128)(2,1)S(1)} %collective-permute-done.12.refs_3_, ...), custom_call_target="tpu_custom_call" | custom-call | flops 1 | bytes 1 | tf_op jit(solution)/shard_map/collect_blocks/pallas_call | solution.py:227
  72.9 1.7 %collective-permute-start.14 = (bf16[4,16,32,128]{3,2,1,0:T(8,128)(2,1)S(1)}, bf16[4,16,32,128]{3,2,1,0:T(8,128)(2,1)S(1)}, u32[]{:S(2)}, u32[]{:S(2)}) collective-permute-start(bf16[4,16,32,128]{3,2,1,0:T(8,128)(2,1)S(1)} %collect_blocks.10), channel_id=1, source_target_pairs={{0,1},{1,0},{2,3},{3,2},{4,5},{5,4},{6,7},{7,6},{8,9},{9,8},{10,11... | collective-permute-start | bytes 1572872 | tf_op jit(solution)/shard_map/ppermute | solution.py:288
  74.6 3.4 %collective-permute-start.8 = (bf16[2,2,32,1024]{3,2,1,0:T(8,128)(2,1)S(1)}, bf16[2,2,32,1024]{3,2,1,0:T(8,128)(2,1)S(1)}, u32[]{:S(2)}, u32[]{:S(2)}) collective-permute-start(bf16[2,2,32,1024]{3,2,1,0:T(8,128)(2,1)S(1)} %get-tuple-element.36), channel_id=1, source_target_pairs={{0,2},{1,3},{2,0},{3,1},{4,6},{5,7},{6,4},{7,5},{8,10},{9,11},{10,... | collective-permute-start | bytes 786440 | tf_op jit(solution)/shard_map/ppermute | solution.py:288
  78.0 1.0 collective-permute-start.9
  78.9 1.5 %collective-permute-start.10 = (bf16[2,2,32,1024]{3,2,1,0:T(8,128)(2,1)S(1)}, bf16[2,2,32,1024]{3,2,1,0:T(8,128)(2,1)S(1)}, u32[]{:S(2)}, u32[]{:S(2)}) collective-permute-start(bf16[2,2,32,1024]{3,2,1,0:T(8,128)(2,1)S(1)} %get-tuple-element.38), channel_id=1, source_target_pairs={{0,6},{1,7},{2,4},{3,5},{4,2},{5,3},{6,0},{7,1},{8,14},{9,15},{10,... | collective-permute-start | bytes 786440 | tf_op jit(solution)/shard_map/ppermute | solution.py:288
  80.4 1.7 %collective-permute-done.14.refs_5_ = bf16[4,16,32,128]{3,2,1,0:T(8,128)(2,1)S(1)} collective-permute-done((bf16[4,16,32,128]{3,2,1,0:T(8,128)(2,1)S(1)}, bf16[4,16,32,128]{3,2,1,0:T(8,128)(2,1)S(1)}, u32[]{:S(2)}, u32[]{:S(2)}) %collective-permute-start.14) | collective-permute-done | bytes 524320 | tf_op jit(solution)/shard_map/ppermute | solution.py:288
  82.1 6.7 %exchange_planes.3 = (bf16[2,32,1024]{2,1,0:T(8,128)(2,1)S(1)}, bf16[2,32,1024]{2,1,0:T(8,128)(2,1)S(1)}, bf16[2,32,1024]{2,1,0:T(8,128)(2,1)S(1)}, bf16[2,32,10...) custom-call(s32[1]{0:T(128)} %bitcast.refs_0_, ...), custom_call_target="tpu_custom_call" | custom-call | flops 1 | bytes 1 | tf_op jit(solution)/shard_map/exchange_planes/pallas_call | solution.py:177
  88.8 8.7 %collective-permute-done.9.refs_3_ = bf16[2,2,32,1024]{3,2,1,0:T(8,128)(2,1)S(1)} collective-permute-done((bf16[2,2,32,1024]{3,2,1,0:T(8,128)(2,1)S(1)}, bf16[2,2,32,1024]{3,2,1,0:T(8,128)(2,1)S(1)}, u32[]{:S(2)}, u32[]{:S(2)}) %collective-permute-start.9) | collective-permute-done | bytes 262176 | tf_op jit(solution)/shard_map/ppermute | solution.py:288
  97.5 2.1 %collect_blocks.11 = bf16[4,2,32,1024]{3,2,1,0:T(8,128)(2,1)S(1)} custom-call(s32[1]{0:T(128)} %get-tuple-element.44.refs_0_, bf16[2,2,32,1024]{3,2,1,0:T(8,128)(2,1)S(1)} %get-tuple-element.35.refs_1_, bf16[2,2,32,1024]{3,2,1,0:T(8,128)(2,1)S(1)} %collective-permute-done.8.refs_2_, bf16[2,2,32,1024]{3,2,1,0:T(8,128)(2,1)S(1)} %collective-permute-done.9.refs_3_, ...), custom_call_target="tpu_custom_call" | custom-call | flops 1 | bytes 1 | tf_op jit(solution)/shard_map/collect_blocks/pallas_call | solution.py:227
  99.6 0.5 collective-permute-start.15
  100.1 3.4 %collective-permute-start.16 = (bf16[2,32,1024]{2,1,0:T(8,128)(2,1)S(1)}, bf16[2,32,1024]{2,1,0:T(8,128)(2,1)S(1)}, u32[]{:S(2)}, u32[]{:S(2)}) collective-permute-start(bf16[2,32,1024]{2,1,0:T(8,128)(2,1)S(1)} %get-tuple-element.46), channel_id=1, source_target_pairs={{0,2},{1,3},{2,0},{3,1},{4,6},{5,7},{6,4},{7,5},{8,10},{9,11},{10,... | collective-permute-start | bytes 393224 | tf_op jit(solution)/shard_map/ppermute | solution.py:288
  103.5 1.9 %collective-permute-start.17 = (bf16[2,32,1024]{2,1,0:T(8,128)(2,1)S(1)}, bf16[2,32,1024]{2,1,0:T(8,128)(2,1)S(1)}, u32[]{:S(2)}, u32[]{:S(2)}) collective-permute-start(bf16[2,32,1024]{2,1,0:T(8,128)(2,1)S(1)} %get-tuple-element.47), channel_id=1, source_target_pairs={{0,4},{1,5},{2,6},{3,7},{4,0},{5,1},{6,2},{7,3},{8,12},{9,13},{10,... | collective-permute-start | bytes 393224 | tf_op jit(solution)/shard_map/ppermute | solution.py:288
  105.4 1.5 %collective-permute-start.18 = (bf16[2,32,1024]{2,1,0:T(8,128)(2,1)S(1)}, bf16[2,32,1024]{2,1,0:T(8,128)(2,1)S(1)}, u32[]{:S(2)}, u32[]{:S(2)}) collective-permute-start(bf16[2,32,1024]{2,1,0:T(8,128)(2,1)S(1)} %get-tuple-element.48), channel_id=1, source_target_pairs={{0,6},{1,7},{2,4},{3,5},{4,2},{5,3},{6,0},{7,1},{8,14},{9,15},{10,... | collective-permute-start | bytes 393224 | tf_op jit(solution)/shard_map/ppermute | solution.py:288
  106.9 1.6 %collective-permute-start.19 = (bf16[2,32,1024]{2,1,0:T(8,128)(2,1)S(1)}, bf16[2,32,1024]{2,1,0:T(8,128)(2,1)S(1)}, u32[]{:S(2)}, u32[]{:S(2)}) collective-permute-start(bf16[2,32,1024]{2,1,0:T(8,128)(2,1)S(1)} %get-tuple-element.49), channel_id=1, source_target_pairs={{0,1},{1,0},{2,3},{3,2},{4,5},{5,4},{6,7},{7,6},{8,9},{9,8},{10,11... | collective-permute-start | bytes 393224 | tf_op jit(solution)/shard_map/ppermute | solution.py:288
  108.5 2.4 %collective-permute-start.20 = (bf16[2,32,1024]{2,1,0:T(8,128)(2,1)S(1)}, bf16[2,32,1024]{2,1,0:T(8,128)(2,1)S(1)}, u32[]{:S(2)}, u32[]{:S(2)}) collective-permute-start(bf16[2,32,1024]{2,1,0:T(8,128)(2,1)S(1)} %get-tuple-element.50), channel_id=1, source_target_pairs={{0,3},{1,2},{2,1},{3,0},{4,7},{5,6},{6,5},{7,4},{8,11},{9,10},{10,... | collective-permute-start | bytes 393224 | tf_op jit(solution)/shard_map/ppermute | solution.py:288
  110.8 6.2 %collective-permute-done.17 = bf16[2,32,1024]{2,1,0:T(8,128)(2,1)S(1)} collective-permute-done((bf16[2,32,1024]{2,1,0:T(8,128)(2,1)S(1)}, bf16[2,32,1024]{2,1,0:T(8,128)(2,1)S(1)}, u32[]{:S(2)}, u32[]{:S(2)}) %collective-permute-start.17) | collective-permute-done | bytes 131104 | tf_op jit(solution)/shard_map/ppermute | solution.py:288
  117.0 3.9 %collective-permute-start.22 = (bf16[2,32,1024]{2,1,0:T(8,128)(2,1)S(1)}, bf16[2,32,1024]{2,1,0:T(8,128)(2,1)S(1)}, u32[]{:S(2)}, u32[]{:S(2)}) collective-permute-start(bf16[2,32,1024]{2,1,0:T(8,128)(2,1)S(1)} %get-tuple-element.52), channel_id=1, source_target_pairs={{0,7},{1,6},{2,5},{3,4},{4,3},{5,2},{6,1},{7,0},{8,15},{9,14},{10,... | collective-permute-start | bytes 393224 | tf_op jit(solution)/shard_map/ppermute | solution.py:288
  120.9 7.0 %collective-permute-done.21 = bf16[2,32,1024]{2,1,0:T(8,128)(2,1)S(1)} collective-permute-done((bf16[2,32,1024]{2,1,0:T(8,128)(2,1)S(1)}, bf16[2,32,1024]{2,1,0:T(8,128)(2,1)S(1)}, u32[]{:S(2)}, u32[]{:S(2)}) %collective-permute-start.21) | collective-permute-done | bytes 131104 | tf_op jit(solution)/shard_map/ppermute | solution.py:288
  127.9 3.6 %line_pass.1 = bf16[512,8,2,128]{3,2,1,0:T(2,128)(2,1)} custom-call(s32[1]{0:T(128)} %bitcast.refs_0_, bf16[2,2,32,1024]{3,2,1,0:T(8,128)(2,1)S(1)} %get-tuple-element.35.refs_1_, bf16[2,2,32,1024]{3,2,1,0:T(8,128)(2,1)S(1)} %collective-permute-done.8.refs_2_, bf16[2,2,32,1024]{3,2,1,0:T(8,128)(2,1)S(1)} %collective-permute-done.9.refs_3_, ...), custom_call_target="tpu_custom_call" | custom-call | flops 1 | bytes 1 | tf_op jit(solution)/shard_map/line_pass/pallas_call | solution.py:277
  (40 shorter events, 0.1 us)
Async XLA Ops:
  0.0 1.6 %copy-start = (bf16[1,16,2,32768]{3,2,1,0:T(2,128)(2,1)S(1)}, bf16[1,16,2,32768]{3,2,1,0:T(2,128)(2,1)}, u32[]{:S(2)}) copy-start(bf16[1,16,2,32768]{3,2,1,0:T(2,128)(2,1)} %param.7) | copy-start | bytes 6291460
  3.0 9.6 %copy-start.10 = (s32[512]{0:T(512)S(1)}, s32[512]{0:T(512)}, u32[]{:S(2)}) copy-start(s32[512]{0:T(512)} %points_ref.1) | copy-start | bytes 6148
  3.0 19.8 %copy-start.11 = (s32[4]{0:T(128)S(1)}, s32[4]{0:T(128)}, u32[]{:S(2)}) copy-start(s32[4]{0:T(128)} %param.9) | copy-start | bytes 52
  5.7 1.3 %copy-start.1 = (bf16[1,16,2,256,128]{4,2,1,3,0:T(2,128)(2,1)}, bf16[1,16,2,256,128]{4,2,1,3,0:T(2,128)(2,1)S(1)}, u32[]{:S(2)}) copy-start(bf16[1,16,2,256,128]{4,2,1,3,0:T(2,128)(2,1)S(1)} %copy_bitcast_fusion) | copy-start | bytes 6291460
  7.0 15.8 %collective-permute-start = (bf16[2,16,32,128]{3,2,1,0:T(8,128)(2,1)}, bf16[2,16,32,128]{3,2,1,0:T(8,128)(2,1)S(1)}, u32[]{:S(2)}, u32[]{:S(2)}) collective-permute-start(bf16[2,16,32,128]{3,2,1,0:T(8,128)(2,1)} %get-tuple-element.30), channel_id=1, source_target_pairs={{0,2},{1,3},{2,0},{3,1},{4,6},{5,7},{6,4},{7,5},{8,10},{9,11},{10,... | collective-permute-start | bytes 786440 | tf_op jit(solution)/shard_map/ppermute | solution.py:288
  10.1 21.6 %collective-permute-start.1 = (bf16[2,16,32,128]{3,2,1,0:T(8,128)(2,1)}, bf16[2,16,32,128]{3,2,1,0:T(8,128)(2,1)S(1)}, u32[]{:S(2)}, u32[]{:S(2)}) collective-permute-start(bf16[2,16,32,128]{3,2,1,0:T(8,128)(2,1)} %get-tuple-element.31), channel_id=1, source_target_pairs={{0,4},{1,5},{2,6},{3,7},{4,0},{5,1},{6,2},{7,3},{8,12},{9,13},{10,... | collective-permute-start | bytes 786440 | tf_op jit(solution)/shard_map/ppermute | solution.py:288
  12.7 19.0 %collective-permute-start.2 = (bf16[2,16,32,128]{3,2,1,0:T(8,128)(2,1)S(1)}, bf16[2,16,32,128]{3,2,1,0:T(8,128)(2,1)S(1)}, u32[]{:S(2)}, u32[]{:S(2)}) collective-permute-start(bf16[2,16,32,128]{3,2,1,0:T(8,128)(2,1)S(1)} %get-tuple-element.32), channel_id=1, source_target_pairs={{0,6},{1,7},{2,4},{3,5},{4,2},{5,3},{6,0},{7,1},{8,14},{9,15},{10,... | collective-permute-start | bytes 786440 | tf_op jit(solution)/shard_map/ppermute | solution.py:288
  12.7 1.6 %copy-start.2 = (bf16[1,16,2,256,128]{4,2,1,3,0:T(2,128)(2,1)S(1)}, bf16[1,16,2,256,128]{4,2,1,3,0:T(2,128)(2,1)}, u32[]{:S(2)}) copy-start(bf16[1,16,2,256,128]{4,2,1,3,0:T(2,128)(2,1)} %copy-done.1) | copy-start | bytes 6291460
  17.2 29.7 %copy-start.3 = (bf16[1,16,2,256,128]{4,2,1,3,0:T(2,128)(2,1)S(1)}, bf16[1,16,2,256,128]{4,2,1,3,0:T(2,128)(2,1)}, u32[]{:S(2)}) copy-start(bf16[1,16,2,256,128]{4,2,1,3,0:T(2,128)(2,1)} %copy-done.1) | copy-start | bytes 6291460
  31.6 22.6 %copy-start.9 = (bf16[256,256]{1,0:T(8,128)(2,1)S(1)}, bf16[256,256]{1,0:T(8,128)(2,1)}, u32[]{:S(2)}) copy-start(bf16[256,256]{1,0:T(8,128)(2,1)} %constant.18.clone.refs_2_.refs_10_) | copy-start | bytes 393220
  33.1 21.5 %collective-permute-start.3 = (bf16[4,16,32,128]{3,2,1,0:T(8,128)(2,1)S(1)}, bf16[4,16,32,128]{3,2,1,0:T(8,128)(2,1)S(1)}, u32[]{:S(2)}, u32[]{:S(2)}) collective-permute-start(bf16[4,16,32,128]{3,2,1,0:T(8,128)(2,1)S(1)} %collect_blocks.7), channel_id=1, source_target_pairs={{0,1},{1,0},{2,3},{3,2},{4,5},{5,4},{6,7},{7,6},{8,9},{9,8},{10,11... | collective-permute-start | bytes 1572872 | tf_op jit(solution)/shard_map/ppermute | solution.py:288
  34.8 7.1 %collective-permute-start.6 = (bf16[1,2,32,512]{3,2,1,0:T(8,128)(2,1)S(1)}, bf16[1,2,32,512]{3,2,1,0:T(8,128)(2,1)S(1)}, u32[]{:S(2)}, u32[]{:S(2)}) collective-permute-start(bf16[1,2,32,512]{3,2,1,0:T(8,128)(2,1)S(1)} %maximum_bitcast_fusion.refs_1_), channel_id=1, source_target_pairs={{0,6},{1,7},{2,4},{3,5},{4,2},{5,3},{6,0},{7,1},{8,14},{9,15},{10,... | collective-permute-start | bytes 196616 | tf_op jit(solution)/shard_map/ppermute | solution.py:288
  37.3 7.7 %collective-permute-start.5 = (bf16[1,2,32,512]{3,2,1,0:T(8,128)(2,1)S(1)}, bf16[1,2,32,512]{3,2,1,0:T(8,128)(2,1)S(1)}, u32[]{:S(2)}, u32[]{:S(2)}) collective-permute-start(bf16[1,2,32,512]{3,2,1,0:T(8,128)(2,1)S(1)} %maximum_bitcast_fusion.refs_1_), channel_id=1, source_target_pairs={{0,4},{1,5},{2,6},{3,7},{4,0},{5,1},{6,2},{7,3},{8,12},{9,13},{10,... | collective-permute-start | bytes 196616 | tf_op jit(solution)/shard_map/ppermute | solution.py:288
  41.7 4.3 %collective-permute-start.4 = (bf16[1,2,32,512]{3,2,1,0:T(8,128)(2,1)S(1)}, bf16[1,2,32,512]{3,2,1,0:T(8,128)(2,1)S(1)}, u32[]{:S(2)}, u32[]{:S(2)}) collective-permute-start(bf16[1,2,32,512]{3,2,1,0:T(8,128)(2,1)S(1)} %maximum_bitcast_fusion.refs_1_), channel_id=1, source_target_pairs={{0,2},{1,3},{2,0},{3,1},{4,6},{5,7},{6,4},{7,5},{8,10},{9,11},{10,... | collective-permute-start | bytes 196616 | tf_op jit(solution)/shard_map/ppermute | solution.py:288
  46.7 7.5 %collective-permute-start.7 = (bf16[4,2,32,512]{3,2,1,0:T(8,128)(2,1)S(1)}, bf16[4,2,32,512]{3,2,1,0:T(8,128)(2,1)S(1)}, u32[]{:S(2)}, u32[]{:S(2)}) collective-permute-start(bf16[4,2,32,512]{3,2,1,0:T(8,128)(2,1)S(1)} %collect_blocks.8.refs_0_), channel_id=1, source_target_pairs={{0,1},{1,0},{2,3},{3,2},{4,5},{5,4},{6,7},{7,6},{8,9},{9,8},{10,11... | collective-permute-start | bytes 786440 | tf_op jit(solution)/shard_map/ppermute | solution.py:288
  49.8 16.1 %collective-permute-start.11 = (bf16[2,16,32,128]{3,2,1,0:T(8,128)(2,1)S(1)}, bf16[2,16,32,128]{3,2,1,0:T(8,128)(2,1)S(1)}, u32[]{:S(2)}, u32[]{:S(2)}) collective-permute-start(bf16[2,16,32,128]{3,2,1,0:T(8,128)(2,1)S(1)} %get-tuple-element.40), channel_id=1, source_target_pairs={{0,2},{1,3},{2,0},{3,1},{4,6},{5,7},{6,4},{7,5},{8,10},{9,11},{10,... | collective-permute-start | bytes 786440 | tf_op jit(solution)/shard_map/ppermute | solution.py:288
  51.3 19.5 %collective-permute-start.12 = (bf16[2,16,32,128]{3,2,1,0:T(8,128)(2,1)S(1)}, bf16[2,16,32,128]{3,2,1,0:T(8,128)(2,1)S(1)}, u32[]{:S(2)}, u32[]{:S(2)}) collective-permute-start(bf16[2,16,32,128]{3,2,1,0:T(8,128)(2,1)S(1)} %get-tuple-element.41), channel_id=1, source_target_pairs={{0,4},{1,5},{2,6},{3,7},{4,0},{5,1},{6,2},{7,3},{8,12},{9,13},{10,... | collective-permute-start | bytes 786440 | tf_op jit(solution)/shard_map/ppermute | solution.py:288
  53.4 17.4 %collective-permute-start.13 = (bf16[2,16,32,128]{3,2,1,0:T(8,128)(2,1)S(1)}, bf16[2,16,32,128]{3,2,1,0:T(8,128)(2,1)S(1)}, u32[]{:S(2)}, u32[]{:S(2)}) collective-permute-start(bf16[2,16,32,128]{3,2,1,0:T(8,128)(2,1)S(1)} %get-tuple-element.42), channel_id=1, source_target_pairs={{0,6},{1,7},{2,4},{3,5},{4,2},{5,3},{6,0},{7,1},{8,14},{9,15},{10,... | collective-permute-start | bytes 786440 | tf_op jit(solution)/shard_map/ppermute | solution.py:288
  54.6 2.2 %copy-start.4 = (bf16[512,4096]{1,0:T(8,128)(2,1)S(1)}, bf16[512,4096]{1,0:T(8,128)(2,1)}, u32[]{:S(2)}) copy-start(bf16[512,4096]{1,0:T(8,128)(2,1)} %refs_8_.3) | copy-start | bytes 12582916
  56.8 2.2 %copy-start.6 = (bf16[2,1024,1024]{2,1,0:T(8,128)(2,1)S(1)}, bf16[2,1024,1024]{2,1,0:T(8,128)(2,1)}, u32[]{:S(2)}) copy-start(bf16[2,1024,1024]{2,1,0:T(8,128)(2,1)} %constant.19.clone.refs_9_) | copy-start | bytes 12582916
  59.0 23.1 %copy-start.5 = (bf16[512,4096]{1,0:T(8,128)(2,1)S(1)}, bf16[512,4096]{1,0:T(8,128)(2,1)}, u32[]{:S(2)}) copy-start(bf16[512,4096]{1,0:T(8,128)(2,1)} %refs_8_.3) | copy-start | bytes 12582916
  59.0 23.1 %copy-start.7 = (bf16[2,1024,1024]{2,1,0:T(8,128)(2,1)S(1)}, bf16[2,1024,1024]{2,1,0:T(8,128)(2,1)}, u32[]{:S(2)}) copy-start(bf16[2,1024,1024]{2,1,0:T(8,128)(2,1)} %constant.19.clone.refs_9_) | copy-start | bytes 12582916
  72.9 9.2 %collective-permute-start.14 = (bf16[4,16,32,128]{3,2,1,0:T(8,128)(2,1)S(1)}, bf16[4,16,32,128]{3,2,1,0:T(8,128)(2,1)S(1)}, u32[]{:S(2)}, u32[]{:S(2)}) collective-permute-start(bf16[4,16,32,128]{3,2,1,0:T(8,128)(2,1)S(1)} %collect_blocks.10), channel_id=1, source_target_pairs={{0,1},{1,0},{2,3},{3,2},{4,5},{5,4},{6,7},{7,6},{8,9},{9,8},{10,11... | collective-permute-start | bytes 1572872 | tf_op jit(solution)/shard_map/ppermute | solution.py:288
  74.6 14.2 %collective-permute-start.8 = (bf16[2,2,32,1024]{3,2,1,0:T(8,128)(2,1)S(1)}, bf16[2,2,32,1024]{3,2,1,0:T(8,128)(2,1)S(1)}, u32[]{:S(2)}, u32[]{:S(2)}) collective-permute-start(bf16[2,2,32,1024]{3,2,1,0:T(8,128)(2,1)S(1)} %get-tuple-element.36), channel_id=1, source_target_pairs={{0,2},{1,3},{2,0},{3,1},{4,6},{5,7},{6,4},{7,5},{8,10},{9,11},{10,... | collective-permute-start | bytes 786440 | tf_op jit(solution)/shard_map/ppermute | solution.py:288
  78.0 19.6 %collective-permute-start.9 = (bf16[2,2,32,1024]{3,2,1,0:T(8,128)(2,1)S(1)}, bf16[2,2,32,1024]{3,2,1,0:T(8,128)(2,1)S(1)}, u32[]{:S(2)}, u32[]{:S(2)}) collective-permute-start(bf16[2,2,32,1024]{3,2,1,0:T(8,128)(2,1)S(1)} %get-tuple-element.37), channel_id=1, source_target_pairs={{0,4},{1,5},{2,6},{3,7},{4,0},{5,1},{6,2},{7,3},{8,12},{9,13},{10,... | collective-permute-start | bytes 786440 | tf_op jit(solution)/shard_map/ppermute | solution.py:288
  78.9 18.6 %collective-permute-start.10 = (bf16[2,2,32,1024]{3,2,1,0:T(8,128)(2,1)S(1)}, bf16[2,2,32,1024]{3,2,1,0:T(8,128)(2,1)S(1)}, u32[]{:S(2)}, u32[]{:S(2)}) collective-permute-start(bf16[2,2,32,1024]{3,2,1,0:T(8,128)(2,1)S(1)} %get-tuple-element.38), channel_id=1, source_target_pairs={{0,6},{1,7},{2,4},{3,5},{4,2},{5,3},{6,0},{7,1},{8,14},{9,15},{10,... | collective-permute-start | bytes 786440 | tf_op jit(solution)/shard_map/ppermute | solution.py:288
  82.1 45.8 %copy-start.8 = (bf16[8,512,512]{2,1,0:T(8,128)(2,1)S(1)}, bf16[8,512,512]{2,1,0:T(8,128)(2,1)}, u32[]{:S(2)}) copy-start(bf16[8,512,512]{2,1,0:T(8,128)(2,1)} %constant.20.clone.refs_17_) | copy-start | bytes 12582916
  99.6 28.3 %collective-permute-start.15 = (bf16[4,2,32,1024]{3,2,1,0:T(8,128)(2,1)S(1)}, bf16[4,2,32,1024]{3,2,1,0:T(8,128)(2,1)S(1)}, u32[]{:S(2)}, u32[]{:S(2)}) collective-permute-start(bf16[4,2,32,1024]{3,2,1,0:T(8,128)(2,1)S(1)} %collect_blocks.11), channel_id=1, source_target_pairs={{0,1},{1,0},{2,3},{3,2},{4,5},{5,4},{6,7},{7,6},{8,9},{9,8},{10,11... | collective-permute-start | bytes 1572872 | tf_op jit(solution)/shard_map/ppermute | solution.py:288
  100.1 8.3 %collective-permute-start.16 = (bf16[2,32,1024]{2,1,0:T(8,128)(2,1)S(1)}, bf16[2,32,1024]{2,1,0:T(8,128)(2,1)S(1)}, u32[]{:S(2)}, u32[]{:S(2)}) collective-permute-start(bf16[2,32,1024]{2,1,0:T(8,128)(2,1)S(1)} %get-tuple-element.46), channel_id=1, source_target_pairs={{0,2},{1,3},{2,0},{3,1},{4,6},{5,7},{6,4},{7,5},{8,10},{9,11},{10,... | collective-permute-start | bytes 393224 | tf_op jit(solution)/shard_map/ppermute | solution.py:288
  103.5 13.5 %collective-permute-start.17 = (bf16[2,32,1024]{2,1,0:T(8,128)(2,1)S(1)}, bf16[2,32,1024]{2,1,0:T(8,128)(2,1)S(1)}, u32[]{:S(2)}, u32[]{:S(2)}) collective-permute-start(bf16[2,32,1024]{2,1,0:T(8,128)(2,1)S(1)} %get-tuple-element.47), channel_id=1, source_target_pairs={{0,4},{1,5},{2,6},{3,7},{4,0},{5,1},{6,2},{7,3},{8,12},{9,13},{10,... | collective-permute-start | bytes 393224 | tf_op jit(solution)/shard_map/ppermute | solution.py:288
  105.4 11.6 %collective-permute-start.18 = (bf16[2,32,1024]{2,1,0:T(8,128)(2,1)S(1)}, bf16[2,32,1024]{2,1,0:T(8,128)(2,1)S(1)}, u32[]{:S(2)}, u32[]{:S(2)}) collective-permute-start(bf16[2,32,1024]{2,1,0:T(8,128)(2,1)S(1)} %get-tuple-element.48), channel_id=1, source_target_pairs={{0,6},{1,7},{2,4},{3,5},{4,2},{5,3},{6,0},{7,1},{8,14},{9,15},{10,... | collective-permute-start | bytes 393224 | tf_op jit(solution)/shard_map/ppermute | solution.py:288
  106.9 14.0 %collective-permute-start.19 = (bf16[2,32,1024]{2,1,0:T(8,128)(2,1)S(1)}, bf16[2,32,1024]{2,1,0:T(8,128)(2,1)S(1)}, u32[]{:S(2)}, u32[]{:S(2)}) collective-permute-start(bf16[2,32,1024]{2,1,0:T(8,128)(2,1)S(1)} %get-tuple-element.49), channel_id=1, source_target_pairs={{0,1},{1,0},{2,3},{3,2},{4,5},{5,4},{6,7},{7,6},{8,9},{9,8},{10,11... | collective-permute-start | bytes 393224 | tf_op jit(solution)/shard_map/ppermute | solution.py:288
  108.5 12.5 %collective-permute-start.20 = (bf16[2,32,1024]{2,1,0:T(8,128)(2,1)S(1)}, bf16[2,32,1024]{2,1,0:T(8,128)(2,1)S(1)}, u32[]{:S(2)}, u32[]{:S(2)}) collective-permute-start(bf16[2,32,1024]{2,1,0:T(8,128)(2,1)S(1)} %get-tuple-element.50), channel_id=1, source_target_pairs={{0,3},{1,2},{2,1},{3,0},{4,7},{5,6},{6,5},{7,4},{8,11},{9,10},{10,... | collective-permute-start | bytes 393224 | tf_op jit(solution)/shard_map/ppermute | solution.py:288
  117.0 10.9 %collective-permute-start.21 = (bf16[2,32,1024]{2,1,0:T(8,128)(2,1)S(1)}, bf16[2,32,1024]{2,1,0:T(8,128)(2,1)S(1)}, u32[]{:S(2)}, u32[]{:S(2)}) collective-permute-start(bf16[2,32,1024]{2,1,0:T(8,128)(2,1)S(1)} %get-tuple-element.51), channel_id=1, source_target_pairs={{0,5},{1,4},{2,7},{3,6},{4,1},{5,0},{6,3},{7,2},{8,13},{9,12},{10,... | collective-permute-start | bytes 393224 | tf_op jit(solution)/shard_map/ppermute | solution.py:288
  117.0 10.9 %collective-permute-start.22 = (bf16[2,32,1024]{2,1,0:T(8,128)(2,1)S(1)}, bf16[2,32,1024]{2,1,0:T(8,128)(2,1)S(1)}, u32[]{:S(2)}, u32[]{:S(2)}) collective-permute-start(bf16[2,32,1024]{2,1,0:T(8,128)(2,1)S(1)} %get-tuple-element.52), channel_id=1, source_target_pairs={{0,7},{1,6},{2,5},{3,4},{4,3},{5,2},{6,1},{7,0},{8,15},{9,14},{10,... | collective-permute-start | bytes 393224 | tf_op jit(solution)/shard_map/ppermute | solution.py:288

commit v2 on v1

--- a/solution.py
+++ b/solution.py
@@ -15,6 +15,7 @@
 BF16 = jnp.bfloat16
 F32 = jnp.float32
 VMEM_BYTES = 24 * 1024 * 1024
+FREE = pl.CostEstimate(flops=1, bytes_accessed=1, transcendentals=0)
 
 
 def round_bf16(values):
@@ -92,14 +93,16 @@
         compiler_params=pltpu.CompilerParams(vmem_limit_bytes=VMEM_BYTES),
         name="pick_points",
     )(points, tiles)
-    return out.transpose(1, 0, 2).reshape(rows, groups * LANES)
-
-
-def coef_kernel(*refs):
-    groups, turn_ref, own_ref, src_ref = refs[:-3], refs[-3], refs[-2], refs[-1]
-    nu = groups[0].shape[3]
-    own = jnp.concatenate([g[k, 0] for g in groups for k in range(g.shape[0])], axis=0)
-    src = jnp.concatenate([g[k, 1] for g in groups for k in range(g.shape[0])], axis=0)
+    return out
+
+
+def coef_kernel(picks, inputs, me_ref, *refs):
+    arrays, turn_ref, own_ref, src_ref = refs[:inputs], refs[-3], refs[-2], refs[-1]
+    values = [arrays[array][lead(me_ref[0])] for array, lead in picks]
+    groups = values[0].shape[0] // 2
+    nu = groups * LANES
+    own = jnp.concatenate([jnp.concatenate([v[g] for g in range(groups)], axis=1) for v in values], axis=0)
+    src = jnp.concatenate([jnp.concatenate([v[groups + g] for g in range(groups)], axis=1) for v in values], axis=0)
     turn = turn_ref[...]
     own_ref[:nu] = own.astype(F32).T.astype(BF16)
     own_ref[nu:] = dot(turn, own).T.astype(BF16)
@@ -107,19 +110,18 @@
     src_ref[:, nu:] = (-dot(turn, src)).astype(BF16)
 
 
-def coefficients(groups, turn):
-    _, _, rows, nu = groups[0].shape
-    high = sum(g.shape[0] for g in groups) * rows
+def coefficients(me, values, turn):
+    arrays, picks = distinct(values)
+    tiles, rows, _ = arrays[0].shape[1:]
+    high, nu = len(values) * rows, tiles // 2 * LANES
     return pl.pallas_call(
-        coef_kernel,
-        out_shape=(
-            jax.ShapeDtypeStruct((2 * nu, high), BF16),
-            jax.ShapeDtypeStruct((high, 2 * nu), BF16),
-        ),
-        compiler_params=pltpu.CompilerParams(vmem_limit_bytes=VMEM_BYTES),
-        cost_estimate=pl.CostEstimate(flops=1, bytes_accessed=1, transcendentals=0),
+        lambda *refs: coef_kernel(picks, len(arrays), *refs),
+        in_specs=[pl.BlockSpec(memory_space=pltpu.SMEM)] + [pl.BlockSpec(memory_space=pltpu.VMEM)] * (len(arrays) + 1),
+        out_shape=(jax.ShapeDtypeStruct((2 * nu, high), BF16), jax.ShapeDtypeStruct((high, 2 * nu), BF16)),
+        compiler_params=pltpu.CompilerParams(vmem_limit_bytes=VMEM_BYTES),
+        cost_estimate=FREE,
         name="coefficients",
-    )(*groups, turn)
+    )(me, *arrays, turn)
 
 
 def exchange_kernel(first_plane, planes, cells, pairs, inputs, me_ref, *refs):
@@ -182,10 +184,26 @@
         + [jax.ShapeDtypeStruct((1,), jnp.int32)],
         scratch_shapes=[pltpu.VMEM((planes * high, area), BF16)] * 2,
         compiler_params=pltpu.CompilerParams(vmem_limit_bytes=VMEM_BYTES),
-        cost_estimate=pl.CostEstimate(flops=1, bytes_accessed=1, transcendentals=0),
+        cost_estimate=FREE,
         name="exchange_planes",
     )(me, *arrays, own, src, coulomb, table, turn)
     return sent, after
+
+
+def gate_kernel(me_ref, *refs):
+    refs[-1][0] = me_ref[0]
+
+
+def gate(me, arrays):
+    smem = pl.BlockSpec(memory_space=pltpu.SMEM)
+    return pl.pallas_call(
+        gate_kernel,
+        in_specs=[smem] + [pl.BlockSpec(memory_space=pl.ANY)] * len(arrays),
+        out_specs=smem,
+        out_shape=jax.ShapeDtypeStruct((1,), jnp.int32),
+        cost_estimate=FREE,
+        name="gate",
+    )(me, *arrays)
 
 
 def collect_kernel(plan, inputs, me_ref, *refs):
@@ -226,7 +244,7 @@
     hbm = pl.BlockSpec(memory_space=pltpu.HBM)
     return pl.pallas_call(
         lambda *refs: collect_kernel(plan, len(arrays), *refs),
-        in_specs=[pl.BlockSpec(memory_space=pltpu.SMEM)] + [hbm] * len(arrays),
+        in_specs=[pl.BlockSpec(memory_space=pltpu.SMEM)] + [pl.BlockSpec(memory_space=pl.ANY)] * len(arrays),
         out_specs=[hbm] * len(wanted),
         out_shape=[
             jax.ShapeDtypeStruct((len(picks),) + picks[0][0].shape[1:], picks[0][0].dtype) for picks in wanted
@@ -237,7 +255,7 @@
             pltpu.SemaphoreType.DMA((len(places),)),
         ],
         compiler_params=pltpu.CompilerParams(vmem_limit_bytes=VMEM_BYTES),
-        cost_estimate=pl.CostEstimate(flops=1, bytes_accessed=1, transcendentals=0),
+        cost_estimate=FREE,
         name="collect_blocks",
     )(me, *arrays)
 
@@ -279,7 +297,7 @@
         grid_spec=spec,
         out_shape=jax.ShapeDtypeStruct((height, tiles, 2, LANES), BF16),
         compiler_params=pltpu.CompilerParams(vmem_limit_bytes=VMEM_BYTES),
-        cost_estimate=pl.CostEstimate(flops=1, bytes_accessed=1, transcendentals=0),
+        cost_estimate=FREE,
         name="line_pass",
     )(me, *[array for array, _ in fields], table)
 
@@ -319,48 +337,48 @@
             for k in order
         ]
 
-    def cross(c, me):
+    def cross(c, distances, me):
         wanted = [
             [(blocks, lambda me, d=d, y=y: ((me ^ d) // 2 * 2 + y) * chunks + c) for y in range(2)]
-            for d in range(0, count, 2)
+            for d in distances
         ]
-        pairs = dict(zip(range(0, count, 2), collect(me, wanted)))
-        return {d: hop(pair, d, count) if d else pair for d, pair in pairs.items()}
+        return {d: hop(pair, d, count) if d else pair for d, pair in zip(distances, collect(me, wanted))}
+
+    def direct(c, distances, me):
+        wanted = [[(blocks, lambda me, d=d: (me ^ d) * chunks + c)] for d in distances]
+        return {d: hop(block, d, count) for d, block in zip(distances, collect(me, wanted))}
 
     own_values = pick(tiles, points)
     everyone = lax.all_gather(own_values, "kgrp", axis=0, tiled=False)
     chosen = partner == lax.axis_index("kgrp")
-    src_values = jnp.sum(jnp.where(chosen[:, None, None], everyone, jnp.zeros_like(everyone)), axis=0)
-    both = jnp.stack([own_values, src_values])[None]
-    over_z = [both] + [hop(both, d, count) for d in range(2, count, 2)]
-    crossing = [cross(c, device) for c in range(chunks)]
+    matched = jnp.sum(jnp.where(chosen[:, None, None, None], everyone, jnp.zeros_like(everyone)), axis=0)
+    values = jnp.concatenate([own_values, matched], axis=0)[None]
+    over_z = [values] + [hop(values, d, count) for d in range(2, count, 2)]
     (here,) = collect(device, [[(part, first) for part in over_z]])
-    own_coef, src_coef = coefficients([here, hop(here, 1, count)], turn)
+    there = hop(here, 1, count)
+    picks = [(there if k % 2 else here, lambda me, i=k // 2: i) for k in order]
+    own_coef, src_coef = coefficients(device, picks, turn)
+
+    received = []
+    for c in range(chunks):
+        distances = list(range(count // 2, count)) + list(range(1, count // 2))
+        arrived = direct(c, distances, gate(device, [values]) if c == 0 else gate(device, [values]))
+        received.append([(arrived[k], first) if k else (blocks, lambda me, c=c: me * chunks + c) for k in order])
 
     plane_t = jnp.asarray(plane_table(scale))
     groups = 2 if bands % 16 == 0 else 1
     line_t = jnp.asarray(line_table(scale, order, planes, bands // groups))
 
-    received = swap_pairs(crossing[0], device)
     fields = []
-    waiting = None
     for c in range(chunks):
-        last = c == chunks - 1
-        pairs = [(at, None) if last else (k // 2, k % 2) for at, k in enumerate(order)]
-        sent, after = exchange(
-            device, received, own_coef, src_coef, coulomb, plane_t, turn, c * chunk_planes, chunk_planes, pairs
+        sent, _ = exchange(
+            device, received[c], own_coef, src_coef, coulomb, plane_t, turn, c * chunk_planes, chunk_planes,
+            [(at, None) for at in range(count)],
         )
-        if waiting is not None:
-            fields += swap_pairs(waiting, after)
-        if last:
-            back = {}
-            for k in sorted(order, reverse=True):
-                at = order.index(k)
-                back[k] = hop(sent[at], k, count) if k else sent[at]
-            fields += [(back[k][None], first) for k in order]
-        else:
-            waiting = {d: hop(sent[d // 2], d, count) if d else sent[0] for d in range(0, count, 2)}
-            received = swap_pairs(crossing[c + 1], after)
+        back = {0: sent[0]}
+        for k in list(range(count // 2, count)) + list(range(1, count // 2)):
+            back[k] = hop(sent[order.index(k)], k, count)
+        fields += [(back[k][None], first) for k in order]
 
     factor = 1.0 / (scale * scale * math.sqrt(GX * GY * GZ))
     out = line_pass(device, fields, line_t, factor, rows, groups, count)

time: 132 us -> 124 us (0.939)
  waiting for transfers between devices: 41.4 us -> 16.8 us
  starting transfers between devices: 41.6 us -> 61.5 us
  Pallas kernels: 32.2 us -> 27.8 us
    ppermute x23 -> x32, waiting for transfers between devices: 41.4 us -> 16.8 us  [hop(): lax.ppermute(array, 'band', [(i, i ^ distance) for i in range(count)])]
    ppermute x23 -> x32, starting transfers between devices: 41.6 us -> 61.5 us  [hop(): lax.ppermute(array, 'band', [(i, i ^ distance) for i in range(count)])]
    pallas_call x6 -> x3, Pallas kernels: 11.8 us -> 7.13 us  [collect(): pl.pallas_call(lambda *refs: collect_kernel(plan, len(arrays), *refs), in...]
    unnamed x24 -> x26, local copies, waits for them, and re-layouts: 8.9 us -> 9.73 us
  transfers between devices with their start and end apart: 23 -> 32, of which waited for: 8 -> 5; matrix products, arithmetic and copies ran while one was open for 0% -> 0% of each run, Pallas kernels for 16% -> 17%
where the time goes in v2:
time: 124 us
  starting transfers between devices  61.5 us (50%)
  Pallas kernels  27.8 us (22%)
  waiting for transfers between devices  16.8 us (14%)
  local copies, waits for them, and re-layouts  11.2 us (9%)
  blocking collectives  6.47 us (5%)
    ppermute x32, starting transfers between devices, hop(): lax.ppermute(array, 'band', [(i, i ^ distance) for i in range(count)])  61.5 us
    ppermute x32, waiting for transfers between devices, hop(): lax.ppermute(array, 'band', [(i, i ^ distance) for i in range(count)])  16.8 us
    pallas_call x2, Pallas kernels, exchange(): pl.pallas_call(lambda *refs: exchange_kernel(first_plane, planes, places,...  13.4 us
    unnamed x26, local copies, waits for them, and re-layouts  9.73 us
    pallas_call x3, Pallas kernels, collect(): pl.pallas_call(lambda *refs: collect_kernel(plan, len(arrays), *refs), in...  7.13 us
    all_gather x1, blocking collectives, body(): everyone = lax.all_gather(own_values, 'kgrp', axis=0, tiled=False)  6.47 us
    pallas_call x1, Pallas kernels, line_pass(): pl.pallas_call(lambda *refs: line_kernel(factor, group_rows, count, *refs...  3.49 us
    pallas_call x1, Pallas kernels, pick(): pl.pallas_call(pick_kernel, in_specs=[pl.BlockSpec(memory_space=pltpu.SME...  2.94 us
  transfers between devices with their start and end apart: 32, of which 5 were waited for; matrix products, arithmetic and copies ran while one was open for 0% of the time, Pallas kernels for 17%

profile of v2, /device:TPU:0, one launch (start us, length us, event | category | flops | bytes accessed | tf_op | source)
XLA Modules:
  0.0 124.1 jit_solution(4471904162590423905)
XLA Ops:
  0.0 1.6 %copy-done = bf16[1,16,2,32768]{3,2,1,0:T(2,128)(2,1)S(1)} copy-done((bf16[1,16,2,32768]{3,2,1,0:T(2,128)(2,1)S(1)}, bf16[1,16,2,32768]{3,2,1,0:T(2,128)(2,1)}, u32[]{:S(2)}) %copy-start) | copy-done | bytes 2097176
  1.6 1.4 %copy_bitcast_fusion = bf16[1,16,2,256,128]{4,2,1,3,0:T(2,128)(2,1)S(1)} fusion(bf16[1,16,2,32768]{3,2,1,0:T(2,128)(2,1)S(1)} %copy-done), kind=kLoop, calls=%fused_computation | loop fusion | bytes 4194304 | tf_op jit(solution)/shard_map/reshape | solution.py:322
  3.1 2.9 %pick_points.1 = bf16[4,32,128]{2,1,0:T(8,128)(2,1)S(1)} custom-call(s32[512]{0:T(512)S(1)} %copy-done.11, bf16[256,32,128]{2,1,0:T(8,128)(2,1)S(1)} %bitcast.34), custom_call_target="tpu_custom_call" | custom-call | tf_op jit(solution)/shard_map/pick_points/pallas_call | solution.py:88
  6.0 1.3 %copy-done.1 = bf16[1,16,2,256,128]{4,2,1,3,0:T(2,128)(2,1)} copy-done((bf16[1,16,2,256,128]{4,2,1,3,0:T(2,128)(2,1)}, bf16[1,16,2,256,128]{4,2,1,3,0:T(2,128)(2,1)S(1)}, u32[]{:S(2)}) %copy-start.1) | copy-done | bytes 2097176
  7.3 6.5 %all-gather = bf16[16,32,128]{2,1,0:T(8,128)(2,1)S(1)} all-gather(bf16[4,32,128]{2,1,0:T(8,128)(2,1)S(1)} %pick_points.1), channel_id=2, replica_groups=mesh['kgrp'=4,'band'=8] {'kgrp'}, dimensions={0}, use_global_device_ids=true | all-gather | bytes 163840 | tf_op jit(solution)/shard_map/all_gather | solution.py:352
  13.8 0.1 select_reduce_fusion
  13.9 4.1 %collective-permute-start.9 = (bf16[1,8,32,128]{3,2,1,0:T(8,128)(2,1)S(1)}, bf16[1,8,32,128]{3,2,1,0:T(8,128)(2,1)S(1)}, u32[]{:S(2)}, u32[]{:S(2)}) collective-permute-start(bf16[1,8,32,128]{3,2,1,0:T(8,128)(2,1)S(1)} %maximum_bitcast_fusion.refs_0_.refs_1_), channel_id=1, source_target_pairs={{0,6},{1,7},{2,4},{3,5},{4,2},{5,3},{6,0},{7,1},{8,14},{9,15},{10,... | collective-permute-start | bytes 196616 | tf_op jit(solution)/shard_map/ppermute | solution.py:306
  18.0 0.6 collective-permute-start.7
  18.6 0.5 gate.1.refs_0_
  19.2 1.6 %copy-done.2 = bf16[1,16,2,256,128]{4,2,1,3,0:T(2,128)(2,1)S(1)} copy-done((bf16[1,16,2,256,128]{4,2,1,3,0:T(2,128)(2,1)S(1)}, bf16[1,16,2,256,128]{4,2,1,3,0:T(2,128)(2,1)}, u32[]{:S(2)}) %copy-start.2) | copy-done | bytes 2097176
  20.8 3.3 %collect_blocks.5 = (bf16[1,16,32,128]{3,2,1,0:T(8,128)(2,1)S(1)}, bf16[1,16,32,128]{3,2,1,0:T(8,128)(2,1)S(1)}, bf16[1,16,32,128]{3,2,1,0:T(8,128)(2,1)S(1)}, b...) custom-call(s32[1]{0:T(128)} %gate.1.refs_0_, ...), custom_call_target="tpu_custom_call" | custom-call | flops 1 | bytes 1 | tf_op jit(solution)/shard_map/collect_blocks/pallas_call | solution.py:245
  24.0 1.5 %collective-permute-start.18 = (bf16[1,16,32,128]{3,2,1,0:T(8,128)(2,1)S(1)}, bf16[1,16,32,128]{3,2,1,0:T(8,128)(2,1)S(1)}, u32[]{:S(2)}, u32[]{:S(2)}) collective-permute-start(bf16[1,16,32,128]{3,2,1,0:T(8,128)(2,1)S(1)} %get-tuple-element.54), channel_id=1, source_target_pairs={{0,2},{1,3},{2,0},{3,1},{4,6},{5,7},{6,4},{7,5},{8,10},{9,11},{10,... | collective-permute-start | bytes 393224 | tf_op jit(solution)/shard_map/ppermute | solution.py:306
  25.5 2.9 %collective-permute-start.19 = (bf16[1,16,32,128]{3,2,1,0:T(8,128)(2,1)S(1)}, bf16[1,16,32,128]{3,2,1,0:T(8,128)(2,1)S(1)}, u32[]{:S(2)}, u32[]{:S(2)}) collective-permute-start(bf16[1,16,32,128]{3,2,1,0:T(8,128)(2,1)S(1)} %get-tuple-element.55), channel_id=1, source_target_pairs={{0,4},{1,5},{2,6},{3,7},{4,0},{5,1},{6,2},{7,3},{8,12},{9,13},{10,... | collective-permute-start | bytes 393224 | tf_op jit(solution)/shard_map/ppermute | solution.py:306
  28.5 1.7 %collective-permute-start.21 = (bf16[1,16,32,128]{3,2,1,0:T(8,128)(2,1)S(1)}, bf16[1,16,32,128]{3,2,1,0:T(8,128)(2,1)S(1)}, u32[]{:S(2)}, u32[]{:S(2)}) collective-permute-start(bf16[1,16,32,128]{3,2,1,0:T(8,128)(2,1)S(1)} %get-tuple-element.57), channel_id=1, source_target_pairs={{0,1},{1,0},{2,3},{3,2},{4,5},{5,4},{6,7},{7,6},{8,9},{9,8},{10,11... | collective-permute-start | bytes 393224 | tf_op jit(solution)/shard_map/ppermute | solution.py:306
  30.2 0.8 copy-done.10
  31.0 0.7 collect_blocks.4.refs_1_
  31.7 0.4 collective-permute-start.10
  32.2 1.4 %collective-permute-start.22 = (bf16[1,16,32,128]{3,2,1,0:T(8,128)(2,1)S(1)}, bf16[1,16,32,128]{3,2,1,0:T(8,128)(2,1)S(1)}, u32[]{:S(2)}, u32[]{:S(2)}) collective-permute-start(bf16[1,16,32,128]{3,2,1,0:T(8,128)(2,1)S(1)} %get-tuple-element.58), channel_id=1, source_target_pairs={{0,3},{1,2},{2,1},{3,0},{4,7},{5,6},{6,5},{7,4},{8,11},{9,10},{10,... | collective-permute-start | bytes 393224 | tf_op jit(solution)/shard_map/ppermute | solution.py:306
  33.6 3.1 %collect_blocks.3 = (bf16[1,16,32,128]{3,2,1,0:T(8,128)(2,1)S(1)}, bf16[1,16,32,128]{3,2,1,0:T(8,128)(2,1)S(1)}, bf16[1,16,32,128]{3,2,1,0:T(8,128)(2,1)S(1)}, b...) custom-call(s32[1]{0:T(128)} %gate.1.refs_0_, ...), custom_call_target="tpu_custom_call" | custom-call | flops 1 | bytes 1 | tf_op jit(solution)/shard_map/collect_blocks/pallas_call | solution.py:245
  36.8 1.6 %collective-permute-done.19.refs_3_ = bf16[1,16,32,128]{3,2,1,0:T(8,128)(2,1)S(1)} collective-permute-done((bf16[1,16,32,128]{3,2,1,0:T(8,128)(2,1)S(1)}, bf16[1,16,32,128]{3,2,1,0:T(8,128)(2,1)S(1)}, u32[]{:S(2)}, u32[]{:S(2)}) %collective-permute-start.19) | collective-permute-done | bytes 131104 | tf_op jit(solution)/shard_map/ppermute | solution.py:306
  38.4 2.2 %collective-permute-start.23 = (bf16[1,16,32,128]{3,2,1,0:T(8,128)(2,1)S(1)}, bf16[1,16,32,128]{3,2,1,0:T(8,128)(2,1)S(1)}, u32[]{:S(2)}, u32[]{:S(2)}) collective-permute-start(bf16[1,16,32,128]{3,2,1,0:T(8,128)(2,1)S(1)} %get-tuple-element.59), channel_id=1, source_target_pairs={{0,5},{1,4},{2,7},{3,6},{4,1},{5,0},{6,3},{7,2},{8,13},{9,12},{10,... | collective-permute-start | bytes 393224 | tf_op jit(solution)/shard_map/ppermute | solution.py:306
  40.6 1.2 collective-permute-start.24
  41.8 5.6 %collective-permute-start = (bf16[1,16,32,128]{3,2,1,0:T(8,128)(2,1)S(1)}, bf16[1,16,32,128]{3,2,1,0:T(8,128)(2,1)S(1)}, u32[]{:S(2)}, u32[]{:S(2)}) collective-permute-start(bf16[1,16,32,128]{3,2,1,0:T(8,128)(2,1)S(1)} %get-tuple-element.37), channel_id=1, source_target_pairs={{0,2},{1,3},{2,0},{3,1},{4,6},{5,7},{6,4},{7,5},{8,10},{9,11},{10,... | collective-permute-start | bytes 393224 | tf_op jit(solution)/shard_map/ppermute | solution.py:306
  47.3 1.0 collective-permute-start.1
  48.4 6.3 %collective-permute-done.23.refs_7_ = bf16[1,16,32,128]{3,2,1,0:T(8,128)(2,1)S(1)} collective-permute-done((bf16[1,16,32,128]{3,2,1,0:T(8,128)(2,1)S(1)}, bf16[1,16,32,128]{3,2,1,0:T(8,128)(2,1)S(1)}, u32[]{:S(2)}, u32[]{:S(2)}) %collective-permute-start.23) | collective-permute-done | bytes 131104 | tf_op jit(solution)/shard_map/ppermute | solution.py:306
  54.7 2.5 %collective-permute-start.2 = (bf16[1,16,32,128]{3,2,1,0:T(8,128)(2,1)S(1)}, bf16[1,16,32,128]{3,2,1,0:T(8,128)(2,1)S(1)}, u32[]{:S(2)}, u32[]{:S(2)}) collective-permute-start(bf16[1,16,32,128]{3,2,1,0:T(8,128)(2,1)S(1)} %get-tuple-element.39), channel_id=1, source_target_pairs={{0,6},{1,7},{2,4},{3,5},{4,2},{5,3},{6,0},{7,1},{8,14},{9,15},{10,... | collective-permute-start | bytes 393224 | tf_op jit(solution)/shard_map/ppermute | solution.py:306
  57.2 2.4 %collective-permute-start.4 = (bf16[1,16,32,128]{3,2,1,0:T(8,128)(2,1)S(1)}, bf16[1,16,32,128]{3,2,1,0:T(8,128)(2,1)S(1)}, u32[]{:S(2)}, u32[]{:S(2)}) collective-permute-start(bf16[1,16,32,128]{3,2,1,0:T(8,128)(2,1)S(1)} %get-tuple-element.41), channel_id=1, source_target_pairs={{0,3},{1,2},{2,1},{3,0},{4,7},{5,6},{6,5},{7,4},{8,11},{9,10},{10,... | collective-permute-start | bytes 393224 | tf_op jit(solution)/shard_map/ppermute | solution.py:306
  59.5 1.1 collective-permute-start.5
  60.6 0.3 coefficients.1
  60.9 5.9 %collective-permute-start.6 = (bf16[1,16,32,128]{3,2,1,0:T(8,128)(2,1)S(1)}, bf16[1,16,32,128]{3,2,1,0:T(8,128)(2,1)S(1)}, u32[]{:S(2)}, u32[]{:S(2)}) collective-permute-start(bf16[1,16,32,128]{3,2,1,0:T(8,128)(2,1)S(1)} %get-tuple-element.43), channel_id=1, source_target_pairs={{0,7},{1,6},{2,5},{3,4},{4,3},{5,2},{6,1},{7,0},{8,15},{9,14},{10,... | collective-permute-start | bytes 393224 | tf_op jit(solution)/shard_map/ppermute | solution.py:306
  66.8 2.2 %copy-done.4 = bf16[512,4096]{1,0:T(8,128)(2,1)S(1)} copy-done((bf16[512,4096]{1,0:T(8,128)(2,1)S(1)}, bf16[512,4096]{1,0:T(8,128)(2,1)}, u32[]{:S(2)}) %copy-start.4) | copy-done | bytes 4194328
  69.0 2.2 %copy-done.6 = bf16[2,1024,1024]{2,1,0:T(8,128)(2,1)S(1)} copy-done((bf16[2,1024,1024]{2,1,0:T(8,128)(2,1)S(1)}, bf16[2,1024,1024]{2,1,0:T(8,128)(2,1)}, u32[]{:S(2)}) %copy-start.6) | copy-done | bytes 4194328
  71.2 6.7 %exchange_planes.3 = (bf16[2,32,1024]{2,1,0:T(8,128)(2,1)S(1)}, bf16[2,32,1024]{2,1,0:T(8,128)(2,1)S(1)}, bf16[2,32,1024]{2,1,0:T(8,128)(2,1)S(1)}, bf16[2,32,10...) custom-call(s32[1]{0:T(128)} %bitcast.me_ref.refs_0_, ...), custom_call_target="tpu_custom_call" | custom-call | flops 1 | bytes 1 | tf_op jit(solution)/shard_map/exchange_planes/pallas_call | solution.py:179
  78.0 0.7 collective-permute-start.26
  78.7 3.7 %collective-permute-start.27 = (bf16[2,32,1024]{2,1,0:T(8,128)(2,1)S(1)}, bf16[2,32,1024]{2,1,0:T(8,128)(2,1)S(1)}, u32[]{:S(2)}, u32[]{:S(2)}) collective-permute-start(bf16[2,32,1024]{2,1,0:T(8,128)(2,1)S(1)} %get-tuple-element.64), channel_id=1, source_target_pairs={{0,6},{1,7},{2,4},{3,5},{4,2},{5,3},{6,0},{7,1},{8,14},{9,15},{10,... | collective-permute-start | bytes 393224 | tf_op jit(solution)/shard_map/ppermute | solution.py:306
  82.4 0.6 collective-permute-start.29
  83.0 6.7 %exchange_planes.2 = (bf16[2,32,1024]{2,1,0:T(8,128)(2,1)S(1)}, bf16[2,32,1024]{2,1,0:T(8,128)(2,1)S(1)}, bf16[2,32,1024]{2,1,0:T(8,128)(2,1)S(1)}, bf16[2,32,10...) custom-call(s32[1]{0:T(128)} %bitcast.me_ref.refs_0_, ...), custom_call_target="tpu_custom_call" | custom-call | flops 1 | bytes 1 | tf_op jit(solution)/shard_map/exchange_planes/pallas_call | solution.py:179
  89.8 1.4 %collective-permute-start.30 = (bf16[2,32,1024]{2,1,0:T(8,128)(2,1)S(1)}, bf16[2,32,1024]{2,1,0:T(8,128)(2,1)S(1)}, u32[]{:S(2)}, u32[]{:S(2)}) collective-permute-start(bf16[2,32,1024]{2,1,0:T(8,128)(2,1)S(1)} %get-tuple-element.67), channel_id=1, source_target_pairs={{0,5},{1,4},{2,7},{3,6},{4,1},{5,0},{6,3},{7,2},{8,13},{9,12},{10,... | collective-permute-start | bytes 393224 | tf_op jit(solution)/shard_map/ppermute | solution.py:306
  91.2 4.7 %collective-permute-start.31 = (bf16[2,32,1024]{2,1,0:T(8,128)(2,1)S(1)}, bf16[2,32,1024]{2,1,0:T(8,128)(2,1)S(1)}, u32[]{:S(2)}, u32[]{:S(2)}) collective-permute-start(bf16[2,32,1024]{2,1,0:T(8,128)(2,1)S(1)} %get-tuple-element.68), channel_id=1, source_target_pairs={{0,7},{1,6},{2,5},{3,4},{4,3},{5,2},{6,1},{7,0},{8,15},{9,14},{10,... | collective-permute-start | bytes 393224 | tf_op jit(solution)/shard_map/ppermute | solution.py:306
  96.0 0.7 collective-permute-start.12
  96.7 3.7 %collective-permute-start.13 = (bf16[2,32,1024]{2,1,0:T(8,128)(2,1)S(1)}, bf16[2,32,1024]{2,1,0:T(8,128)(2,1)S(1)}, u32[]{:S(2)}, u32[]{:S(2)}) collective-permute-start(bf16[2,32,1024]{2,1,0:T(8,128)(2,1)S(1)} %get-tuple-element.49), channel_id=1, source_target_pairs={{0,6},{1,7},{2,4},{3,5},{4,2},{5,3},{6,0},{7,1},{8,14},{9,15},{10,... | collective-permute-start | bytes 393224 | tf_op jit(solution)/shard_map/ppermute | solution.py:306
  100.3 1.5 %collective-permute-done.30 = bf16[2,32,1024]{2,1,0:T(8,128)(2,1)S(1)} collective-permute-done((bf16[2,32,1024]{2,1,0:T(8,128)(2,1)S(1)}, bf16[2,32,1024]{2,1,0:T(8,128)(2,1)S(1)}, u32[]{:S(2)}, u32[]{:S(2)}) %collective-permute-start.30) | collective-permute-done | bytes 131104 | tf_op jit(solution)/shard_map/ppermute | solution.py:306
  101.8 0.7 collective-permute-start.14
  102.5 8.4 %collective-permute-start.15 = (bf16[2,32,1024]{2,1,0:T(8,128)(2,1)S(1)}, bf16[2,32,1024]{2,1,0:T(8,128)(2,1)S(1)}, u32[]{:S(2)}, u32[]{:S(2)}) collective-permute-start(bf16[2,32,1024]{2,1,0:T(8,128)(2,1)S(1)} %get-tuple-element.51), channel_id=1, source_target_pairs={{0,3},{1,2},{2,1},{3,0},{4,7},{5,6},{6,5},{7,4},{8,11},{9,10},{10,... | collective-permute-start | bytes 393224 | tf_op jit(solution)/shard_map/ppermute | solution.py:306
  111.0 1.4 %collective-permute-done.12 = bf16[2,32,1024]{2,1,0:T(8,128)(2,1)S(1)} collective-permute-done((bf16[2,32,1024]{2,1,0:T(8,128)(2,1)S(1)}, bf16[2,32,1024]{2,1,0:T(8,128)(2,1)S(1)}, u32[]{:S(2)}, u32[]{:S(2)}) %collective-permute-start.12) | collective-permute-done | bytes 131104 | tf_op jit(solution)/shard_map/ppermute | solution.py:306
  112.4 2.3 %collective-permute-start.17 = (bf16[2,32,1024]{2,1,0:T(8,128)(2,1)S(1)}, bf16[2,32,1024]{2,1,0:T(8,128)(2,1)S(1)}, u32[]{:S(2)}, u32[]{:S(2)}) collective-permute-start(bf16[2,32,1024]{2,1,0:T(8,128)(2,1)S(1)} %get-tuple-element.53), channel_id=1, source_target_pairs={{0,7},{1,6},{2,5},{3,4},{4,3},{5,2},{6,1},{7,0},{8,15},{9,14},{10,... | collective-permute-start | bytes 393224 | tf_op jit(solution)/shard_map/ppermute | solution.py:306
  114.7 5.9 %collective-permute-done.16 = bf16[2,32,1024]{2,1,0:T(8,128)(2,1)S(1)} collective-permute-done((bf16[2,32,1024]{2,1,0:T(8,128)(2,1)S(1)}, bf16[2,32,1024]{2,1,0:T(8,128)(2,1)S(1)}, u32[]{:S(2)}, u32[]{:S(2)}) %collective-permute-start.16) | collective-permute-done | bytes 131104 | tf_op jit(solution)/shard_map/ppermute | solution.py:306
  120.6 3.5 %line_pass.1 = bf16[512,8,2,128]{3,2,1,0:T(2,128)(2,1)} custom-call(s32[1]{0:T(128)} %bitcast.me_ref.refs_0_, bf16[1,2,32,1024]{3,2,1,0:T(8,128)(2,1)S(1)} %bitcast.45, bf16[1,2,32,1024]{3,2,1,0:T(8,128)(2,1)S(1)} %bitcast.48, bf16[1,2,32,1024]{3,2,1,0:T(8,128)(2,1)S(1)} %bitcast.49, bf16[1,2,32,1024]{3,2,1,0:T(8,128)(2,1)S(1)} %bitcast.50, ...), custom_call_target="tpu_custom_call" | custom-call | flops 1 | bytes 1 | tf_op jit(solution)/shard_map/line_pass/pallas_call | solution.py:295
  (56 shorter events, 0.3 us)
Async XLA Ops:
  0.0 1.6 %copy-start = (bf16[1,16,2,32768]{3,2,1,0:T(2,128)(2,1)S(1)}, bf16[1,16,2,32768]{3,2,1,0:T(2,128)(2,1)}, u32[]{:S(2)}) copy-start(bf16[1,16,2,32768]{3,2,1,0:T(2,128)(2,1)} %param.7) | copy-start | bytes 6291460
  1.6 1.5 %copy-start.11 = (s32[512]{0:T(512)S(1)}, s32[512]{0:T(512)}, u32[]{:S(2)}) copy-start(s32[512]{0:T(512)} %points_ref.1) | copy-start | bytes 6148
  3.0 10.8 %copy-start.12 = (s32[4]{0:T(128)S(1)}, s32[4]{0:T(128)}, u32[]{:S(2)}) copy-start(s32[4]{0:T(128)} %param.9) | copy-start | bytes 52
  6.0 1.3 %copy-start.1 = (bf16[1,16,2,256,128]{4,2,1,3,0:T(2,128)(2,1)}, bf16[1,16,2,256,128]{4,2,1,3,0:T(2,128)(2,1)S(1)}, u32[]{:S(2)}) copy-start(bf16[1,16,2,256,128]{4,2,1,3,0:T(2,128)(2,1)S(1)} %copy_bitcast_fusion) | copy-start | bytes 6291460
  13.9 4.7 %copy-start.9 = (bf16[1,8,32,128]{3,2,1,0:T(8,128)(2,1)}, bf16[1,8,32,128]{3,2,1,0:T(8,128)(2,1)S(1)}, u32[]{:S(2)}) copy-start(bf16[1,8,32,128]{3,2,1,0:T(8,128)(2,1)S(1)} %maximum_bitcast_fusion.refs_0_.refs_1_) | copy-start | bytes 196612
  13.9 14.5 %collective-permute-start.9 = (bf16[1,8,32,128]{3,2,1,0:T(8,128)(2,1)S(1)}, bf16[1,8,32,128]{3,2,1,0:T(8,128)(2,1)S(1)}, u32[]{:S(2)}, u32[]{:S(2)}) collective-permute-start(bf16[1,8,32,128]{3,2,1,0:T(8,128)(2,1)S(1)} %maximum_bitcast_fusion.refs_0_.refs_1_), channel_id=1, source_target_pairs={{0,6},{1,7},{2,4},{3,5},{4,2},{5,3},{6,0},{7,1},{8,14},{9,15},{10,... | collective-permute-start | bytes 196616 | tf_op jit(solution)/shard_map/ppermute | solution.py:306
  18.0 10.5 %collective-permute-start.8 = (bf16[1,8,32,128]{3,2,1,0:T(8,128)(2,1)S(1)}, bf16[1,8,32,128]{3,2,1,0:T(8,128)(2,1)S(1)}, u32[]{:S(2)}, u32[]{:S(2)}) collective-permute-start(bf16[1,8,32,128]{3,2,1,0:T(8,128)(2,1)S(1)} %maximum_bitcast_fusion.refs_0_.refs_1_), channel_id=1, source_target_pairs={{0,4},{1,5},{2,6},{3,7},{4,0},{5,1},{6,2},{7,3},{8,12},{9,13},{10,... | collective-permute-start | bytes 196616 | tf_op jit(solution)/shard_map/ppermute | solution.py:306
  18.0 12.2 %collective-permute-start.7 = (bf16[1,8,32,128]{3,2,1,0:T(8,128)(2,1)S(1)}, bf16[1,8,32,128]{3,2,1,0:T(8,128)(2,1)S(1)}, u32[]{:S(2)}, u32[]{:S(2)}) collective-permute-start(bf16[1,8,32,128]{3,2,1,0:T(8,128)(2,1)S(1)} %maximum_bitcast_fusion.refs_0_.refs_1_), channel_id=1, source_target_pairs={{0,2},{1,3},{2,0},{3,1},{4,6},{5,7},{6,4},{7,5},{8,10},{9,11},{10,... | collective-permute-start | bytes 196616 | tf_op jit(solution)/shard_map/ppermute | solution.py:306
  19.2 1.6 %copy-start.2 = (bf16[1,16,2,256,128]{4,2,1,3,0:T(2,128)(2,1)S(1)}, bf16[1,16,2,256,128]{4,2,1,3,0:T(2,128)(2,1)}, u32[]{:S(2)}) copy-start(bf16[1,16,2,256,128]{4,2,1,3,0:T(2,128)(2,1)} %copy-done.1) | copy-start | bytes 6291460
  20.8 12.9 %copy-start.3 = (bf16[1,16,2,256,128]{4,2,1,3,0:T(2,128)(2,1)S(1)}, bf16[1,16,2,256,128]{4,2,1,3,0:T(2,128)(2,1)}, u32[]{:S(2)}) copy-start(bf16[1,16,2,256,128]{4,2,1,3,0:T(2,128)(2,1)} %copy-done.1) | copy-start | bytes 6291460
  20.8 39.9 %copy-start.8 = (bf16[256,256]{1,0:T(8,128)(2,1)S(1)}, bf16[256,256]{1,0:T(8,128)(2,1)}, u32[]{:S(2)}) copy-start(bf16[256,256]{1,0:T(8,128)(2,1)} %constant.18.clone.refs_3_.refs_13_) | copy-start | bytes 393220
  24.0 8.1 %collective-permute-start.18 = (bf16[1,16,32,128]{3,2,1,0:T(8,128)(2,1)S(1)}, bf16[1,16,32,128]{3,2,1,0:T(8,128)(2,1)S(1)}, u32[]{:S(2)}, u32[]{:S(2)}) collective-permute-start(bf16[1,16,32,128]{3,2,1,0:T(8,128)(2,1)S(1)} %get-tuple-element.54), channel_id=1, source_target_pairs={{0,2},{1,3},{2,0},{3,1},{4,6},{5,7},{6,4},{7,5},{8,10},{9,11},{10,... | collective-permute-start | bytes 393224 | tf_op jit(solution)/shard_map/ppermute | solution.py:306
  25.5 12.9 %collective-permute-start.19 = (bf16[1,16,32,128]{3,2,1,0:T(8,128)(2,1)S(1)}, bf16[1,16,32,128]{3,2,1,0:T(8,128)(2,1)S(1)}, u32[]{:S(2)}, u32[]{:S(2)}) collective-permute-start(bf16[1,16,32,128]{3,2,1,0:T(8,128)(2,1)S(1)} %get-tuple-element.55), channel_id=1, source_target_pairs={{0,4},{1,5},{2,6},{3,7},{4,0},{5,1},{6,2},{7,3},{8,12},{9,13},{10,... | collective-permute-start | bytes 393224 | tf_op jit(solution)/shard_map/ppermute | solution.py:306
  28.4 12.2 %collective-permute-start.20 = (bf16[1,16,32,128]{3,2,1,0:T(8,128)(2,1)S(1)}, bf16[1,16,32,128]{3,2,1,0:T(8,128)(2,1)S(1)}, u32[]{:S(2)}, u32[]{:S(2)}) collective-permute-start(bf16[1,16,32,128]{3,2,1,0:T(8,128)(2,1)S(1)} %get-tuple-element.56), channel_id=1, source_target_pairs={{0,6},{1,7},{2,4},{3,5},{4,2},{5,3},{6,0},{7,1},{8,14},{9,15},{10,... | collective-permute-start | bytes 393224 | tf_op jit(solution)/shard_map/ppermute | solution.py:306
  28.5 13.3 %collective-permute-start.21 = (bf16[1,16,32,128]{3,2,1,0:T(8,128)(2,1)S(1)}, bf16[1,16,32,128]{3,2,1,0:T(8,128)(2,1)S(1)}, u32[]{:S(2)}, u32[]{:S(2)}) collective-permute-start(bf16[1,16,32,128]{3,2,1,0:T(8,128)(2,1)S(1)} %get-tuple-element.57), channel_id=1, source_target_pairs={{0,1},{1,0},{2,3},{3,2},{4,5},{5,4},{6,7},{7,6},{8,9},{9,8},{10,11... | collective-permute-start | bytes 393224 | tf_op jit(solution)/shard_map/ppermute | solution.py:306
  30.2 0.8 copy-start.10
  31.7 27.8 %collective-permute-start.10 = (bf16[4,8,32,128]{3,2,1,0:T(8,128)(2,1)S(1)}, bf16[4,8,32,128]{3,2,1,0:T(8,128)(2,1)S(1)}, u32[]{:S(2)}, u32[]{:S(2)}) collective-permute-start(bf16[4,8,32,128]{3,2,1,0:T(8,128)(2,1)S(1)} %collect_blocks.4.refs_1_), channel_id=1, source_target_pairs={{0,1},{1,0},{2,3},{3,2},{4,5},{5,4},{6,7},{7,6},{8,9},{9,8},{10,11... | collective-permute-start | bytes 786440 | tf_op jit(solution)/shard_map/ppermute | solution.py:306
  32.2 15.2 %collective-permute-start.22 = (bf16[1,16,32,128]{3,2,1,0:T(8,128)(2,1)S(1)}, bf16[1,16,32,128]{3,2,1,0:T(8,128)(2,1)S(1)}, u32[]{:S(2)}, u32[]{:S(2)}) collective-permute-start(bf16[1,16,32,128]{3,2,1,0:T(8,128)(2,1)S(1)} %get-tuple-element.58), channel_id=1, source_target_pairs={{0,3},{1,2},{2,1},{3,0},{4,7},{5,6},{6,5},{7,4},{8,11},{9,10},{10,... | collective-permute-start | bytes 393224 | tf_op jit(solution)/shard_map/ppermute | solution.py:306
  38.4 16.3 %collective-permute-start.23 = (bf16[1,16,32,128]{3,2,1,0:T(8,128)(2,1)S(1)}, bf16[1,16,32,128]{3,2,1,0:T(8,128)(2,1)S(1)}, u32[]{:S(2)}, u32[]{:S(2)}) collective-permute-start(bf16[1,16,32,128]{3,2,1,0:T(8,128)(2,1)S(1)} %get-tuple-element.59), channel_id=1, source_target_pairs={{0,5},{1,4},{2,7},{3,6},{4,1},{5,0},{6,3},{7,2},{8,13},{9,12},{10,... | collective-permute-start | bytes 393224 | tf_op jit(solution)/shard_map/ppermute | solution.py:306
  40.6 16.6 %collective-permute-start.24 = (bf16[1,16,32,128]{3,2,1,0:T(8,128)(2,1)S(1)}, bf16[1,16,32,128]{3,2,1,0:T(8,128)(2,1)S(1)}, u32[]{:S(2)}, u32[]{:S(2)}) collective-permute-start(bf16[1,16,32,128]{3,2,1,0:T(8,128)(2,1)S(1)} %get-tuple-element.60), channel_id=1, source_target_pairs={{0,7},{1,6},{2,5},{3,4},{4,3},{5,2},{6,1},{7,0},{8,15},{9,14},{10,... | collective-permute-start | bytes 393224 | tf_op jit(solution)/shard_map/ppermute | solution.py:306
  41.8 15.4 %collective-permute-start = (bf16[1,16,32,128]{3,2,1,0:T(8,128)(2,1)S(1)}, bf16[1,16,32,128]{3,2,1,0:T(8,128)(2,1)S(1)}, u32[]{:S(2)}, u32[]{:S(2)}) collective-permute-start(bf16[1,16,32,128]{3,2,1,0:T(8,128)(2,1)S(1)} %get-tuple-element.37), channel_id=1, source_target_pairs={{0,2},{1,3},{2,0},{3,1},{4,6},{5,7},{6,4},{7,5},{8,10},{9,11},{10,... | collective-permute-start | bytes 393224 | tf_op jit(solution)/shard_map/ppermute | solution.py:306
  47.3 13.6 %collective-permute-start.1 = (bf16[1,16,32,128]{3,2,1,0:T(8,128)(2,1)S(1)}, bf16[1,16,32,128]{3,2,1,0:T(8,128)(2,1)S(1)}, u32[]{:S(2)}, u32[]{:S(2)}) collective-permute-start(bf16[1,16,32,128]{3,2,1,0:T(8,128)(2,1)S(1)} %get-tuple-element.38), channel_id=1, source_target_pairs={{0,4},{1,5},{2,6},{3,7},{4,0},{5,1},{6,2},{7,3},{8,12},{9,13},{10,... | collective-permute-start | bytes 393224 | tf_op jit(solution)/shard_map/ppermute | solution.py:306
  54.7 23.2 %collective-permute-start.2 = (bf16[1,16,32,128]{3,2,1,0:T(8,128)(2,1)S(1)}, bf16[1,16,32,128]{3,2,1,0:T(8,128)(2,1)S(1)}, u32[]{:S(2)}, u32[]{:S(2)}) collective-permute-start(bf16[1,16,32,128]{3,2,1,0:T(8,128)(2,1)S(1)} %get-tuple-element.39), channel_id=1, source_target_pairs={{0,6},{1,7},{2,4},{3,5},{4,2},{5,3},{6,0},{7,1},{8,14},{9,15},{10,... | collective-permute-start | bytes 393224 | tf_op jit(solution)/shard_map/ppermute | solution.py:306
  57.2 20.8 %collective-permute-start.3 = (bf16[1,16,32,128]{3,2,1,0:T(8,128)(2,1)S(1)}, bf16[1,16,32,128]{3,2,1,0:T(8,128)(2,1)S(1)}, u32[]{:S(2)}, u32[]{:S(2)}) collective-permute-start(bf16[1,16,32,128]{3,2,1,0:T(8,128)(2,1)S(1)} %get-tuple-element.40), channel_id=1, source_target_pairs={{0,1},{1,0},{2,3},{3,2},{4,5},{5,4},{6,7},{7,6},{8,9},{9,8},{10,11... | collective-permute-start | bytes 393224 | tf_op jit(solution)/shard_map/ppermute | solution.py:306
  57.2 21.5 %collective-permute-start.4 = (bf16[1,16,32,128]{3,2,1,0:T(8,128)(2,1)S(1)}, bf16[1,16,32,128]{3,2,1,0:T(8,128)(2,1)S(1)}, u32[]{:S(2)}, u32[]{:S(2)}) collective-permute-start(bf16[1,16,32,128]{3,2,1,0:T(8,128)(2,1)S(1)} %get-tuple-element.41), channel_id=1, source_target_pairs={{0,3},{1,2},{2,1},{3,0},{4,7},{5,6},{6,5},{7,4},{8,11},{9,10},{10,... | collective-permute-start | bytes 393224 | tf_op jit(solution)/shard_map/ppermute | solution.py:306
  59.5 22.8 %collective-permute-start.5 = (bf16[1,16,32,128]{3,2,1,0:T(8,128)(2,1)S(1)}, bf16[1,16,32,128]{3,2,1,0:T(8,128)(2,1)S(1)}, u32[]{:S(2)}, u32[]{:S(2)}) collective-permute-start(bf16[1,16,32,128]{3,2,1,0:T(8,128)(2,1)S(1)} %get-tuple-element.42), channel_id=1, source_target_pairs={{0,5},{1,4},{2,7},{3,6},{4,1},{5,0},{6,3},{7,2},{8,13},{9,12},{10,... | collective-permute-start | bytes 393224 | tf_op jit(solution)/shard_map/ppermute | solution.py:306
  60.9 21.4 %collective-permute-start.6 = (bf16[1,16,32,128]{3,2,1,0:T(8,128)(2,1)S(1)}, bf16[1,16,32,128]{3,2,1,0:T(8,128)(2,1)S(1)}, u32[]{:S(2)}, u32[]{:S(2)}) collective-permute-start(bf16[1,16,32,128]{3,2,1,0:T(8,128)(2,1)S(1)} %get-tuple-element.43), channel_id=1, source_target_pairs={{0,7},{1,6},{2,5},{3,4},{4,3},{5,2},{6,1},{7,0},{8,15},{9,14},{10,... | collective-permute-start | bytes 393224 | tf_op jit(solution)/shard_map/ppermute | solution.py:306
  66.8 2.2 %copy-start.4 = (bf16[512,4096]{1,0:T(8,128)(2,1)S(1)}, bf16[512,4096]{1,0:T(8,128)(2,1)}, u32[]{:S(2)}) copy-start(bf16[512,4096]{1,0:T(8,128)(2,1)} %refs_11_.3) | copy-start | bytes 12582916
  69.0 2.2 %copy-start.6 = (bf16[2,1024,1024]{2,1,0:T(8,128)(2,1)S(1)}, bf16[2,1024,1024]{2,1,0:T(8,128)(2,1)}, u32[]{:S(2)}) copy-start(bf16[2,1024,1024]{2,1,0:T(8,128)(2,1)} %constant.19.clone.refs_12_) | copy-start | bytes 12582916
  71.2 11.8 %copy-start.5 = (bf16[512,4096]{1,0:T(8,128)(2,1)S(1)}, bf16[512,4096]{1,0:T(8,128)(2,1)}, u32[]{:S(2)}) copy-start(bf16[512,4096]{1,0:T(8,128)(2,1)} %refs_11_.3) | copy-start | bytes 12582916
  77.9 11.8 %collective-permute-start.25 = (bf16[2,32,1024]{2,1,0:T(8,128)(2,1)S(1)}, bf16[2,32,1024]{2,1,0:T(8,128)(2,1)S(1)}, u32[]{:S(2)}, u32[]{:S(2)}) collective-permute-start(bf16[2,32,1024]{2,1,0:T(8,128)(2,1)S(1)} %get-tuple-element.62), channel_id=1, source_target_pairs={{0,2},{1,3},{2,0},{3,1},{4,6},{5,7},{6,4},{7,5},{8,10},{9,11},{10,... | collective-permute-start | bytes 393224 | tf_op jit(solution)/shard_map/ppermute | solution.py:306
  78.0 13.2 %collective-permute-start.26 = (bf16[2,32,1024]{2,1,0:T(8,128)(2,1)S(1)}, bf16[2,32,1024]{2,1,0:T(8,128)(2,1)S(1)}, u32[]{:S(2)}, u32[]{:S(2)}) collective-permute-start(bf16[2,32,1024]{2,1,0:T(8,128)(2,1)S(1)} %get-tuple-element.63), channel_id=1, source_target_pairs={{0,4},{1,5},{2,6},{3,7},{4,0},{5,1},{6,2},{7,3},{8,12},{9,13},{10,... | collective-permute-start | bytes 393224 | tf_op jit(solution)/shard_map/ppermute | solution.py:306
  78.7 17.2 %collective-permute-start.27 = (bf16[2,32,1024]{2,1,0:T(8,128)(2,1)S(1)}, bf16[2,32,1024]{2,1,0:T(8,128)(2,1)S(1)}, u32[]{:S(2)}, u32[]{:S(2)}) collective-permute-start(bf16[2,32,1024]{2,1,0:T(8,128)(2,1)S(1)} %get-tuple-element.64), channel_id=1, source_target_pairs={{0,6},{1,7},{2,4},{3,5},{4,2},{5,3},{6,0},{7,1},{8,14},{9,15},{10,... | collective-permute-start | bytes 393224 | tf_op jit(solution)/shard_map/ppermute | solution.py:306
  82.4 13.6 %collective-permute-start.28 = (bf16[2,32,1024]{2,1,0:T(8,128)(2,1)S(1)}, bf16[2,32,1024]{2,1,0:T(8,128)(2,1)S(1)}, u32[]{:S(2)}, u32[]{:S(2)}) collective-permute-start(bf16[2,32,1024]{2,1,0:T(8,128)(2,1)S(1)} %get-tuple-element.65), channel_id=1, source_target_pairs={{0,1},{1,0},{2,3},{3,2},{4,5},{5,4},{6,7},{7,6},{8,9},{9,8},{10,11... | collective-permute-start | bytes 393224 | tf_op jit(solution)/shard_map/ppermute | solution.py:306
  82.4 14.3 %collective-permute-start.29 = (bf16[2,32,1024]{2,1,0:T(8,128)(2,1)S(1)}, bf16[2,32,1024]{2,1,0:T(8,128)(2,1)S(1)}, u32[]{:S(2)}, u32[]{:S(2)}) collective-permute-start(bf16[2,32,1024]{2,1,0:T(8,128)(2,1)S(1)} %get-tuple-element.66), channel_id=1, source_target_pairs={{0,3},{1,2},{2,1},{3,0},{4,7},{5,6},{6,5},{7,4},{8,11},{9,10},{10,... | collective-permute-start | bytes 393224 | tf_op jit(solution)/shard_map/ppermute | solution.py:306
  83.0 37.6 %copy-start.7 = (bf16[8,512,512]{2,1,0:T(8,128)(2,1)S(1)}, bf16[8,512,512]{2,1,0:T(8,128)(2,1)}, u32[]{:S(2)}) copy-start(bf16[8,512,512]{2,1,0:T(8,128)(2,1)} %constant.20.clone.refs_17_) | copy-start | bytes 12582916
  89.8 12.0 %collective-permute-start.30 = (bf16[2,32,1024]{2,1,0:T(8,128)(2,1)S(1)}, bf16[2,32,1024]{2,1,0:T(8,128)(2,1)S(1)}, u32[]{:S(2)}, u32[]{:S(2)}) collective-permute-start(bf16[2,32,1024]{2,1,0:T(8,128)(2,1)S(1)} %get-tuple-element.67), channel_id=1, source_target_pairs={{0,5},{1,4},{2,7},{3,6},{4,1},{5,0},{6,3},{7,2},{8,13},{9,12},{10,... | collective-permute-start | bytes 393224 | tf_op jit(solution)/shard_map/ppermute | solution.py:306
  91.2 11.3 %collective-permute-start.31 = (bf16[2,32,1024]{2,1,0:T(8,128)(2,1)S(1)}, bf16[2,32,1024]{2,1,0:T(8,128)(2,1)S(1)}, u32[]{:S(2)}, u32[]{:S(2)}) collective-permute-start(bf16[2,32,1024]{2,1,0:T(8,128)(2,1)S(1)} %get-tuple-element.68), channel_id=1, source_target_pairs={{0,7},{1,6},{2,5},{3,4},{4,3},{5,2},{6,1},{7,0},{8,15},{9,14},{10,... | collective-permute-start | bytes 393224 | tf_op jit(solution)/shard_map/ppermute | solution.py:306
  95.9 15.0 %collective-permute-start.11 = (bf16[2,32,1024]{2,1,0:T(8,128)(2,1)S(1)}, bf16[2,32,1024]{2,1,0:T(8,128)(2,1)S(1)}, u32[]{:S(2)}, u32[]{:S(2)}) collective-permute-start(bf16[2,32,1024]{2,1,0:T(8,128)(2,1)S(1)} %get-tuple-element.47), channel_id=1, source_target_pairs={{0,2},{1,3},{2,0},{3,1},{4,6},{5,7},{6,4},{7,5},{8,10},{9,11},{10,... | collective-permute-start | bytes 393224 | tf_op jit(solution)/shard_map/ppermute | solution.py:306
  96.0 16.4 %collective-permute-start.12 = (bf16[2,32,1024]{2,1,0:T(8,128)(2,1)S(1)}, bf16[2,32,1024]{2,1,0:T(8,128)(2,1)S(1)}, u32[]{:S(2)}, u32[]{:S(2)}) collective-permute-start(bf16[2,32,1024]{2,1,0:T(8,128)(2,1)S(1)} %get-tuple-element.48), channel_id=1, source_target_pairs={{0,4},{1,5},{2,6},{3,7},{4,0},{5,1},{6,2},{7,3},{8,12},{9,13},{10,... | collective-permute-start | bytes 393224 | tf_op jit(solution)/shard_map/ppermute | solution.py:306
  96.7 18.1 %collective-permute-start.13 = (bf16[2,32,1024]{2,1,0:T(8,128)(2,1)S(1)}, bf16[2,32,1024]{2,1,0:T(8,128)(2,1)S(1)}, u32[]{:S(2)}, u32[]{:S(2)}) collective-permute-start(bf16[2,32,1024]{2,1,0:T(8,128)(2,1)S(1)} %get-tuple-element.49), channel_id=1, source_target_pairs={{0,6},{1,7},{2,4},{3,5},{4,2},{5,3},{6,0},{7,1},{8,14},{9,15},{10,... | collective-permute-start | bytes 393224 | tf_op jit(solution)/shard_map/ppermute | solution.py:306
  101.8 12.9 %collective-permute-start.14 = (bf16[2,32,1024]{2,1,0:T(8,128)(2,1)S(1)}, bf16[2,32,1024]{2,1,0:T(8,128)(2,1)S(1)}, u32[]{:S(2)}, u32[]{:S(2)}) collective-permute-start(bf16[2,32,1024]{2,1,0:T(8,128)(2,1)S(1)} %get-tuple-element.50), channel_id=1, source_target_pairs={{0,1},{1,0},{2,3},{3,2},{4,5},{5,4},{6,7},{7,6},{8,9},{9,8},{10,11... | collective-permute-start | bytes 393224 | tf_op jit(solution)/shard_map/ppermute | solution.py:306
  102.5 12.2 %collective-permute-start.15 = (bf16[2,32,1024]{2,1,0:T(8,128)(2,1)S(1)}, bf16[2,32,1024]{2,1,0:T(8,128)(2,1)S(1)}, u32[]{:S(2)}, u32[]{:S(2)}) collective-permute-start(bf16[2,32,1024]{2,1,0:T(8,128)(2,1)S(1)} %get-tuple-element.51), channel_id=1, source_target_pairs={{0,3},{1,2},{2,1},{3,0},{4,7},{5,6},{6,5},{7,4},{8,11},{9,10},{10,... | collective-permute-start | bytes 393224 | tf_op jit(solution)/shard_map/ppermute | solution.py:306
  111.0 9.6 %collective-permute-start.16 = (bf16[2,32,1024]{2,1,0:T(8,128)(2,1)S(1)}, bf16[2,32,1024]{2,1,0:T(8,128)(2,1)S(1)}, u32[]{:S(2)}, u32[]{:S(2)}) collective-permute-start(bf16[2,32,1024]{2,1,0:T(8,128)(2,1)S(1)} %get-tuple-element.52), channel_id=1, source_target_pairs={{0,5},{1,4},{2,7},{3,6},{4,1},{5,0},{6,3},{7,2},{8,13},{9,12},{10,... | collective-permute-start | bytes 393224 | tf_op jit(solution)/shard_map/ppermute | solution.py:306
  112.4 8.2 %collective-permute-start.17 = (bf16[2,32,1024]{2,1,0:T(8,128)(2,1)S(1)}, bf16[2,32,1024]{2,1,0:T(8,128)(2,1)S(1)}, u32[]{:S(2)}, u32[]{:S(2)}) collective-permute-start(bf16[2,32,1024]{2,1,0:T(8,128)(2,1)S(1)} %get-tuple-element.53), channel_id=1, source_target_pairs={{0,7},{1,6},{2,5},{3,4},{4,3},{5,2},{6,1},{7,0},{8,15},{9,14},{10,... | collective-permute-start | bytes 393224 | tf_op jit(solution)/shard_map/ppermute | solution.py:306

commit v3 on v2

--- a/solution.py
+++ b/solution.py
@@ -67,7 +67,8 @@
     return jnp.dot(a, b, preferred_element_type=F32)
 
 
-def pick_kernel(points_ref, tiles_ref, out_ref):
+def pick_kernel(points_ref, tiles_ref, *refs):
+    out_ref = refs[-1]
     rows = tiles_ref.shape[1]
     lane = lax.broadcasted_iota(jnp.int32, (rows, LANES), 1)
 
@@ -82,22 +83,23 @@
         out_ref[group] = total.astype(BF16)
 
 
-def pick(tiles, points):
+def pick(tiles, points, ahead):
     groups = points.shape[0] // LANES
     rows = tiles.shape[1]
     out = pl.pallas_call(
         pick_kernel,
-        in_specs=[pl.BlockSpec(memory_space=pltpu.SMEM), pl.BlockSpec(memory_space=pltpu.VMEM)],
+        in_specs=[pl.BlockSpec(memory_space=pltpu.SMEM), pl.BlockSpec(memory_space=pltpu.VMEM)]
+        + [pl.BlockSpec(memory_space=pl.ANY)] * len(ahead),
         out_specs=pl.BlockSpec(memory_space=pltpu.VMEM),
         out_shape=jax.ShapeDtypeStruct((groups, rows, LANES), BF16),
         compiler_params=pltpu.CompilerParams(vmem_limit_bytes=VMEM_BYTES),
         name="pick_points",
-    )(points, tiles)
+    )(points, tiles, *ahead)
     return out
 
 
 def coef_kernel(picks, inputs, me_ref, *refs):
-    arrays, turn_ref, own_ref, src_ref = refs[:inputs], refs[-3], refs[-2], refs[-1]
+    arrays, turn_ref, own_ref, src_ref = refs[:inputs], refs[inputs], refs[-2], refs[-1]
     values = [arrays[array][lead(me_ref[0])] for array, lead in picks]
     groups = values[0].shape[0] // 2
     nu = groups * LANES
@@ -110,18 +112,18 @@
     src_ref[:, nu:] = (-dot(turn, src)).astype(BF16)
 
 
-def coefficients(me, values, turn):
+def coefficients(me, values, turn, held):
     arrays, picks = distinct(values)
     tiles, rows, _ = arrays[0].shape[1:]
     high, nu = len(values) * rows, tiles // 2 * LANES
     return pl.pallas_call(
         lambda *refs: coef_kernel(picks, len(arrays), *refs),
-        in_specs=[pl.BlockSpec(memory_space=pltpu.SMEM)] + [pl.BlockSpec(memory_space=pltpu.VMEM)] * (len(arrays) + 1),
+        in_specs=[pl.BlockSpec(memory_space=pltpu.SMEM)] + [pl.BlockSpec(memory_space=pltpu.VMEM)] * (len(arrays) + 1 + len(held)),
         out_shape=(jax.ShapeDtypeStruct((2 * nu, high), BF16), jax.ShapeDtypeStruct((high, 2 * nu), BF16)),
         compiler_params=pltpu.CompilerParams(vmem_limit_bytes=VMEM_BYTES),
         cost_estimate=FREE,
         name="coefficients",
-    )(me, *arrays, turn)
+    )(me, *arrays, turn, *held)
 
 
 def exchange_kernel(first_plane, planes, cells, pairs, inputs, me_ref, *refs):
@@ -190,22 +192,6 @@
     return sent, after
 
 
-def gate_kernel(me_ref, *refs):
-    refs[-1][0] = me_ref[0]
-
-
-def gate(me, arrays):
-    smem = pl.BlockSpec(memory_space=pltpu.SMEM)
-    return pl.pallas_call(
-        gate_kernel,
-        in_specs=[smem] + [pl.BlockSpec(memory_space=pl.ANY)] * len(arrays),
-        out_specs=smem,
-        out_shape=jax.ShapeDtypeStruct((1,), jnp.int32),
-        cost_estimate=FREE,
-        name="gate",
-    )(me, *arrays)
-
-
 def collect_kernel(plan, inputs, me_ref, *refs):
     arrays, outs = refs[:inputs], refs[inputs : inputs + len(plan)]
     buffer, in_sems, out_sems = refs[-3:]
@@ -233,6 +219,31 @@
             arrays.append(array)
         places.append((at, lead))
     return arrays, places
+
+
+def send_kernel(leads, me_ref, blocks_ref, *refs):
+    outs, sems = refs[:-1], refs[-1]
+    copies = [
+        pltpu.make_async_copy(blocks_ref.at[lead(me_ref[0])], out.at[0], sems.at[n])
+        for n, (lead, out) in enumerate(zip(leads, outs))
+    ]
+    for copy in copies:
+        copy.start()
+    for copy in copies:
+        copy.wait()
+
+
+def send_blocks(me, blocks, leads):
+    return pl.pallas_call(
+        lambda *refs: send_kernel(leads, *refs),
+        in_specs=[pl.BlockSpec(memory_space=pltpu.SMEM), pl.BlockSpec(memory_space=pltpu.VMEM)],
+        out_specs=[pl.BlockSpec(memory_space=pltpu.HBM)] * len(leads),
+        out_shape=[jax.ShapeDtypeStruct((1,) + blocks.shape[1:], blocks.dtype)] * len(leads),
+        scratch_shapes=[pltpu.SemaphoreType.DMA((len(leads),))],
+        compiler_params=pltpu.CompilerParams(vmem_limit_bytes=VMEM_BYTES),
+        cost_estimate=FREE,
+        name="send_blocks",
+    )(me, blocks)
 
 
 def collect(me, wanted):
@@ -318,6 +329,8 @@
     chunk_tiles = chunk_planes * plane_tiles
 
     order = list(range(0, count, 2)) + list(range(1, count, 2))
+    far = count // 2
+    order_back = [0, 2] + list(range(far, count)) + [k for k in range(far - 1, 0, -1) if k != 2]
 
     tiles = orbitals.reshape(1, bands, 2, all_cells // LANES, LANES).transpose(0, 3, 1, 2, 4)
     tiles = lax.optimization_barrier(tiles.reshape(all_cells // LANES, rows, LANES))
@@ -329,26 +342,13 @@
     def first(me):
         return 0
 
-    def swap_pairs(pairs, me):
-        (other,) = collect(me, [[(pairs[d], lambda me: 1 - me % 2) for d in sorted(pairs)]])
-        swapped = hop(other, 1, count)
-        return [
-            (swapped, lambda me, k=k: k // 2) if k % 2 else (pairs[k], lambda me: me % 2)
-            for k in order
-        ]
-
-    def cross(c, distances, me):
-        wanted = [
-            [(blocks, lambda me, d=d, y=y: ((me ^ d) // 2 * 2 + y) * chunks + c) for y in range(2)]
-            for d in distances
-        ]
-        return {d: hop(pair, d, count) if d else pair for d, pair in zip(distances, collect(me, wanted))}
-
-    def direct(c, distances, me):
-        wanted = [[(blocks, lambda me, d=d: (me ^ d) * chunks + c)] for d in distances]
-        return {d: hop(block, d, count) for d, block in zip(distances, collect(me, wanted))}
-
-    own_values = pick(tiles, points)
+    def blocks_for(c, distances, me):
+        return send_blocks(me, blocks, [lambda me, d=d: (me ^ d) * chunks + c for d in distances])
+
+    distances = list(range(count // 2, count)) + list(range(1, count // 2))
+    late = distances[len(distances) - 1 :]
+    sends = [blocks_for(c, [d for d in distances if c == 0 or d not in late], device) for c in range(chunks)]
+    own_values = pick(tiles, points, sends[0])
     everyone = lax.all_gather(own_values, "kgrp", axis=0, tiled=False)
     chosen = partner == lax.axis_index("kgrp")
     matched = jnp.sum(jnp.where(chosen[:, None, None, None], everyone, jnp.zeros_like(everyone)), axis=0)
@@ -356,29 +356,36 @@
     over_z = [values] + [hop(values, d, count) for d in range(2, count, 2)]
     (here,) = collect(device, [[(part, first) for part in over_z]])
     there = hop(here, 1, count)
+    plane_t = jnp.asarray(plane_table(scale))
     picks = [(there if k % 2 else here, lambda me, i=k // 2: i) for k in order]
-    own_coef, src_coef = coefficients(device, picks, turn)
+    own_coef, src_coef = coefficients(device, picks, turn, [coulomb, plane_t])
 
     received = []
     for c in range(chunks):
         distances = list(range(count // 2, count)) + list(range(1, count // 2))
-        arrived = direct(c, distances, gate(device, [values]) if c == 0 else gate(device, [values]))
-        received.append([(arrived[k], first) if k else (blocks, lambda me, c=c: me * chunks + c) for k in order])
-
-    plane_t = jnp.asarray(plane_table(scale))
+        arrived = {
+            d: hop(block, d, count)
+            for d, block in zip([d for d in distances if c == 0 or d not in late], sends[c])
+        }
+        received.append(arrived)
+
     groups = 2 if bands % 16 == 0 else 1
-    line_t = jnp.asarray(line_table(scale, order, planes, bands // groups))
+    line_t = jnp.asarray(line_table(scale, order_back, planes, bands // groups))
 
     fields = []
     for c in range(chunks):
-        sent, _ = exchange(
-            device, received[c], own_coef, src_coef, coulomb, plane_t, turn, c * chunk_planes, chunk_planes,
+        arrived = received[c]
+        if c:
+            arrived.update({d: hop(block, d, count) for d, block in zip(late, blocks_for(c, late, after))})
+        here = [(arrived[k], first) if k else (blocks, lambda me, c=c: me * chunks + c) for k in order]
+        sent, after = exchange(
+            device, here, own_coef, src_coef, coulomb, plane_t, turn, c * chunk_planes, chunk_planes,
             [(at, None) for at in range(count)],
         )
         back = {0: sent[0]}
         for k in list(range(count // 2, count)) + list(range(1, count // 2)):
             back[k] = hop(sent[order.index(k)], k, count)
-        fields += [(back[k][None], first) for k in order]
+        fields += [(back[k][None], first) for k in order_back]
 
     factor = 1.0 / (scale * scale * math.sqrt(GX * GY * GZ))
     out = line_pass(device, fields, line_t, factor, rows, groups, count)

time: 124 us -> 118 us (0.952)
  waiting for transfers between devices: 16.8 us -> 26.7 us
  local copies, waits for them, and re-layouts: 11.2 us -> 3.06 us
  starting transfers between devices: 61.5 us -> 56.2 us
  Pallas kernels: 27.8 us -> 24 us
    ppermute x32, waiting for transfers between devices: 16.8 us -> 26.7 us  [hop(): lax.ppermute(array, 'band', [(i, i ^ distance) for i in range(count)])]
    unnamed x26 -> x14, local copies, waits for them, and re-layouts: 9.73 us -> 1.62 us
    pallas_call x3 -> x1, Pallas kernels: 7.13 us -> 0.73 us  [collect(): pl.pallas_call(lambda *refs: collect_kernel(plan, len(arrays), *refs), in...]
    ppermute x32, starting transfers between devices: 61.5 us -> 56.2 us  [hop(): lax.ppermute(array, 'band', [(i, i ^ distance) for i in range(count)])]
    pallas_call x1 -> x3, Pallas kernels: 0.52 us -> 3.13 us  [send_blocks(): pl.pallas_call(lambda *refs: send_kernel(leads, *refs), in_specs=[pl.Bloc...]
  transfers between devices with their start and end apart: 32 -> 32, of which waited for: 5 -> 11; matrix products, arithmetic and copies ran while one was open for 0% -> 0% of each run, Pallas kernels for 17% -> 14%
where the time goes in v3:
time: 118 us; the launch traced here: 117 us
  starting transfers between devices  56.2 us (48%)
  waiting for transfers between devices  26.7 us (23%)
  Pallas kernels  24 us (20%)
  blocking collectives  6.61 us (6%)
  local copies, waits for them, and re-layouts  3.06 us (3%)
    ppermute x32, starting transfers between devices, hop(): lax.ppermute(array, 'band', [(i, i ^ distance) for i in range(count)])  56.2 us
    ppermute x32, waiting for transfers between devices, hop(): lax.ppermute(array, 'band', [(i, i ^ distance) for i in range(count)])  26.7 us
    pallas_call x2, Pallas kernels, exchange(): pl.pallas_call(lambda *refs: exchange_kernel(first_plane, planes, places,...  13.4 us
    all_gather x1, blocking collectives, body(): everyone = lax.all_gather(own_values, 'kgrp', axis=0, tiled=False)  6.61 us
    pallas_call x1, Pallas kernels, line_pass(): pl.pallas_call(lambda *refs: line_kernel(factor, group_rows, count, *refs...  3.49 us
    pallas_call x3, Pallas kernels, send_blocks(): pl.pallas_call(lambda *refs: send_kernel(leads, *refs), in_specs=[pl.Bloc...  3.13 us
    pallas_call x1, Pallas kernels, pick(): pl.pallas_call(pick_kernel, in_specs=[pl.BlockSpec(memory_space=pltpu.SME...  2.94 us
  transfers between devices with their start and end apart: 32, of which 11 were waited for; matrix products, arithmetic and copies ran while one was open for 0% of the time, Pallas kernels for 14%

profile of v3, /device:TPU:0, one launch (start us, length us, event | category | flops | bytes accessed | tf_op | source)
XLA Modules:
  0.0 116.9 jit_solution(14846794400726729814)
XLA Ops:
  0.0 1.6 %copy-done = bf16[1,16,2,32768]{3,2,1,0:T(2,128)(2,1)S(1)} copy-done((bf16[1,16,2,32768]{3,2,1,0:T(2,128)(2,1)S(1)}, bf16[1,16,2,32768]{3,2,1,0:T(2,128)(2,1)}, u32[]{:S(2)}) %copy-start) | copy-done | bytes 2097176
  1.6 1.4 %copy_bitcast_fusion = bf16[1,16,2,256,128]{4,2,1,3,0:T(2,128)(2,1)S(1)} fusion(bf16[1,16,2,32768]{3,2,1,0:T(2,128)(2,1)S(1)} %copy-done), kind=kLoop, calls=%fused_computation | loop fusion | bytes 4194304 | tf_op jit(solution)/shard_map/reshape | solution.py:335
  3.0 1.3 %send_blocks.3 = (bf16[1,16,32,128]{3,2,1,0:T(8,128)(2,1)S(1)}, bf16[1,16,32,128]{3,2,1,0:T(8,128)(2,1)S(1)}, bf16[1,16,32,128]{3,2,1,0:T(8,128)(2,1)S(1)}, bf16...) custom-call(s32[1]{0:T(128)} %bitcast.refs_0_, ...), custom_call_target="tpu_custom_call" | custom-call | flops 1 | bytes 1 | tf_op jit(solution)/shard_map/send_blocks/pallas_call | solution.py:237
  4.4 2.9 %pick_points.1 = bf16[4,32,128]{2,1,0:T(8,128)(2,1)S(1)} custom-call(s32[512]{0:T(512)S(1)} %copy-done.5, bf16[256,32,128]{2,1,0:T(8,128)(2,1)S(1)} %bitcast.35, bf16[1,16,32,128]{3,2,1,0:T(8,128)(2,1)S(1)} %get-tuple-element.38.refs_0_, bf16[1,16,32,128]{3,2,1,0:T(8,128)(2,1)S(1)} %get-tuple-element.42.refs_1_, ...), custom_call_target="tpu_custom_call" | custom-call | tf_op jit(solution)/shard_map/pick_points/pallas_call | solution.py:89
  7.3 6.6 %all-gather = bf16[16,32,128]{2,1,0:T(8,128)(2,1)S(1)} all-gather(bf16[4,32,128]{2,1,0:T(8,128)(2,1)S(1)} %pick_points.1), channel_id=2, replica_groups=mesh['kgrp'=4,'band'=8] {'kgrp'}, dimensions={0}, use_global_device_ids=true | all-gather | bytes 163840 | tf_op jit(solution)/shard_map/all_gather | solution.py:352
  14.0 4.1 %collective-permute-start.9 = (bf16[1,8,32,128]{3,2,1,0:T(8,128)(2,1)S(1)}, bf16[1,8,32,128]{3,2,1,0:T(8,128)(2,1)S(1)}, u32[]{:S(2)}, u32[]{:S(2)}) collective-permute-start(bf16[1,8,32,128]{3,2,1,0:T(8,128)(2,1)S(1)} %maximum_bitcast_fusion.refs_1_), channel_id=1, source_target_pairs={{0,6},{1,7},{2,4},{3,5},{4,2},{5,3},{6,0},{7,1},{8,14},{9,15},{10,... | collective-permute-start | bytes 196616 | tf_op jit(solution)/shard_map/ppermute | solution.py:317
  18.1 0.6 collective-permute-start.7
  18.8 1.0 send_blocks.4
  19.8 1.5 %collective-permute-start.18 = (bf16[1,16,32,128]{3,2,1,0:T(8,128)(2,1)S(1)}, bf16[1,16,32,128]{3,2,1,0:T(8,128)(2,1)S(1)}, u32[]{:S(2)}, u32[]{:S(2)}) collective-permute-start(bf16[1,16,32,128]{3,2,1,0:T(8,128)(2,1)S(1)} %get-tuple-element.54), channel_id=1, source_target_pairs={{0,2},{1,3},{2,0},{3,1},{4,6},{5,7},{6,4},{7,5},{8,10},{9,11},{10,... | collective-permute-start | bytes 393224 | tf_op jit(solution)/shard_map/ppermute | solution.py:317
  21.3 0.6 collective-permute-start
  21.9 2.4 %collective-permute-start.1 = (bf16[1,16,32,128]{3,2,1,0:T(8,128)(2,1)S(1)}, bf16[1,16,32,128]{3,2,1,0:T(8,128)(2,1)S(1)}, u32[]{:S(2)}, u32[]{:S(2)}) collective-permute-start(bf16[1,16,32,128]{3,2,1,0:T(8,128)(2,1)S(1)} %get-tuple-element.38.refs_0_), channel_id=1, source_target_pairs={{0,4},{1,5},{2,6},{3,7},{4,0},{5,1},{6,2},{7,3},{8,12},{9,13},{10,... | collective-permute-start | bytes 393224 | tf_op jit(solution)/shard_map/ppermute | solution.py:317
  24.3 2.3 %collective-permute-start.2 = (bf16[1,16,32,128]{3,2,1,0:T(8,128)(2,1)S(1)}, bf16[1,16,32,128]{3,2,1,0:T(8,128)(2,1)S(1)}, u32[]{:S(2)}, u32[]{:S(2)}) collective-permute-start(bf16[1,16,32,128]{3,2,1,0:T(8,128)(2,1)S(1)} %get-tuple-element.39.refs_2_), channel_id=1, source_target_pairs={{0,6},{1,7},{2,4},{3,5},{4,2},{5,3},{6,0},{7,1},{8,14},{9,15},{10,... | collective-permute-start | bytes 393224 | tf_op jit(solution)/shard_map/ppermute | solution.py:317
  26.6 0.7 collect_blocks.1.refs_1_
  27.3 1.6 %collective-permute-start.10 = (bf16[4,8,32,128]{3,2,1,0:T(8,128)(2,1)S(1)}, bf16[4,8,32,128]{3,2,1,0:T(8,128)(2,1)S(1)}, u32[]{:S(2)}, u32[]{:S(2)}) collective-permute-start(bf16[4,8,32,128]{3,2,1,0:T(8,128)(2,1)S(1)} %collect_blocks.1.refs_1_), channel_id=1, source_target_pairs={{0,1},{1,0},{2,3},{3,2},{4,5},{5,4},{6,7},{7,6},{8,9},{9,8},{10,11... | collective-permute-start | bytes 786440 | tf_op jit(solution)/shard_map/ppermute | solution.py:317
  28.9 0.9 collective-permute-done.18.refs_2_
  29.8 1.5 %collective-permute-start.3 = (bf16[1,16,32,128]{3,2,1,0:T(8,128)(2,1)S(1)}, bf16[1,16,32,128]{3,2,1,0:T(8,128)(2,1)S(1)}, u32[]{:S(2)}, u32[]{:S(2)}) collective-permute-start(bf16[1,16,32,128]{3,2,1,0:T(8,128)(2,1)S(1)} %get-tuple-element.40.refs_4_), channel_id=1, source_target_pairs={{0,1},{1,0},{2,3},{3,2},{4,5},{5,4},{6,7},{7,6},{8,9},{9,8},{10,11... | collective-permute-start | bytes 393224 | tf_op jit(solution)/shard_map/ppermute | solution.py:317
  31.4 0.9 collective-permute-done.refs_2_
  32.2 0.5 collective-permute-start.4
  32.7 3.7 %collective-permute-start.5 = (bf16[1,16,32,128]{3,2,1,0:T(8,128)(2,1)S(1)}, bf16[1,16,32,128]{3,2,1,0:T(8,128)(2,1)S(1)}, u32[]{:S(2)}, u32[]{:S(2)}) collective-permute-start(bf16[1,16,32,128]{3,2,1,0:T(8,128)(2,1)S(1)} %get-tuple-element.42.refs_1_), channel_id=1, source_target_pairs={{0,5},{1,4},{2,7},{3,6},{4,1},{5,0},{6,3},{7,2},{8,13},{9,12},{10,... | collective-permute-start | bytes 393224 | tf_op jit(solution)/shard_map/ppermute | solution.py:317
  36.4 3.5 %collective-permute-start.6 = (bf16[1,16,32,128]{3,2,1,0:T(8,128)(2,1)S(1)}, bf16[1,16,32,128]{3,2,1,0:T(8,128)(2,1)S(1)}, u32[]{:S(2)}, u32[]{:S(2)}) collective-permute-start(bf16[1,16,32,128]{3,2,1,0:T(8,128)(2,1)S(1)} %get-tuple-element.43.refs_3_), channel_id=1, source_target_pairs={{0,7},{1,6},{2,5},{3,4},{4,3},{5,2},{6,1},{7,0},{8,15},{9,14},{10,... | collective-permute-start | bytes 393224 | tf_op jit(solution)/shard_map/ppermute | solution.py:317
  39.9 3.5 %collective-permute-done.3.refs_5_ = bf16[1,16,32,128]{3,2,1,0:T(8,128)(2,1)S(1)} collective-permute-done((bf16[1,16,32,128]{3,2,1,0:T(8,128)(2,1)S(1)}, bf16[1,16,32,128]{3,2,1,0:T(8,128)(2,1)S(1)}, u32[]{:S(2)}, u32[]{:S(2)}) %collective-permute-start.3) | collective-permute-done | bytes 131104 | tf_op jit(solution)/shard_map/ppermute | solution.py:317
  43.4 0.8 collective-permute-start.20
  44.1 8.2 %collective-permute-done.5.refs_7_ = bf16[1,16,32,128]{3,2,1,0:T(8,128)(2,1)S(1)} collective-permute-done((bf16[1,16,32,128]{3,2,1,0:T(8,128)(2,1)S(1)}, bf16[1,16,32,128]{3,2,1,0:T(8,128)(2,1)S(1)}, u32[]{:S(2)}, u32[]{:S(2)}) %collective-permute-start.5) | collective-permute-done | bytes 131104 | tf_op jit(solution)/shard_map/ppermute | solution.py:317
  52.3 1.7 %collective-permute-start.21 = (bf16[1,16,32,128]{3,2,1,0:T(8,128)(2,1)S(1)}, bf16[1,16,32,128]{3,2,1,0:T(8,128)(2,1)S(1)}, u32[]{:S(2)}, u32[]{:S(2)}) collective-permute-start(bf16[1,16,32,128]{3,2,1,0:T(8,128)(2,1)S(1)} %get-tuple-element.57), channel_id=1, source_target_pairs={{0,1},{1,0},{2,3},{3,2},{4,5},{5,4},{6,7},{7,6},{8,9},{9,8},{10,11... | collective-permute-start | bytes 393224 | tf_op jit(solution)/shard_map/ppermute | solution.py:317
  54.0 3.3 %collective-permute-start.23 = (bf16[1,16,32,128]{3,2,1,0:T(8,128)(2,1)S(1)}, bf16[1,16,32,128]{3,2,1,0:T(8,128)(2,1)S(1)}, u32[]{:S(2)}, u32[]{:S(2)}) collective-permute-start(bf16[1,16,32,128]{3,2,1,0:T(8,128)(2,1)S(1)} %get-tuple-element.59), channel_id=1, source_target_pairs={{0,5},{1,4},{2,7},{3,6},{4,1},{5,0},{6,3},{7,2},{8,13},{9,12},{10,... | collective-permute-start | bytes 393224 | tf_op jit(solution)/shard_map/ppermute | solution.py:317
  57.3 1.7 %collective-permute-start.24 = (bf16[1,16,32,128]{3,2,1,0:T(8,128)(2,1)S(1)}, bf16[1,16,32,128]{3,2,1,0:T(8,128)(2,1)S(1)}, u32[]{:S(2)}, u32[]{:S(2)}) collective-permute-start(bf16[1,16,32,128]{3,2,1,0:T(8,128)(2,1)S(1)} %get-tuple-element.60), channel_id=1, source_target_pairs={{0,7},{1,6},{2,5},{3,4},{4,3},{5,2},{6,1},{7,0},{8,15},{9,14},{10,... | collective-permute-start | bytes 393224 | tf_op jit(solution)/shard_map/ppermute | solution.py:317
  59.0 0.3 coefficients.1
  59.3 6.7 %exchange_planes.2 = (bf16[2,32,1024]{2,1,0:T(8,128)(2,1)S(1)}, bf16[2,32,1024]{2,1,0:T(8,128)(2,1)S(1)}, bf16[2,32,1024]{2,1,0:T(8,128)(2,1)S(1)}, bf16[2,32,10...) custom-call(s32[1]{0:T(128)} %bitcast.refs_0_, ...), custom_call_target="tpu_custom_call" | custom-call | flops 1 | bytes 1 | tf_op jit(solution)/shard_map/exchange_planes/pallas_call | solution.py:181
  66.0 0.8 send_blocks.5
  67.0 3.1 %collective-permute-start.11 = (bf16[2,32,1024]{2,1,0:T(8,128)(2,1)S(1)}, bf16[2,32,1024]{2,1,0:T(8,128)(2,1)S(1)}, u32[]{:S(2)}, u32[]{:S(2)}) collective-permute-start(bf16[2,32,1024]{2,1,0:T(8,128)(2,1)S(1)} %get-tuple-element.47), channel_id=1, source_target_pairs={{0,2},{1,3},{2,0},{3,1},{4,6},{5,7},{6,4},{7,5},{8,10},{9,11},{10,... | collective-permute-start | bytes 393224 | tf_op jit(solution)/shard_map/ppermute | solution.py:317
  70.1 0.5 collective-permute-start.12
  70.7 2.2 %collective-permute-start.13 = (bf16[2,32,1024]{2,1,0:T(8,128)(2,1)S(1)}, bf16[2,32,1024]{2,1,0:T(8,128)(2,1)S(1)}, u32[]{:S(2)}, u32[]{:S(2)}) collective-permute-start(bf16[2,32,1024]{2,1,0:T(8,128)(2,1)S(1)} %get-tuple-element.49), channel_id=1, source_target_pairs={{0,5},{1,4},{2,7},{3,6},{4,1},{5,0},{6,3},{7,2},{8,13},{9,12},{10,... | collective-permute-start | bytes 393224 | tf_op jit(solution)/shard_map/ppermute | solution.py:317
  72.8 2.8 %collective-permute-start.14 = (bf16[2,32,1024]{2,1,0:T(8,128)(2,1)S(1)}, bf16[2,32,1024]{2,1,0:T(8,128)(2,1)S(1)}, u32[]{:S(2)}, u32[]{:S(2)}) collective-permute-start(bf16[2,32,1024]{2,1,0:T(8,128)(2,1)S(1)} %get-tuple-element.50), channel_id=1, source_target_pairs={{0,6},{1,7},{2,4},{3,5},{4,2},{5,3},{6,0},{7,1},{8,14},{9,15},{10,... | collective-permute-start | bytes 393224 | tf_op jit(solution)/shard_map/ppermute | solution.py:317
  75.6 0.6 collective-permute-done.22.refs_6_
  76.2 1.6 %collective-permute-start.15 = (bf16[2,32,1024]{2,1,0:T(8,128)(2,1)S(1)}, bf16[2,32,1024]{2,1,0:T(8,128)(2,1)S(1)}, u32[]{:S(2)}, u32[]{:S(2)}) collective-permute-start(bf16[2,32,1024]{2,1,0:T(8,128)(2,1)S(1)} %get-tuple-element.51), channel_id=1, source_target_pairs={{0,7},{1,6},{2,5},{3,4},{4,3},{5,2},{6,1},{7,0},{8,15},{9,14},{10,... | collective-permute-start | bytes 393224 | tf_op jit(solution)/shard_map/ppermute | solution.py:317
  77.8 6.7 %exchange_planes.3 = (bf16[2,32,1024]{2,1,0:T(8,128)(2,1)S(1)}, bf16[2,32,1024]{2,1,0:T(8,128)(2,1)S(1)}, bf16[2,32,1024]{2,1,0:T(8,128)(2,1)S(1)}, bf16[2,32,10...) custom-call(s32[1]{0:T(128)} %bitcast.refs_0_, ...), custom_call_target="tpu_custom_call" | custom-call | flops 1 | bytes 1 | tf_op jit(solution)/shard_map/exchange_planes/pallas_call | solution.py:181
  84.6 2.7 %collective-permute-done.12 = bf16[2,32,1024]{2,1,0:T(8,128)(2,1)S(1)} collective-permute-done((bf16[2,32,1024]{2,1,0:T(8,128)(2,1)S(1)}, bf16[2,32,1024]{2,1,0:T(8,128)(2,1)S(1)}, u32[]{:S(2)}, u32[]{:S(2)}) %collective-permute-start.12) | collective-permute-done | bytes 131104 | tf_op jit(solution)/shard_map/ppermute | solution.py:317
  87.3 1.2 %collective-permute-start.17 = (bf16[2,32,1024]{2,1,0:T(8,128)(2,1)S(1)}, bf16[2,32,1024]{2,1,0:T(8,128)(2,1)S(1)}, u32[]{:S(2)}, u32[]{:S(2)}) collective-permute-start(bf16[2,32,1024]{2,1,0:T(8,128)(2,1)S(1)} %get-tuple-element.53), channel_id=1, source_target_pairs={{0,1},{1,0},{2,3},{3,2},{4,5},{5,4},{6,7},{7,6},{8,9},{9,8},{10,11... | collective-permute-start | bytes 393224 | tf_op jit(solution)/shard_map/ppermute | solution.py:317
  88.5 2.2 %collective-permute-done.13 = bf16[2,32,1024]{2,1,0:T(8,128)(2,1)S(1)} collective-permute-done((bf16[2,32,1024]{2,1,0:T(8,128)(2,1)S(1)}, bf16[2,32,1024]{2,1,0:T(8,128)(2,1)S(1)}, u32[]{:S(2)}, u32[]{:S(2)}) %collective-permute-start.13) | collective-permute-done | bytes 131104 | tf_op jit(solution)/shard_map/ppermute | solution.py:317
  90.7 2.4 %collective-permute-start.26 = (bf16[2,32,1024]{2,1,0:T(8,128)(2,1)S(1)}, bf16[2,32,1024]{2,1,0:T(8,128)(2,1)S(1)}, u32[]{:S(2)}, u32[]{:S(2)}) collective-permute-start(bf16[2,32,1024]{2,1,0:T(8,128)(2,1)S(1)} %get-tuple-element.63), channel_id=1, source_target_pairs={{0,4},{1,5},{2,6},{3,7},{4,0},{5,1},{6,2},{7,3},{8,12},{9,13},{10,... | collective-permute-start | bytes 393224 | tf_op jit(solution)/shard_map/ppermute | solution.py:317
  93.2 5.1 %collective-permute-start.27 = (bf16[2,32,1024]{2,1,0:T(8,128)(2,1)S(1)}, bf16[2,32,1024]{2,1,0:T(8,128)(2,1)S(1)}, u32[]{:S(2)}, u32[]{:S(2)}) collective-permute-start(bf16[2,32,1024]{2,1,0:T(8,128)(2,1)S(1)} %get-tuple-element.64), channel_id=1, source_target_pairs={{0,5},{1,4},{2,7},{3,6},{4,1},{5,0},{6,3},{7,2},{8,13},{9,12},{10,... | collective-permute-start | bytes 393224 | tf_op jit(solution)/shard_map/ppermute | solution.py:317
  98.3 4.1 %collective-permute-start.28 = (bf16[2,32,1024]{2,1,0:T(8,128)(2,1)S(1)}, bf16[2,32,1024]{2,1,0:T(8,128)(2,1)S(1)}, u32[]{:S(2)}, u32[]{:S(2)}) collective-permute-start(bf16[2,32,1024]{2,1,0:T(8,128)(2,1)S(1)} %get-tuple-element.65), channel_id=1, source_target_pairs={{0,6},{1,7},{2,4},{3,5},{4,2},{5,3},{6,0},{7,1},{8,14},{9,15},{10,... | collective-permute-start | bytes 393224 | tf_op jit(solution)/shard_map/ppermute | solution.py:317
  102.4 0.6 collective-permute-start.29
  103.0 2.4 %collective-permute-done.26 = bf16[2,32,1024]{2,1,0:T(8,128)(2,1)S(1)} collective-permute-done((bf16[2,32,1024]{2,1,0:T(8,128)(2,1)S(1)}, bf16[2,32,1024]{2,1,0:T(8,128)(2,1)S(1)}, u32[]{:S(2)}, u32[]{:S(2)}) %collective-permute-start.26) | collective-permute-done | bytes 131104 | tf_op jit(solution)/shard_map/ppermute | solution.py:317
  105.4 2.7 %collective-permute-start.31 = (bf16[2,32,1024]{2,1,0:T(8,128)(2,1)S(1)}, bf16[2,32,1024]{2,1,0:T(8,128)(2,1)S(1)}, u32[]{:S(2)}, u32[]{:S(2)}) collective-permute-start(bf16[2,32,1024]{2,1,0:T(8,128)(2,1)S(1)} %get-tuple-element.68), channel_id=1, source_target_pairs={{0,1},{1,0},{2,3},{3,2},{4,5},{5,4},{6,7},{7,6},{8,9},{9,8},{10,11... | collective-permute-start | bytes 393224 | tf_op jit(solution)/shard_map/ppermute | solution.py:317
  108.1 3.7 %collective-permute-done.27 = bf16[2,32,1024]{2,1,0:T(8,128)(2,1)S(1)} collective-permute-done((bf16[2,32,1024]{2,1,0:T(8,128)(2,1)S(1)}, bf16[2,32,1024]{2,1,0:T(8,128)(2,1)S(1)}, u32[]{:S(2)}, u32[]{:S(2)}) %collective-permute-start.27) | collective-permute-done | bytes 131104 | tf_op jit(solution)/shard_map/ppermute | solution.py:317
  112.1 1.3 %collective-permute-done.31 = bf16[2,32,1024]{2,1,0:T(8,128)(2,1)S(1)} collective-permute-done((bf16[2,32,1024]{2,1,0:T(8,128)(2,1)S(1)}, bf16[2,32,1024]{2,1,0:T(8,128)(2,1)S(1)}, u32[]{:S(2)}, u32[]{:S(2)}) %collective-permute-start.31) | collective-permute-done | bytes 131104 | tf_op jit(solution)/shard_map/ppermute | solution.py:317
  113.4 3.5 %line_pass.1 = bf16[512,8,2,128]{3,2,1,0:T(2,128)(2,1)} custom-call(s32[1]{0:T(128)} %bitcast.refs_0_, bf16[1,2,32,1024]{3,2,1,0:T(8,128)(2,1)S(1)} %bitcast.40, bf16[1,2,32,1024]{3,2,1,0:T(8,128)(2,1)S(1)} %bitcast.41, bf16[1,2,32,1024]{3,2,1,0:T(8,128)(2,1)S(1)} %bitcast.42, bf16[1,2,32,1024]{3,2,1,0:T(8,128)(2,1)S(1)} %bitcast.43, ...), custom_call_target="tpu_custom_call" | custom-call | flops 1 | bytes 1 | tf_op jit(solution)/shard_map/line_pass/pallas_call | solution.py:306
  (44 shorter events, 0.6 us)
Async XLA Ops:
  0.0 1.6 %copy-start = (bf16[1,16,2,32768]{3,2,1,0:T(2,128)(2,1)S(1)}, bf16[1,16,2,32768]{3,2,1,0:T(2,128)(2,1)}, u32[]{:S(2)}) copy-start(bf16[1,16,2,32768]{3,2,1,0:T(2,128)(2,1)} %param.7) | copy-start | bytes 6291460
  1.6 57.4 %copy-start.2 = (bf16[2,1024,1024]{2,1,0:T(8,128)(2,1)S(1)}, bf16[2,1024,1024]{2,1,0:T(8,128)(2,1)}, u32[]{:S(2)}) copy-start(bf16[2,1024,1024]{2,1,0:T(8,128)(2,1)} %constant.19.clone.refs_5_.refs_12_) | copy-start | bytes 12582916
  3.0 1.3 %copy-start.5 = (s32[512]{0:T(512)S(1)}, s32[512]{0:T(512)}, u32[]{:S(2)}) copy-start(s32[512]{0:T(512)} %points_ref.1) | copy-start | bytes 6148
  4.3 9.6 %copy-start.6 = (s32[4]{0:T(128)S(1)}, s32[4]{0:T(128)}, u32[]{:S(2)}) copy-start(s32[4]{0:T(128)} %param.9) | copy-start | bytes 52
  4.3 54.6 %copy-start.1 = (bf16[512,4096]{1,0:T(8,128)(2,1)S(1)}, bf16[512,4096]{1,0:T(8,128)(2,1)}, u32[]{:S(2)}) copy-start(bf16[512,4096]{1,0:T(8,128)(2,1)} %refs_11_.3) | copy-start | bytes 12582916
  7.3 51.7 %copy-start.4 = (bf16[256,256]{1,0:T(8,128)(2,1)S(1)}, bf16[256,256]{1,0:T(8,128)(2,1)}, u32[]{:S(2)}) copy-start(bf16[256,256]{1,0:T(8,128)(2,1)} %constant.18.clone.refs_3_.refs_13_) | copy-start | bytes 393220
  14.0 7.8 %collective-permute-start.9 = (bf16[1,8,32,128]{3,2,1,0:T(8,128)(2,1)S(1)}, bf16[1,8,32,128]{3,2,1,0:T(8,128)(2,1)S(1)}, u32[]{:S(2)}, u32[]{:S(2)}) collective-permute-start(bf16[1,8,32,128]{3,2,1,0:T(8,128)(2,1)S(1)} %maximum_bitcast_fusion.refs_1_), channel_id=1, source_target_pairs={{0,6},{1,7},{2,4},{3,5},{4,2},{5,3},{6,0},{7,1},{8,14},{9,15},{10,... | collective-permute-start | bytes 196616 | tf_op jit(solution)/shard_map/ppermute | solution.py:317
  18.1 6.2 %collective-permute-start.8 = (bf16[1,8,32,128]{3,2,1,0:T(8,128)(2,1)S(1)}, bf16[1,8,32,128]{3,2,1,0:T(8,128)(2,1)S(1)}, u32[]{:S(2)}, u32[]{:S(2)}) collective-permute-start(bf16[1,8,32,128]{3,2,1,0:T(8,128)(2,1)S(1)} %maximum_bitcast_fusion.refs_1_), channel_id=1, source_target_pairs={{0,4},{1,5},{2,6},{3,7},{4,0},{5,1},{6,2},{7,3},{8,12},{9,13},{10,... | collective-permute-start | bytes 196616 | tf_op jit(solution)/shard_map/ppermute | solution.py:317
  18.1 8.5 %collective-permute-start.7 = (bf16[1,8,32,128]{3,2,1,0:T(8,128)(2,1)S(1)}, bf16[1,8,32,128]{3,2,1,0:T(8,128)(2,1)S(1)}, u32[]{:S(2)}, u32[]{:S(2)}) collective-permute-start(bf16[1,8,32,128]{3,2,1,0:T(8,128)(2,1)S(1)} %maximum_bitcast_fusion.refs_1_), channel_id=1, source_target_pairs={{0,2},{1,3},{2,0},{3,1},{4,6},{5,7},{6,4},{7,5},{8,10},{9,11},{10,... | collective-permute-start | bytes 196616 | tf_op jit(solution)/shard_map/ppermute | solution.py:317
  19.8 10.0 %collective-permute-start.18 = (bf16[1,16,32,128]{3,2,1,0:T(8,128)(2,1)S(1)}, bf16[1,16,32,128]{3,2,1,0:T(8,128)(2,1)S(1)}, u32[]{:S(2)}, u32[]{:S(2)}) collective-permute-start(bf16[1,16,32,128]{3,2,1,0:T(8,128)(2,1)S(1)} %get-tuple-element.54), channel_id=1, source_target_pairs={{0,2},{1,3},{2,0},{3,1},{4,6},{5,7},{6,4},{7,5},{8,10},{9,11},{10,... | collective-permute-start | bytes 393224 | tf_op jit(solution)/shard_map/ppermute | solution.py:317
  21.3 11.0 %collective-permute-start = (bf16[1,16,32,128]{3,2,1,0:T(8,128)(2,1)S(1)}, bf16[1,16,32,128]{3,2,1,0:T(8,128)(2,1)S(1)}, u32[]{:S(2)}, u32[]{:S(2)}) collective-permute-start(bf16[1,16,32,128]{3,2,1,0:T(8,128)(2,1)S(1)} %get-tuple-element.37.refs_5_), channel_id=1, source_target_pairs={{0,2},{1,3},{2,0},{3,1},{4,6},{5,7},{6,4},{7,5},{8,10},{9,11},{10,... | collective-permute-start | bytes 393224 | tf_op jit(solution)/shard_map/ppermute | solution.py:317
  21.9 10.8 %collective-permute-start.1 = (bf16[1,16,32,128]{3,2,1,0:T(8,128)(2,1)S(1)}, bf16[1,16,32,128]{3,2,1,0:T(8,128)(2,1)S(1)}, u32[]{:S(2)}, u32[]{:S(2)}) collective-permute-start(bf16[1,16,32,128]{3,2,1,0:T(8,128)(2,1)S(1)} %get-tuple-element.38.refs_0_), channel_id=1, source_target_pairs={{0,4},{1,5},{2,6},{3,7},{4,0},{5,1},{6,2},{7,3},{8,12},{9,13},{10,... | collective-permute-start | bytes 393224 | tf_op jit(solution)/shard_map/ppermute | solution.py:317
  24.3 12.2 %collective-permute-start.2 = (bf16[1,16,32,128]{3,2,1,0:T(8,128)(2,1)S(1)}, bf16[1,16,32,128]{3,2,1,0:T(8,128)(2,1)S(1)}, u32[]{:S(2)}, u32[]{:S(2)}) collective-permute-start(bf16[1,16,32,128]{3,2,1,0:T(8,128)(2,1)S(1)} %get-tuple-element.39.refs_2_), channel_id=1, source_target_pairs={{0,6},{1,7},{2,4},{3,5},{4,2},{5,3},{6,0},{7,1},{8,14},{9,15},{10,... | collective-permute-start | bytes 393224 | tf_op jit(solution)/shard_map/ppermute | solution.py:317
  27.3 30.0 %collective-permute-start.10 = (bf16[4,8,32,128]{3,2,1,0:T(8,128)(2,1)S(1)}, bf16[4,8,32,128]{3,2,1,0:T(8,128)(2,1)S(1)}, u32[]{:S(2)}, u32[]{:S(2)}) collective-permute-start(bf16[4,8,32,128]{3,2,1,0:T(8,128)(2,1)S(1)} %collect_blocks.1.refs_1_), channel_id=1, source_target_pairs={{0,1},{1,0},{2,3},{3,2},{4,5},{5,4},{6,7},{7,6},{8,9},{9,8},{10,11... | collective-permute-start | bytes 786440 | tf_op jit(solution)/shard_map/ppermute | solution.py:317
  29.8 13.6 %collective-permute-start.3 = (bf16[1,16,32,128]{3,2,1,0:T(8,128)(2,1)S(1)}, bf16[1,16,32,128]{3,2,1,0:T(8,128)(2,1)S(1)}, u32[]{:S(2)}, u32[]{:S(2)}) collective-permute-start(bf16[1,16,32,128]{3,2,1,0:T(8,128)(2,1)S(1)} %get-tuple-element.40.refs_4_), channel_id=1, source_target_pairs={{0,1},{1,0},{2,3},{3,2},{4,5},{5,4},{6,7},{7,6},{8,9},{9,8},{10,11... | collective-permute-start | bytes 393224 | tf_op jit(solution)/shard_map/ppermute | solution.py:317
  32.2 11.2 %collective-permute-start.4 = (bf16[1,16,32,128]{3,2,1,0:T(8,128)(2,1)S(1)}, bf16[1,16,32,128]{3,2,1,0:T(8,128)(2,1)S(1)}, u32[]{:S(2)}, u32[]{:S(2)}) collective-permute-start(bf16[1,16,32,128]{3,2,1,0:T(8,128)(2,1)S(1)} %get-tuple-element.41.refs_6_), channel_id=1, source_target_pairs={{0,3},{1,2},{2,1},{3,0},{4,7},{5,6},{6,5},{7,4},{8,11},{9,10},{10,... | collective-permute-start | bytes 393224 | tf_op jit(solution)/shard_map/ppermute | solution.py:317
  32.7 19.6 %collective-permute-start.5 = (bf16[1,16,32,128]{3,2,1,0:T(8,128)(2,1)S(1)}, bf16[1,16,32,128]{3,2,1,0:T(8,128)(2,1)S(1)}, u32[]{:S(2)}, u32[]{:S(2)}) collective-permute-start(bf16[1,16,32,128]{3,2,1,0:T(8,128)(2,1)S(1)} %get-tuple-element.42.refs_1_), channel_id=1, source_target_pairs={{0,5},{1,4},{2,7},{3,6},{4,1},{5,0},{6,3},{7,2},{8,13},{9,12},{10,... | collective-permute-start | bytes 393224 | tf_op jit(solution)/shard_map/ppermute | solution.py:317
  36.4 17.6 %collective-permute-start.6 = (bf16[1,16,32,128]{3,2,1,0:T(8,128)(2,1)S(1)}, bf16[1,16,32,128]{3,2,1,0:T(8,128)(2,1)S(1)}, u32[]{:S(2)}, u32[]{:S(2)}) collective-permute-start(bf16[1,16,32,128]{3,2,1,0:T(8,128)(2,1)S(1)} %get-tuple-element.43.refs_3_), channel_id=1, source_target_pairs={{0,7},{1,6},{2,5},{3,4},{4,3},{5,2},{6,1},{7,0},{8,15},{9,14},{10,... | collective-permute-start | bytes 393224 | tf_op jit(solution)/shard_map/ppermute | solution.py:317
  43.4 23.5 %collective-permute-start.19 = (bf16[1,16,32,128]{3,2,1,0:T(8,128)(2,1)S(1)}, bf16[1,16,32,128]{3,2,1,0:T(8,128)(2,1)S(1)}, u32[]{:S(2)}, u32[]{:S(2)}) collective-permute-start(bf16[1,16,32,128]{3,2,1,0:T(8,128)(2,1)S(1)} %get-tuple-element.55), channel_id=1, source_target_pairs={{0,4},{1,5},{2,6},{3,7},{4,0},{5,1},{6,2},{7,3},{8,12},{9,13},{10,... | collective-permute-start | bytes 393224 | tf_op jit(solution)/shard_map/ppermute | solution.py:317
  43.4 23.6 %collective-permute-start.20 = (bf16[1,16,32,128]{3,2,1,0:T(8,128)(2,1)S(1)}, bf16[1,16,32,128]{3,2,1,0:T(8,128)(2,1)S(1)}, u32[]{:S(2)}, u32[]{:S(2)}) collective-permute-start(bf16[1,16,32,128]{3,2,1,0:T(8,128)(2,1)S(1)} %get-tuple-element.56), channel_id=1, source_target_pairs={{0,6},{1,7},{2,4},{3,5},{4,2},{5,3},{6,0},{7,1},{8,14},{9,15},{10,... | collective-permute-start | bytes 393224 | tf_op jit(solution)/shard_map/ppermute | solution.py:317
  52.3 17.8 %collective-permute-start.21 = (bf16[1,16,32,128]{3,2,1,0:T(8,128)(2,1)S(1)}, bf16[1,16,32,128]{3,2,1,0:T(8,128)(2,1)S(1)}, u32[]{:S(2)}, u32[]{:S(2)}) collective-permute-start(bf16[1,16,32,128]{3,2,1,0:T(8,128)(2,1)S(1)} %get-tuple-element.57), channel_id=1, source_target_pairs={{0,1},{1,0},{2,3},{3,2},{4,5},{5,4},{6,7},{7,6},{8,9},{9,8},{10,11... | collective-permute-start | bytes 393224 | tf_op jit(solution)/shard_map/ppermute | solution.py:317
  54.0 16.6 %collective-permute-start.23 = (bf16[1,16,32,128]{3,2,1,0:T(8,128)(2,1)S(1)}, bf16[1,16,32,128]{3,2,1,0:T(8,128)(2,1)S(1)}, u32[]{:S(2)}, u32[]{:S(2)}) collective-permute-start(bf16[1,16,32,128]{3,2,1,0:T(8,128)(2,1)S(1)} %get-tuple-element.59), channel_id=1, source_target_pairs={{0,5},{1,4},{2,7},{3,6},{4,1},{5,0},{6,3},{7,2},{8,13},{9,12},{10,... | collective-permute-start | bytes 393224 | tf_op jit(solution)/shard_map/ppermute | solution.py:317
  57.3 15.5 %collective-permute-start.24 = (bf16[1,16,32,128]{3,2,1,0:T(8,128)(2,1)S(1)}, bf16[1,16,32,128]{3,2,1,0:T(8,128)(2,1)S(1)}, u32[]{:S(2)}, u32[]{:S(2)}) collective-permute-start(bf16[1,16,32,128]{3,2,1,0:T(8,128)(2,1)S(1)} %get-tuple-element.60), channel_id=1, source_target_pairs={{0,7},{1,6},{2,5},{3,4},{4,3},{5,2},{6,1},{7,0},{8,15},{9,14},{10,... | collective-permute-start | bytes 393224 | tf_op jit(solution)/shard_map/ppermute | solution.py:317
  66.9 9.3 %collective-permute-start.22 = (bf16[1,16,32,128]{3,2,1,0:T(8,128)(2,1)S(1)}, bf16[1,16,32,128]{3,2,1,0:T(8,128)(2,1)S(1)}, u32[]{:S(2)}, u32[]{:S(2)}) collective-permute-start(bf16[1,16,32,128]{3,2,1,0:T(8,128)(2,1)S(1)} %send_blocks.5), channel_id=1, source_target_pairs={{0,3},{1,2},{2,1},{3,0},{4,7},{5,6},{6,5},{7,4},{8,11},{9,10},{10,... | collective-permute-start | bytes 393224 | tf_op jit(solution)/shard_map/ppermute | solution.py:317
  67.0 17.5 %collective-permute-start.11 = (bf16[2,32,1024]{2,1,0:T(8,128)(2,1)S(1)}, bf16[2,32,1024]{2,1,0:T(8,128)(2,1)S(1)}, u32[]{:S(2)}, u32[]{:S(2)}) collective-permute-start(bf16[2,32,1024]{2,1,0:T(8,128)(2,1)S(1)} %get-tuple-element.47), channel_id=1, source_target_pairs={{0,2},{1,3},{2,0},{3,1},{4,6},{5,7},{6,4},{7,5},{8,10},{9,11},{10,... | collective-permute-start | bytes 393224 | tf_op jit(solution)/shard_map/ppermute | solution.py:317
  70.1 17.2 %collective-permute-start.12 = (bf16[2,32,1024]{2,1,0:T(8,128)(2,1)S(1)}, bf16[2,32,1024]{2,1,0:T(8,128)(2,1)S(1)}, u32[]{:S(2)}, u32[]{:S(2)}) collective-permute-start(bf16[2,32,1024]{2,1,0:T(8,128)(2,1)S(1)} %get-tuple-element.48), channel_id=1, source_target_pairs={{0,4},{1,5},{2,6},{3,7},{4,0},{5,1},{6,2},{7,3},{8,12},{9,13},{10,... | collective-permute-start | bytes 393224 | tf_op jit(solution)/shard_map/ppermute | solution.py:317
  70.7 20.1 %collective-permute-start.13 = (bf16[2,32,1024]{2,1,0:T(8,128)(2,1)S(1)}, bf16[2,32,1024]{2,1,0:T(8,128)(2,1)S(1)}, u32[]{:S(2)}, u32[]{:S(2)}) collective-permute-start(bf16[2,32,1024]{2,1,0:T(8,128)(2,1)S(1)} %get-tuple-element.49), channel_id=1, source_target_pairs={{0,5},{1,4},{2,7},{3,6},{4,1},{5,0},{6,3},{7,2},{8,13},{9,12},{10,... | collective-permute-start | bytes 393224 | tf_op jit(solution)/shard_map/ppermute | solution.py:317
  72.8 17.9 %collective-permute-start.14 = (bf16[2,32,1024]{2,1,0:T(8,128)(2,1)S(1)}, bf16[2,32,1024]{2,1,0:T(8,128)(2,1)S(1)}, u32[]{:S(2)}, u32[]{:S(2)}) collective-permute-start(bf16[2,32,1024]{2,1,0:T(8,128)(2,1)S(1)} %get-tuple-element.50), channel_id=1, source_target_pairs={{0,6},{1,7},{2,4},{3,5},{4,2},{5,3},{6,0},{7,1},{8,14},{9,15},{10,... | collective-permute-start | bytes 393224 | tf_op jit(solution)/shard_map/ppermute | solution.py:317
  76.2 17.0 %collective-permute-start.15 = (bf16[2,32,1024]{2,1,0:T(8,128)(2,1)S(1)}, bf16[2,32,1024]{2,1,0:T(8,128)(2,1)S(1)}, u32[]{:S(2)}, u32[]{:S(2)}) collective-permute-start(bf16[2,32,1024]{2,1,0:T(8,128)(2,1)S(1)} %get-tuple-element.51), channel_id=1, source_target_pairs={{0,7},{1,6},{2,5},{3,4},{4,3},{5,2},{6,1},{7,0},{8,15},{9,14},{10,... | collective-permute-start | bytes 393224 | tf_op jit(solution)/shard_map/ppermute | solution.py:317
  77.8 35.7 %copy-start.3 = (bf16[8,512,512]{2,1,0:T(8,128)(2,1)S(1)}, bf16[8,512,512]{2,1,0:T(8,128)(2,1)}, u32[]{:S(2)}) copy-start(bf16[8,512,512]{2,1,0:T(8,128)(2,1)} %constant.20.clone.refs_17_) | copy-start | bytes 12582916
  84.5 13.8 %collective-permute-start.16 = (bf16[2,32,1024]{2,1,0:T(8,128)(2,1)S(1)}, bf16[2,32,1024]{2,1,0:T(8,128)(2,1)S(1)}, u32[]{:S(2)}, u32[]{:S(2)}) collective-permute-start(bf16[2,32,1024]{2,1,0:T(8,128)(2,1)S(1)} %get-tuple-element.52), channel_id=1, source_target_pairs={{0,3},{1,2},{2,1},{3,0},{4,7},{5,6},{6,5},{7,4},{8,11},{9,10},{10,... | collective-permute-start | bytes 393224 | tf_op jit(solution)/shard_map/ppermute | solution.py:317
  87.3 15.1 %collective-permute-start.17 = (bf16[2,32,1024]{2,1,0:T(8,128)(2,1)S(1)}, bf16[2,32,1024]{2,1,0:T(8,128)(2,1)S(1)}, u32[]{:S(2)}, u32[]{:S(2)}) collective-permute-start(bf16[2,32,1024]{2,1,0:T(8,128)(2,1)S(1)} %get-tuple-element.53), channel_id=1, source_target_pairs={{0,1},{1,0},{2,3},{3,2},{4,5},{5,4},{6,7},{7,6},{8,9},{9,8},{10,11... | collective-permute-start | bytes 393224 | tf_op jit(solution)/shard_map/ppermute | solution.py:317
  90.7 12.3 %collective-permute-start.25 = (bf16[2,32,1024]{2,1,0:T(8,128)(2,1)S(1)}, bf16[2,32,1024]{2,1,0:T(8,128)(2,1)S(1)}, u32[]{:S(2)}, u32[]{:S(2)}) collective-permute-start(bf16[2,32,1024]{2,1,0:T(8,128)(2,1)S(1)} %get-tuple-element.62), channel_id=1, source_target_pairs={{0,2},{1,3},{2,0},{3,1},{4,6},{5,7},{6,4},{7,5},{8,10},{9,11},{10,... | collective-permute-start | bytes 393224 | tf_op jit(solution)/shard_map/ppermute | solution.py:317
  90.7 14.7 %collective-permute-start.26 = (bf16[2,32,1024]{2,1,0:T(8,128)(2,1)S(1)}, bf16[2,32,1024]{2,1,0:T(8,128)(2,1)S(1)}, u32[]{:S(2)}, u32[]{:S(2)}) collective-permute-start(bf16[2,32,1024]{2,1,0:T(8,128)(2,1)S(1)} %get-tuple-element.63), channel_id=1, source_target_pairs={{0,4},{1,5},{2,6},{3,7},{4,0},{5,1},{6,2},{7,3},{8,12},{9,13},{10,... | collective-permute-start | bytes 393224 | tf_op jit(solution)/shard_map/ppermute | solution.py:317
  93.2 18.7 %collective-permute-start.27 = (bf16[2,32,1024]{2,1,0:T(8,128)(2,1)S(1)}, bf16[2,32,1024]{2,1,0:T(8,128)(2,1)S(1)}, u32[]{:S(2)}, u32[]{:S(2)}) collective-permute-start(bf16[2,32,1024]{2,1,0:T(8,128)(2,1)S(1)} %get-tuple-element.64), channel_id=1, source_target_pairs={{0,5},{1,4},{2,7},{3,6},{4,1},{5,0},{6,3},{7,2},{8,13},{9,12},{10,... | collective-permute-start | bytes 393224 | tf_op jit(solution)/shard_map/ppermute | solution.py:317
  98.3 13.6 %collective-permute-start.28 = (bf16[2,32,1024]{2,1,0:T(8,128)(2,1)S(1)}, bf16[2,32,1024]{2,1,0:T(8,128)(2,1)S(1)}, u32[]{:S(2)}, u32[]{:S(2)}) collective-permute-start(bf16[2,32,1024]{2,1,0:T(8,128)(2,1)S(1)} %get-tuple-element.65), channel_id=1, source_target_pairs={{0,6},{1,7},{2,4},{3,5},{4,2},{5,3},{6,0},{7,1},{8,14},{9,15},{10,... | collective-permute-start | bytes 393224 | tf_op jit(solution)/shard_map/ppermute | solution.py:317
  102.4 9.5 %collective-permute-start.29 = (bf16[2,32,1024]{2,1,0:T(8,128)(2,1)S(1)}, bf16[2,32,1024]{2,1,0:T(8,128)(2,1)S(1)}, u32[]{:S(2)}, u32[]{:S(2)}) collective-permute-start(bf16[2,32,1024]{2,1,0:T(8,128)(2,1)S(1)} %get-tuple-element.66), channel_id=1, source_target_pairs={{0,7},{1,6},{2,5},{3,4},{4,3},{5,2},{6,1},{7,0},{8,15},{9,14},{10,... | collective-permute-start | bytes 393224 | tf_op jit(solution)/shard_map/ppermute | solution.py:317
  103.0 9.1 %collective-permute-start.30 = (bf16[2,32,1024]{2,1,0:T(8,128)(2,1)S(1)}, bf16[2,32,1024]{2,1,0:T(8,128)(2,1)S(1)}, u32[]{:S(2)}, u32[]{:S(2)}) collective-permute-start(bf16[2,32,1024]{2,1,0:T(8,128)(2,1)S(1)} %get-tuple-element.67), channel_id=1, source_target_pairs={{0,3},{1,2},{2,1},{3,0},{4,7},{5,6},{6,5},{7,4},{8,11},{9,10},{10,... | collective-permute-start | bytes 393224 | tf_op jit(solution)/shard_map/ppermute | solution.py:317
  105.4 8.0 %collective-permute-start.31 = (bf16[2,32,1024]{2,1,0:T(8,128)(2,1)S(1)}, bf16[2,32,1024]{2,1,0:T(8,128)(2,1)S(1)}, u32[]{:S(2)}, u32[]{:S(2)}) collective-permute-start(bf16[2,32,1024]{2,1,0:T(8,128)(2,1)S(1)} %get-tuple-element.68), channel_id=1, source_target_pairs={{0,1},{1,0},{2,3},{3,2},{4,5},{5,4},{6,7},{7,6},{8,9},{9,8},{10,11... | collective-permute-start | bytes 393224 | tf_op jit(solution)/shard_map/ppermute | solution.py:317

commit v4 on v3

--- a/solution.py
+++ b/solution.py
@@ -79,7 +79,7 @@
             tile = tiles_ref[lax.shift_right_logical(point, 7)].astype(F32)
             return jnp.where(lane == m, pltpu.roll(tile, (m - point) & (LANES - 1), 1), total)
 
-        total = lax.fori_loop(0, LANES, step, jnp.zeros((rows, LANES), F32), unroll=32)
+        total = lax.fori_loop(0, LANES, step, jnp.zeros((rows, LANES), F32), unroll=128)
         out_ref[group] = total.astype(BF16)
 
 
@@ -328,9 +328,9 @@
     plane_tiles = GY * GZ // LANES
     chunk_tiles = chunk_planes * plane_tiles
 
-    order = list(range(0, count, 2)) + list(range(1, count, 2))
     far = count // 2
-    order_back = [0, 2] + list(range(far, count)) + [k for k in range(far - 1, 0, -1) if k != 2]
+    order = list(dict.fromkeys(k for k in [0, far, 2, 1, far + 1, far + 2, *range(count)] if k < count))
+    order_back = list(dict.fromkeys(k for k in [0, 2, *range(far, count), *range(far - 1, 0, -1)] if k < count))
 
     tiles = orbitals.reshape(1, bands, 2, all_cells // LANES, LANES).transpose(0, 3, 1, 2, 4)
     tiles = lax.optimization_barrier(tiles.reshape(all_cells // LANES, rows, LANES))
@@ -345,7 +345,7 @@
     def blocks_for(c, distances, me):
         return send_blocks(me, blocks, [lambda me, d=d: (me ^ d) * chunks + c for d in distances])
 
-    distances = list(range(count // 2, count)) + list(range(1, count // 2))
+    distances = list(range(far, count)) + list(range(1, far))
     late = distances[len(distances) - 1 :]
     sends = [blocks_for(c, [d for d in distances if c == 0 or d not in late], device) for c in range(chunks)]
     own_values = pick(tiles, points, sends[0])
@@ -362,7 +362,6 @@
 
     received = []
     for c in range(chunks):
-        distances = list(range(count // 2, count)) + list(range(1, count // 2))
         arrived = {
             d: hop(block, d, count)
             for d, block in zip([d for d in distances if c == 0 or d not in late], sends[c])
@@ -383,7 +382,7 @@
             [(at, None) for at in range(count)],
         )
         back = {0: sent[0]}
-        for k in list(range(count // 2, count)) + list(range(1, count // 2)):
+        for k in distances:
             back[k] = hop(sent[order.index(k)], k, count)
         fields += [(back[k][None], first) for k in order_back]
 

time: 118 us -> 116 us (0.983)
  starting transfers between devices: 56.2 us -> 53.2 us
  waiting for transfers between devices: 26.7 us -> 29.5 us
    ppermute x32, starting transfers between devices: 56.2 us -> 53.2 us  [hop(): lax.ppermute(array, 'band', [(i, i ^ distance) for i in range(count)])]
    ppermute x32, waiting for transfers between devices: 26.7 us -> 29.5 us  [hop(): lax.ppermute(array, 'band', [(i, i ^ distance) for i in range(count)])]
where the time goes in v4:
time: 116 us
  starting transfers between devices  53.2 us (46%)
  waiting for transfers between devices  29.5 us (25%)
  Pallas kernels  23.1 us (20%)
  blocking collectives  6.61 us (6%)
  local copies, waits for them, and re-layouts  3.06 us (3%)
    ppermute x32, starting transfers between devices, hop(): lax.ppermute(array, 'band', [(i, i ^ distance) for i in range(count)])  53.2 us
    ppermute x32, waiting for transfers between devices, hop(): lax.ppermute(array, 'band', [(i, i ^ distance) for i in range(count)])  29.5 us
    pallas_call x2, Pallas kernels, exchange(): pl.pallas_call(lambda *refs: exchange_kernel(first_plane, planes, places,...  13.4 us
    all_gather x1, blocking collectives, body(): everyone = lax.all_gather(own_values, 'kgrp', axis=0, tiled=False)  6.61 us
    pallas_call x1, Pallas kernels, line_pass(): pl.pallas_call(lambda *refs: line_kernel(factor, group_rows, count, *refs...  3.49 us
    pallas_call x3, Pallas kernels, send_blocks(): pl.pallas_call(lambda *refs: send_kernel(leads, *refs), in_specs=[pl.Bloc...  3.13 us
  transfers between devices with their start and end apart: 32, of which 11 were waited for; matrix products, arithmetic and copies ran while one was open for 0% of the time, Pallas kernels for 14%

profile of v4, /device:TPU:0, one launch (start us, length us, event | category | flops | bytes accessed | tf_op | source)
XLA Modules:
  0.0 115.7 jit_solution(11381415146903883860)
XLA Ops:
  0.0 1.6 %copy-done = bf16[1,16,2,32768]{3,2,1,0:T(2,128)(2,1)S(1)} copy-done((bf16[1,16,2,32768]{3,2,1,0:T(2,128)(2,1)S(1)}, bf16[1,16,2,32768]{3,2,1,0:T(2,128)(2,1)}, u32[]{:S(2)}) %copy-start) | copy-done | bytes 2097176
  1.6 1.4 %copy_bitcast_fusion = bf16[1,16,2,256,128]{4,2,1,3,0:T(2,128)(2,1)S(1)} fusion(bf16[1,16,2,32768]{3,2,1,0:T(2,128)(2,1)S(1)} %copy-done), kind=kLoop, calls=%fused_computation | loop fusion | bytes 4194304 | tf_op jit(solution)/shard_map/reshape | solution.py:335
  3.0 1.3 %send_blocks.3 = (bf16[1,16,32,128]{3,2,1,0:T(8,128)(2,1)S(1)}, bf16[1,16,32,128]{3,2,1,0:T(8,128)(2,1)S(1)}, bf16[1,16,32,128]{3,2,1,0:T(8,128)(2,1)S(1)}, bf16...) custom-call(s32[1]{0:T(128)} %bitcast.refs_0_, ...), custom_call_target="tpu_custom_call" | custom-call | flops 1 | bytes 1 | tf_op jit(solution)/shard_map/send_blocks/pallas_call | solution.py:237
  4.4 2.0 %pick_points.1 = bf16[4,32,128]{2,1,0:T(8,128)(2,1)S(1)} custom-call(s32[512]{0:T(512)S(1)} %copy-done.5, bf16[256,32,128]{2,1,0:T(8,128)(2,1)S(1)} %bitcast.35, bf16[1,16,32,128]{3,2,1,0:T(8,128)(2,1)S(1)} %get-tuple-element.37.refs_0_, bf16[1,16,32,128]{3,2,1,0:T(8,128)(2,1)S(1)} %get-tuple-element.40.refs_1_, ...), custom_call_target="tpu_custom_call" | custom-call | tf_op jit(solution)/shard_map/pick_points/pallas_call | solution.py:89
  6.3 6.6 %all-gather = bf16[16,32,128]{2,1,0:T(8,128)(2,1)S(1)} all-gather(bf16[4,32,128]{2,1,0:T(8,128)(2,1)S(1)} %pick_points.1), channel_id=2, replica_groups=mesh['kgrp'=4,'band'=8] {'kgrp'}, dimensions={0}, use_global_device_ids=true | all-gather | bytes 163840 | tf_op jit(solution)/shard_map/all_gather | solution.py:352
  13.1 4.1 %collective-permute-start.9 = (bf16[1,8,32,128]{3,2,1,0:T(8,128)(2,1)S(1)}, bf16[1,8,32,128]{3,2,1,0:T(8,128)(2,1)S(1)}, u32[]{:S(2)}, u32[]{:S(2)}) collective-permute-start(bf16[1,8,32,128]{3,2,1,0:T(8,128)(2,1)S(1)} %maximum_bitcast_fusion.refs_1_), channel_id=1, source_target_pairs={{0,6},{1,7},{2,4},{3,5},{4,2},{5,3},{6,0},{7,1},{8,14},{9,15},{10,... | collective-permute-start | bytes 196616 | tf_op jit(solution)/shard_map/ppermute | solution.py:317
  17.1 0.6 collective-permute-start.7
  17.8 1.0 send_blocks.4
  18.8 2.4 %collective-permute-start.18 = (bf16[1,16,32,128]{3,2,1,0:T(8,128)(2,1)S(1)}, bf16[1,16,32,128]{3,2,1,0:T(8,128)(2,1)S(1)}, u32[]{:S(2)}, u32[]{:S(2)}) collective-permute-start(bf16[1,16,32,128]{3,2,1,0:T(8,128)(2,1)S(1)} %get-tuple-element.54), channel_id=1, source_target_pairs={{0,4},{1,5},{2,6},{3,7},{4,0},{5,1},{6,2},{7,3},{8,12},{9,13},{10,... | collective-permute-start | bytes 393224 | tf_op jit(solution)/shard_map/ppermute | solution.py:317
  21.2 0.6 collective-permute-start
  21.8 1.5 %collective-permute-start.1 = (bf16[1,16,32,128]{3,2,1,0:T(8,128)(2,1)S(1)}, bf16[1,16,32,128]{3,2,1,0:T(8,128)(2,1)S(1)}, u32[]{:S(2)}, u32[]{:S(2)}) collective-permute-start(bf16[1,16,32,128]{3,2,1,0:T(8,128)(2,1)S(1)} %get-tuple-element.38.refs_5_), channel_id=1, source_target_pairs={{0,2},{1,3},{2,0},{3,1},{4,6},{5,7},{6,4},{7,5},{8,10},{9,11},{10,... | collective-permute-start | bytes 393224 | tf_op jit(solution)/shard_map/ppermute | solution.py:317
  23.3 0.8 collective-permute-done.8.refs_3_
  24.1 1.5 %collective-permute-start.2 = (bf16[1,16,32,128]{3,2,1,0:T(8,128)(2,1)S(1)}, bf16[1,16,32,128]{3,2,1,0:T(8,128)(2,1)S(1)}, u32[]{:S(2)}, u32[]{:S(2)}) collective-permute-start(bf16[1,16,32,128]{3,2,1,0:T(8,128)(2,1)S(1)} %get-tuple-element.39.refs_4_), channel_id=1, source_target_pairs={{0,1},{1,0},{2,3},{3,2},{4,5},{5,4},{6,7},{7,6},{8,9},{9,8},{10,11... | collective-permute-start | bytes 393224 | tf_op jit(solution)/shard_map/ppermute | solution.py:317
  25.6 0.7 collect_blocks.1.refs_1_
  26.3 0.6 collective-permute-start.10
  26.9 5.0 %collective-permute-done.18.refs_2_ = bf16[1,16,32,128]{3,2,1,0:T(8,128)(2,1)S(1)} collective-permute-done((bf16[1,16,32,128]{3,2,1,0:T(8,128)(2,1)S(1)}, bf16[1,16,32,128]{3,2,1,0:T(8,128)(2,1)S(1)}, u32[]{:S(2)}, u32[]{:S(2)}) %collective-permute-start.18) | collective-permute-done | bytes 131104 | tf_op jit(solution)/shard_map/ppermute | solution.py:317
  31.9 0.5 collective-permute-start.3
  32.4 1.9 %collective-permute-done.refs_2_ = bf16[1,16,32,128]{3,2,1,0:T(8,128)(2,1)S(1)} collective-permute-done((bf16[1,16,32,128]{3,2,1,0:T(8,128)(2,1)S(1)}, bf16[1,16,32,128]{3,2,1,0:T(8,128)(2,1)S(1)}, u32[]{:S(2)}, u32[]{:S(2)}) %collective-permute-start) | collective-permute-done | bytes 131104 | tf_op jit(solution)/shard_map/ppermute | solution.py:317
  34.3 5.7 %collective-permute-start.4 = (bf16[1,16,32,128]{3,2,1,0:T(8,128)(2,1)S(1)}, bf16[1,16,32,128]{3,2,1,0:T(8,128)(2,1)S(1)}, u32[]{:S(2)}, u32[]{:S(2)}) collective-permute-start(bf16[1,16,32,128]{3,2,1,0:T(8,128)(2,1)S(1)} %get-tuple-element.41.refs_2_), channel_id=1, source_target_pairs={{0,6},{1,7},{2,4},{3,5},{4,2},{5,3},{6,0},{7,1},{8,14},{9,15},{10,... | collective-permute-start | bytes 393224 | tf_op jit(solution)/shard_map/ppermute | solution.py:317
  40.0 1.2 %collective-permute-start.6 = (bf16[1,16,32,128]{3,2,1,0:T(8,128)(2,1)S(1)}, bf16[1,16,32,128]{3,2,1,0:T(8,128)(2,1)S(1)}, u32[]{:S(2)}, u32[]{:S(2)}) collective-permute-start(bf16[1,16,32,128]{3,2,1,0:T(8,128)(2,1)S(1)} %get-tuple-element.43.refs_3_), channel_id=1, source_target_pairs={{0,7},{1,6},{2,5},{3,4},{4,3},{5,2},{6,1},{7,0},{8,15},{9,14},{10,... | collective-permute-start | bytes 393224 | tf_op jit(solution)/shard_map/ppermute | solution.py:317
  41.3 1.5 %collective-permute-done.3.refs_5_ = bf16[1,16,32,128]{3,2,1,0:T(8,128)(2,1)S(1)} collective-permute-done((bf16[1,16,32,128]{3,2,1,0:T(8,128)(2,1)S(1)}, bf16[1,16,32,128]{3,2,1,0:T(8,128)(2,1)S(1)}, u32[]{:S(2)}, u32[]{:S(2)}) %collective-permute-start.3) | collective-permute-done | bytes 131104 | tf_op jit(solution)/shard_map/ppermute | solution.py:317
  42.8 0.5 collective-permute-start.19
  43.3 0.7 collective-permute-done.4.refs_6_
  44.0 2.2 %collective-permute-start.20 = (bf16[1,16,32,128]{3,2,1,0:T(8,128)(2,1)S(1)}, bf16[1,16,32,128]{3,2,1,0:T(8,128)(2,1)S(1)}, u32[]{:S(2)}, u32[]{:S(2)}) collective-permute-start(bf16[1,16,32,128]{3,2,1,0:T(8,128)(2,1)S(1)} %get-tuple-element.56), channel_id=1, source_target_pairs={{0,1},{1,0},{2,3},{3,2},{4,5},{5,4},{6,7},{7,6},{8,9},{9,8},{10,11... | collective-permute-start | bytes 393224 | tf_op jit(solution)/shard_map/ppermute | solution.py:317
  46.2 4.0 %collective-permute-done.5.refs_7_ = bf16[1,16,32,128]{3,2,1,0:T(8,128)(2,1)S(1)} collective-permute-done((bf16[1,16,32,128]{3,2,1,0:T(8,128)(2,1)S(1)}, bf16[1,16,32,128]{3,2,1,0:T(8,128)(2,1)S(1)}, u32[]{:S(2)}, u32[]{:S(2)}) %collective-permute-start.5) | collective-permute-done | bytes 131104 | tf_op jit(solution)/shard_map/ppermute | solution.py:317
  50.2 0.3 collective-permute-start.21
  50.5 0.5 collective-permute-done.6.refs_8_
  51.0 4.2 %collective-permute-start.22 = (bf16[1,16,32,128]{3,2,1,0:T(8,128)(2,1)S(1)}, bf16[1,16,32,128]{3,2,1,0:T(8,128)(2,1)S(1)}, u32[]{:S(2)}, u32[]{:S(2)}) collective-permute-start(bf16[1,16,32,128]{3,2,1,0:T(8,128)(2,1)S(1)} %get-tuple-element.58), channel_id=1, source_target_pairs={{0,6},{1,7},{2,4},{3,5},{4,2},{5,3},{6,0},{7,1},{8,14},{9,15},{10,... | collective-permute-start | bytes 393224 | tf_op jit(solution)/shard_map/ppermute | solution.py:317
  55.4 0.3 coefficients.1
  55.8 6.7 %exchange_planes.2 = (bf16[2,32,1024]{2,1,0:T(8,128)(2,1)S(1)}, bf16[2,32,1024]{2,1,0:T(8,128)(2,1)S(1)}, bf16[2,32,1024]{2,1,0:T(8,128)(2,1)S(1)}, bf16[2,32,10...) custom-call(s32[1]{0:T(128)} %bitcast.refs_0_, ...), custom_call_target="tpu_custom_call" | custom-call | flops 1 | bytes 1 | tf_op jit(solution)/shard_map/exchange_planes/pallas_call | solution.py:181
  62.5 0.8 send_blocks.5
  63.3 7.8 %collective-permute-start.23 = (bf16[1,16,32,128]{3,2,1,0:T(8,128)(2,1)S(1)}, bf16[1,16,32,128]{3,2,1,0:T(8,128)(2,1)S(1)}, u32[]{:S(2)}, u32[]{:S(2)}) collective-permute-start(bf16[1,16,32,128]{3,2,1,0:T(8,128)(2,1)S(1)} %send_blocks.5), channel_id=1, source_target_pairs={{0,3},{1,2},{2,1},{3,0},{4,7},{5,6},{6,5},{7,4},{8,11},{9,10},{10,... | collective-permute-start | bytes 393224 | tf_op jit(solution)/shard_map/ppermute | solution.py:317
  71.1 1.5 %collective-permute-start.12 = (bf16[2,32,1024]{2,1,0:T(8,128)(2,1)S(1)}, bf16[2,32,1024]{2,1,0:T(8,128)(2,1)S(1)}, u32[]{:S(2)}, u32[]{:S(2)}) collective-permute-start(bf16[2,32,1024]{2,1,0:T(8,128)(2,1)S(1)} %get-tuple-element.48), channel_id=1, source_target_pairs={{0,4},{1,5},{2,6},{3,7},{4,0},{5,1},{6,2},{7,3},{8,12},{9,13},{10,... | collective-permute-start | bytes 393224 | tf_op jit(solution)/shard_map/ppermute | solution.py:317
  72.6 1.5 %collective-permute-start.13 = (bf16[2,32,1024]{2,1,0:T(8,128)(2,1)S(1)}, bf16[2,32,1024]{2,1,0:T(8,128)(2,1)S(1)}, u32[]{:S(2)}, u32[]{:S(2)}) collective-permute-start(bf16[2,32,1024]{2,1,0:T(8,128)(2,1)S(1)} %get-tuple-element.49), channel_id=1, source_target_pairs={{0,5},{1,4},{2,7},{3,6},{4,1},{5,0},{6,3},{7,2},{8,13},{9,12},{10,... | collective-permute-start | bytes 393224 | tf_op jit(solution)/shard_map/ppermute | solution.py:317
  74.1 1.4 %collective-permute-start.14 = (bf16[2,32,1024]{2,1,0:T(8,128)(2,1)S(1)}, bf16[2,32,1024]{2,1,0:T(8,128)(2,1)S(1)}, u32[]{:S(2)}, u32[]{:S(2)}) collective-permute-start(bf16[2,32,1024]{2,1,0:T(8,128)(2,1)S(1)} %get-tuple-element.50), channel_id=1, source_target_pairs={{0,6},{1,7},{2,4},{3,5},{4,2},{5,3},{6,0},{7,1},{8,14},{9,15},{10,... | collective-permute-start | bytes 393224 | tf_op jit(solution)/shard_map/ppermute | solution.py:317
  75.6 3.4 %collective-permute-done.23.refs_7_ = bf16[1,16,32,128]{3,2,1,0:T(8,128)(2,1)S(1)} collective-permute-done((bf16[1,16,32,128]{3,2,1,0:T(8,128)(2,1)S(1)}, bf16[1,16,32,128]{3,2,1,0:T(8,128)(2,1)S(1)}, u32[]{:S(2)}, u32[]{:S(2)}) %collective-permute-start.23) | collective-permute-done | bytes 131104 | tf_op jit(solution)/shard_map/ppermute | solution.py:317
  78.9 2.2 %collective-permute-start.15 = (bf16[2,32,1024]{2,1,0:T(8,128)(2,1)S(1)}, bf16[2,32,1024]{2,1,0:T(8,128)(2,1)S(1)}, u32[]{:S(2)}, u32[]{:S(2)}) collective-permute-start(bf16[2,32,1024]{2,1,0:T(8,128)(2,1)S(1)} %get-tuple-element.51), channel_id=1, source_target_pairs={{0,7},{1,6},{2,5},{3,4},{4,3},{5,2},{6,1},{7,0},{8,15},{9,14},{10,... | collective-permute-start | bytes 393224 | tf_op jit(solution)/shard_map/ppermute | solution.py:317
  81.1 6.7 %exchange_planes.3 = (bf16[2,32,1024]{2,1,0:T(8,128)(2,1)S(1)}, bf16[2,32,1024]{2,1,0:T(8,128)(2,1)S(1)}, bf16[2,32,1024]{2,1,0:T(8,128)(2,1)S(1)}, bf16[2,32,10...) custom-call(s32[1]{0:T(128)} %bitcast.refs_0_, ...), custom_call_target="tpu_custom_call" | custom-call | flops 1 | bytes 1 | tf_op jit(solution)/shard_map/exchange_planes/pallas_call | solution.py:181
  88.0 3.4 %collective-permute-start.25 = (bf16[2,32,1024]{2,1,0:T(8,128)(2,1)S(1)}, bf16[2,32,1024]{2,1,0:T(8,128)(2,1)S(1)}, u32[]{:S(2)}, u32[]{:S(2)}) collective-permute-start(bf16[2,32,1024]{2,1,0:T(8,128)(2,1)S(1)} %get-tuple-element.62), channel_id=1, source_target_pairs={{0,2},{1,3},{2,0},{3,1},{4,6},{5,7},{6,4},{7,5},{8,10},{9,11},{10,... | collective-permute-start | bytes 393224 | tf_op jit(solution)/shard_map/ppermute | solution.py:317
  91.4 0.3 collective-permute-start.26
  91.7 3.6 %collective-permute-start.27 = (bf16[2,32,1024]{2,1,0:T(8,128)(2,1)S(1)}, bf16[2,32,1024]{2,1,0:T(8,128)(2,1)S(1)}, u32[]{:S(2)}, u32[]{:S(2)}) collective-permute-start(bf16[2,32,1024]{2,1,0:T(8,128)(2,1)S(1)} %get-tuple-element.64), channel_id=1, source_target_pairs={{0,5},{1,4},{2,7},{3,6},{4,1},{5,0},{6,3},{7,2},{8,13},{9,12},{10,... | collective-permute-start | bytes 393224 | tf_op jit(solution)/shard_map/ppermute | solution.py:317
  95.3 3.1 %collective-permute-start.28 = (bf16[2,32,1024]{2,1,0:T(8,128)(2,1)S(1)}, bf16[2,32,1024]{2,1,0:T(8,128)(2,1)S(1)}, u32[]{:S(2)}, u32[]{:S(2)}) collective-permute-start(bf16[2,32,1024]{2,1,0:T(8,128)(2,1)S(1)} %get-tuple-element.65), channel_id=1, source_target_pairs={{0,6},{1,7},{2,4},{3,5},{4,2},{5,3},{6,0},{7,1},{8,14},{9,15},{10,... | collective-permute-start | bytes 393224 | tf_op jit(solution)/shard_map/ppermute | solution.py:317
  98.4 1.6 %collective-permute-start.29 = (bf16[2,32,1024]{2,1,0:T(8,128)(2,1)S(1)}, bf16[2,32,1024]{2,1,0:T(8,128)(2,1)S(1)}, u32[]{:S(2)}, u32[]{:S(2)}) collective-permute-start(bf16[2,32,1024]{2,1,0:T(8,128)(2,1)S(1)} %get-tuple-element.66), channel_id=1, source_target_pairs={{0,7},{1,6},{2,5},{3,4},{4,3},{5,2},{6,1},{7,0},{8,15},{9,14},{10,... | collective-permute-start | bytes 393224 | tf_op jit(solution)/shard_map/ppermute | solution.py:317
  100.0 7.2 %collective-permute-done.26 = bf16[2,32,1024]{2,1,0:T(8,128)(2,1)S(1)} collective-permute-done((bf16[2,32,1024]{2,1,0:T(8,128)(2,1)S(1)}, bf16[2,32,1024]{2,1,0:T(8,128)(2,1)S(1)}, u32[]{:S(2)}, u32[]{:S(2)}) %collective-permute-start.26) | collective-permute-done | bytes 131104 | tf_op jit(solution)/shard_map/ppermute | solution.py:317
  107.2 0.5 collective-permute-start.31
  107.7 2.2 %collective-permute-done.27 = bf16[2,32,1024]{2,1,0:T(8,128)(2,1)S(1)} collective-permute-done((bf16[2,32,1024]{2,1,0:T(8,128)(2,1)S(1)}, bf16[2,32,1024]{2,1,0:T(8,128)(2,1)S(1)}, u32[]{:S(2)}, u32[]{:S(2)}) %collective-permute-start.27) | collective-permute-done | bytes 131104 | tf_op jit(solution)/shard_map/ppermute | solution.py:317
  110.0 2.2 %collective-permute-done.31 = bf16[2,32,1024]{2,1,0:T(8,128)(2,1)S(1)} collective-permute-done((bf16[2,32,1024]{2,1,0:T(8,128)(2,1)S(1)}, bf16[2,32,1024]{2,1,0:T(8,128)(2,1)S(1)}, u32[]{:S(2)}, u32[]{:S(2)}) %collective-permute-start.31) | collective-permute-done | bytes 131104 | tf_op jit(solution)/shard_map/ppermute | solution.py:317
  112.2 3.5 %line_pass.1 = bf16[512,8,2,128]{3,2,1,0:T(2,128)(2,1)} custom-call(s32[1]{0:T(128)} %bitcast.refs_0_, bf16[1,2,32,1024]{3,2,1,0:T(8,128)(2,1)S(1)} %bitcast.40, bf16[1,2,32,1024]{3,2,1,0:T(8,128)(2,1)S(1)} %bitcast.41, bf16[1,2,32,1024]{3,2,1,0:T(8,128)(2,1)S(1)} %bitcast.42, bf16[1,2,32,1024]{3,2,1,0:T(8,128)(2,1)S(1)} %bitcast.43, ...), custom_call_target="tpu_custom_call" | custom-call | flops 1 | bytes 1 | tf_op jit(solution)/shard_map/line_pass/pallas_call | solution.py:306
  (44 shorter events, 0.6 us)
Async XLA Ops:
  0.0 1.6 %copy-start = (bf16[1,16,2,32768]{3,2,1,0:T(2,128)(2,1)S(1)}, bf16[1,16,2,32768]{3,2,1,0:T(2,128)(2,1)}, u32[]{:S(2)}) copy-start(bf16[1,16,2,32768]{3,2,1,0:T(2,128)(2,1)} %param.7) | copy-start | bytes 6291460
  1.6 53.8 %copy-start.2 = (bf16[2,1024,1024]{2,1,0:T(8,128)(2,1)S(1)}, bf16[2,1024,1024]{2,1,0:T(8,128)(2,1)}, u32[]{:S(2)}) copy-start(bf16[2,1024,1024]{2,1,0:T(8,128)(2,1)} %constant.19.clone.refs_5_.refs_12_) | copy-start | bytes 12582916
  3.0 1.3 %copy-start.5 = (s32[512]{0:T(512)S(1)}, s32[512]{0:T(512)}, u32[]{:S(2)}) copy-start(s32[512]{0:T(512)} %points_ref.1) | copy-start | bytes 6148
  4.3 8.6 %copy-start.6 = (s32[4]{0:T(128)S(1)}, s32[4]{0:T(128)}, u32[]{:S(2)}) copy-start(s32[4]{0:T(128)} %param.9) | copy-start | bytes 52
  4.3 51.1 %copy-start.1 = (bf16[512,4096]{1,0:T(8,128)(2,1)S(1)}, bf16[512,4096]{1,0:T(8,128)(2,1)}, u32[]{:S(2)}) copy-start(bf16[512,4096]{1,0:T(8,128)(2,1)} %refs_11_.3) | copy-start | bytes 12582916
  6.3 49.1 %copy-start.4 = (bf16[256,256]{1,0:T(8,128)(2,1)S(1)}, bf16[256,256]{1,0:T(8,128)(2,1)}, u32[]{:S(2)}) copy-start(bf16[256,256]{1,0:T(8,128)(2,1)} %constant.18.clone.refs_3_.refs_13_) | copy-start | bytes 393220
  13.1 8.7 %collective-permute-start.9 = (bf16[1,8,32,128]{3,2,1,0:T(8,128)(2,1)S(1)}, bf16[1,8,32,128]{3,2,1,0:T(8,128)(2,1)S(1)}, u32[]{:S(2)}, u32[]{:S(2)}) collective-permute-start(bf16[1,8,32,128]{3,2,1,0:T(8,128)(2,1)S(1)} %maximum_bitcast_fusion.refs_1_), channel_id=1, source_target_pairs={{0,6},{1,7},{2,4},{3,5},{4,2},{5,3},{6,0},{7,1},{8,14},{9,15},{10,... | collective-permute-start | bytes 196616 | tf_op jit(solution)/shard_map/ppermute | solution.py:317
  17.1 6.9 %collective-permute-start.8 = (bf16[1,8,32,128]{3,2,1,0:T(8,128)(2,1)S(1)}, bf16[1,8,32,128]{3,2,1,0:T(8,128)(2,1)S(1)}, u32[]{:S(2)}, u32[]{:S(2)}) collective-permute-start(bf16[1,8,32,128]{3,2,1,0:T(8,128)(2,1)S(1)} %maximum_bitcast_fusion.refs_1_), channel_id=1, source_target_pairs={{0,4},{1,5},{2,6},{3,7},{4,0},{5,1},{6,2},{7,3},{8,12},{9,13},{10,... | collective-permute-start | bytes 196616 | tf_op jit(solution)/shard_map/ppermute | solution.py:317
  17.1 8.4 %collective-permute-start.7 = (bf16[1,8,32,128]{3,2,1,0:T(8,128)(2,1)S(1)}, bf16[1,8,32,128]{3,2,1,0:T(8,128)(2,1)S(1)}, u32[]{:S(2)}, u32[]{:S(2)}) collective-permute-start(bf16[1,8,32,128]{3,2,1,0:T(8,128)(2,1)S(1)} %maximum_bitcast_fusion.refs_1_), channel_id=1, source_target_pairs={{0,2},{1,3},{2,0},{3,1},{4,6},{5,7},{6,4},{7,5},{8,10},{9,11},{10,... | collective-permute-start | bytes 196616 | tf_op jit(solution)/shard_map/ppermute | solution.py:317
  18.8 13.1 %collective-permute-start.18 = (bf16[1,16,32,128]{3,2,1,0:T(8,128)(2,1)S(1)}, bf16[1,16,32,128]{3,2,1,0:T(8,128)(2,1)S(1)}, u32[]{:S(2)}, u32[]{:S(2)}) collective-permute-start(bf16[1,16,32,128]{3,2,1,0:T(8,128)(2,1)S(1)} %get-tuple-element.54), channel_id=1, source_target_pairs={{0,4},{1,5},{2,6},{3,7},{4,0},{5,1},{6,2},{7,3},{8,12},{9,13},{10,... | collective-permute-start | bytes 393224 | tf_op jit(solution)/shard_map/ppermute | solution.py:317
  21.2 13.1 %collective-permute-start = (bf16[1,16,32,128]{3,2,1,0:T(8,128)(2,1)S(1)}, bf16[1,16,32,128]{3,2,1,0:T(8,128)(2,1)S(1)}, u32[]{:S(2)}, u32[]{:S(2)}) collective-permute-start(bf16[1,16,32,128]{3,2,1,0:T(8,128)(2,1)S(1)} %get-tuple-element.37.refs_0_), channel_id=1, source_target_pairs={{0,4},{1,5},{2,6},{3,7},{4,0},{5,1},{6,2},{7,3},{8,12},{9,13},{10,... | collective-permute-start | bytes 393224 | tf_op jit(solution)/shard_map/ppermute | solution.py:317
  21.8 18.2 %collective-permute-start.1 = (bf16[1,16,32,128]{3,2,1,0:T(8,128)(2,1)S(1)}, bf16[1,16,32,128]{3,2,1,0:T(8,128)(2,1)S(1)}, u32[]{:S(2)}, u32[]{:S(2)}) collective-permute-start(bf16[1,16,32,128]{3,2,1,0:T(8,128)(2,1)S(1)} %get-tuple-element.38.refs_5_), channel_id=1, source_target_pairs={{0,2},{1,3},{2,0},{3,1},{4,6},{5,7},{6,4},{7,5},{8,10},{9,11},{10,... | collective-permute-start | bytes 393224 | tf_op jit(solution)/shard_map/ppermute | solution.py:317
  24.1 16.0 %collective-permute-start.2 = (bf16[1,16,32,128]{3,2,1,0:T(8,128)(2,1)S(1)}, bf16[1,16,32,128]{3,2,1,0:T(8,128)(2,1)S(1)}, u32[]{:S(2)}, u32[]{:S(2)}) collective-permute-start(bf16[1,16,32,128]{3,2,1,0:T(8,128)(2,1)S(1)} %get-tuple-element.39.refs_4_), channel_id=1, source_target_pairs={{0,1},{1,0},{2,3},{3,2},{4,5},{5,4},{6,7},{7,6},{8,9},{9,8},{10,11... | collective-permute-start | bytes 393224 | tf_op jit(solution)/shard_map/ppermute | solution.py:317
  26.3 28.9 %collective-permute-start.10 = (bf16[4,8,32,128]{3,2,1,0:T(8,128)(2,1)S(1)}, bf16[4,8,32,128]{3,2,1,0:T(8,128)(2,1)S(1)}, u32[]{:S(2)}, u32[]{:S(2)}) collective-permute-start(bf16[4,8,32,128]{3,2,1,0:T(8,128)(2,1)S(1)} %collect_blocks.1.refs_1_), channel_id=1, source_target_pairs={{0,1},{1,0},{2,3},{3,2},{4,5},{5,4},{6,7},{7,6},{8,9},{9,8},{10,11... | collective-permute-start | bytes 786440 | tf_op jit(solution)/shard_map/ppermute | solution.py:317
  31.9 10.9 %collective-permute-start.3 = (bf16[1,16,32,128]{3,2,1,0:T(8,128)(2,1)S(1)}, bf16[1,16,32,128]{3,2,1,0:T(8,128)(2,1)S(1)}, u32[]{:S(2)}, u32[]{:S(2)}) collective-permute-start(bf16[1,16,32,128]{3,2,1,0:T(8,128)(2,1)S(1)} %get-tuple-element.40.refs_1_), channel_id=1, source_target_pairs={{0,5},{1,4},{2,7},{3,6},{4,1},{5,0},{6,3},{7,2},{8,13},{9,12},{10,... | collective-permute-start | bytes 393224 | tf_op jit(solution)/shard_map/ppermute | solution.py:317
  34.3 9.7 %collective-permute-start.4 = (bf16[1,16,32,128]{3,2,1,0:T(8,128)(2,1)S(1)}, bf16[1,16,32,128]{3,2,1,0:T(8,128)(2,1)S(1)}, u32[]{:S(2)}, u32[]{:S(2)}) collective-permute-start(bf16[1,16,32,128]{3,2,1,0:T(8,128)(2,1)S(1)} %get-tuple-element.41.refs_2_), channel_id=1, source_target_pairs={{0,6},{1,7},{2,4},{3,5},{4,2},{5,3},{6,0},{7,1},{8,14},{9,15},{10,... | collective-permute-start | bytes 393224 | tf_op jit(solution)/shard_map/ppermute | solution.py:317
  40.0 10.2 %collective-permute-start.5 = (bf16[1,16,32,128]{3,2,1,0:T(8,128)(2,1)S(1)}, bf16[1,16,32,128]{3,2,1,0:T(8,128)(2,1)S(1)}, u32[]{:S(2)}, u32[]{:S(2)}) collective-permute-start(bf16[1,16,32,128]{3,2,1,0:T(8,128)(2,1)S(1)} %get-tuple-element.42.refs_6_), channel_id=1, source_target_pairs={{0,3},{1,2},{2,1},{3,0},{4,7},{5,6},{6,5},{7,4},{8,11},{9,10},{10,... | collective-permute-start | bytes 393224 | tf_op jit(solution)/shard_map/ppermute | solution.py:317
  40.0 11.0 %collective-permute-start.6 = (bf16[1,16,32,128]{3,2,1,0:T(8,128)(2,1)S(1)}, bf16[1,16,32,128]{3,2,1,0:T(8,128)(2,1)S(1)}, u32[]{:S(2)}, u32[]{:S(2)}) collective-permute-start(bf16[1,16,32,128]{3,2,1,0:T(8,128)(2,1)S(1)} %get-tuple-element.43.refs_3_), channel_id=1, source_target_pairs={{0,7},{1,6},{2,5},{3,4},{4,3},{5,2},{6,1},{7,0},{8,15},{9,14},{10,... | collective-permute-start | bytes 393224 | tf_op jit(solution)/shard_map/ppermute | solution.py:317
  42.8 20.5 %collective-permute-start.19 = (bf16[1,16,32,128]{3,2,1,0:T(8,128)(2,1)S(1)}, bf16[1,16,32,128]{3,2,1,0:T(8,128)(2,1)S(1)}, u32[]{:S(2)}, u32[]{:S(2)}) collective-permute-start(bf16[1,16,32,128]{3,2,1,0:T(8,128)(2,1)S(1)} %get-tuple-element.55), channel_id=1, source_target_pairs={{0,2},{1,3},{2,0},{3,1},{4,6},{5,7},{6,4},{7,5},{8,10},{9,11},{10,... | collective-permute-start | bytes 393224 | tf_op jit(solution)/shard_map/ppermute | solution.py:317
  44.0 27.1 %collective-permute-start.20 = (bf16[1,16,32,128]{3,2,1,0:T(8,128)(2,1)S(1)}, bf16[1,16,32,128]{3,2,1,0:T(8,128)(2,1)S(1)}, u32[]{:S(2)}, u32[]{:S(2)}) collective-permute-start(bf16[1,16,32,128]{3,2,1,0:T(8,128)(2,1)S(1)} %get-tuple-element.56), channel_id=1, source_target_pairs={{0,1},{1,0},{2,3},{3,2},{4,5},{5,4},{6,7},{7,6},{8,9},{9,8},{10,11... | collective-permute-start | bytes 393224 | tf_op jit(solution)/shard_map/ppermute | solution.py:317
  50.2 20.9 %collective-permute-start.21 = (bf16[1,16,32,128]{3,2,1,0:T(8,128)(2,1)S(1)}, bf16[1,16,32,128]{3,2,1,0:T(8,128)(2,1)S(1)}, u32[]{:S(2)}, u32[]{:S(2)}) collective-permute-start(bf16[1,16,32,128]{3,2,1,0:T(8,128)(2,1)S(1)} %get-tuple-element.57), channel_id=1, source_target_pairs={{0,5},{1,4},{2,7},{3,6},{4,1},{5,0},{6,3},{7,2},{8,13},{9,12},{10,... | collective-permute-start | bytes 393224 | tf_op jit(solution)/shard_map/ppermute | solution.py:317
  51.0 21.6 %collective-permute-start.22 = (bf16[1,16,32,128]{3,2,1,0:T(8,128)(2,1)S(1)}, bf16[1,16,32,128]{3,2,1,0:T(8,128)(2,1)S(1)}, u32[]{:S(2)}, u32[]{:S(2)}) collective-permute-start(bf16[1,16,32,128]{3,2,1,0:T(8,128)(2,1)S(1)} %get-tuple-element.58), channel_id=1, source_target_pairs={{0,6},{1,7},{2,4},{3,5},{4,2},{5,3},{6,0},{7,1},{8,14},{9,15},{10,... | collective-permute-start | bytes 393224 | tf_op jit(solution)/shard_map/ppermute | solution.py:317
  55.2 18.9 %collective-permute-start.24 = (bf16[1,16,32,128]{3,2,1,0:T(8,128)(2,1)S(1)}, bf16[1,16,32,128]{3,2,1,0:T(8,128)(2,1)S(1)}, u32[]{:S(2)}, u32[]{:S(2)}) collective-permute-start(bf16[1,16,32,128]{3,2,1,0:T(8,128)(2,1)S(1)} %get-tuple-element.60), channel_id=1, source_target_pairs={{0,7},{1,6},{2,5},{3,4},{4,3},{5,2},{6,1},{7,0},{8,15},{9,14},{10,... | collective-permute-start | bytes 393224 | tf_op jit(solution)/shard_map/ppermute | solution.py:317
  63.3 15.6 %collective-permute-start.23 = (bf16[1,16,32,128]{3,2,1,0:T(8,128)(2,1)S(1)}, bf16[1,16,32,128]{3,2,1,0:T(8,128)(2,1)S(1)}, u32[]{:S(2)}, u32[]{:S(2)}) collective-permute-start(bf16[1,16,32,128]{3,2,1,0:T(8,128)(2,1)S(1)} %send_blocks.5), channel_id=1, source_target_pairs={{0,3},{1,2},{2,1},{3,0},{4,7},{5,6},{6,5},{7,4},{8,11},{9,10},{10,... | collective-permute-start | bytes 393224 | tf_op jit(solution)/shard_map/ppermute | solution.py:317
  71.1 16.7 %collective-permute-start.11 = (bf16[2,32,1024]{2,1,0:T(8,128)(2,1)S(1)}, bf16[2,32,1024]{2,1,0:T(8,128)(2,1)S(1)}, u32[]{:S(2)}, u32[]{:S(2)}) collective-permute-start(bf16[2,32,1024]{2,1,0:T(8,128)(2,1)S(1)} %get-tuple-element.47), channel_id=1, source_target_pairs={{0,2},{1,3},{2,0},{3,1},{4,6},{5,7},{6,4},{7,5},{8,10},{9,11},{10,... | collective-permute-start | bytes 393224 | tf_op jit(solution)/shard_map/ppermute | solution.py:317
  71.1 16.8 %collective-permute-start.12 = (bf16[2,32,1024]{2,1,0:T(8,128)(2,1)S(1)}, bf16[2,32,1024]{2,1,0:T(8,128)(2,1)S(1)}, u32[]{:S(2)}, u32[]{:S(2)}) collective-permute-start(bf16[2,32,1024]{2,1,0:T(8,128)(2,1)S(1)} %get-tuple-element.48), channel_id=1, source_target_pairs={{0,4},{1,5},{2,6},{3,7},{4,0},{5,1},{6,2},{7,3},{8,12},{9,13},{10,... | collective-permute-start | bytes 393224 | tf_op jit(solution)/shard_map/ppermute | solution.py:317
  72.6 15.4 %collective-permute-start.13 = (bf16[2,32,1024]{2,1,0:T(8,128)(2,1)S(1)}, bf16[2,32,1024]{2,1,0:T(8,128)(2,1)S(1)}, u32[]{:S(2)}, u32[]{:S(2)}) collective-permute-start(bf16[2,32,1024]{2,1,0:T(8,128)(2,1)S(1)} %get-tuple-element.49), channel_id=1, source_target_pairs={{0,5},{1,4},{2,7},{3,6},{4,1},{5,0},{6,3},{7,2},{8,13},{9,12},{10,... | collective-permute-start | bytes 393224 | tf_op jit(solution)/shard_map/ppermute | solution.py:317
  74.1 17.3 %collective-permute-start.14 = (bf16[2,32,1024]{2,1,0:T(8,128)(2,1)S(1)}, bf16[2,32,1024]{2,1,0:T(8,128)(2,1)S(1)}, u32[]{:S(2)}, u32[]{:S(2)}) collective-permute-start(bf16[2,32,1024]{2,1,0:T(8,128)(2,1)S(1)} %get-tuple-element.50), channel_id=1, source_target_pairs={{0,6},{1,7},{2,4},{3,5},{4,2},{5,3},{6,0},{7,1},{8,14},{9,15},{10,... | collective-permute-start | bytes 393224 | tf_op jit(solution)/shard_map/ppermute | solution.py:317
  78.9 12.7 %collective-permute-start.15 = (bf16[2,32,1024]{2,1,0:T(8,128)(2,1)S(1)}, bf16[2,32,1024]{2,1,0:T(8,128)(2,1)S(1)}, u32[]{:S(2)}, u32[]{:S(2)}) collective-permute-start(bf16[2,32,1024]{2,1,0:T(8,128)(2,1)S(1)} %get-tuple-element.51), channel_id=1, source_target_pairs={{0,7},{1,6},{2,5},{3,4},{4,3},{5,2},{6,1},{7,0},{8,15},{9,14},{10,... | collective-permute-start | bytes 393224 | tf_op jit(solution)/shard_map/ppermute | solution.py:317
  81.1 31.0 %copy-start.3 = (bf16[8,512,512]{2,1,0:T(8,128)(2,1)S(1)}, bf16[8,512,512]{2,1,0:T(8,128)(2,1)}, u32[]{:S(2)}) copy-start(bf16[8,512,512]{2,1,0:T(8,128)(2,1)} %constant.20.clone.refs_17_) | copy-start | bytes 12582916
  87.8 7.4 %collective-permute-start.16 = (bf16[2,32,1024]{2,1,0:T(8,128)(2,1)S(1)}, bf16[2,32,1024]{2,1,0:T(8,128)(2,1)S(1)}, u32[]{:S(2)}, u32[]{:S(2)}) collective-permute-start(bf16[2,32,1024]{2,1,0:T(8,128)(2,1)S(1)} %get-tuple-element.52), channel_id=1, source_target_pairs={{0,3},{1,2},{2,1},{3,0},{4,7},{5,6},{6,5},{7,4},{8,11},{9,10},{10,... | collective-permute-start | bytes 393224 | tf_op jit(solution)/shard_map/ppermute | solution.py:317
  87.9 10.5 %collective-permute-start.17 = (bf16[2,32,1024]{2,1,0:T(8,128)(2,1)S(1)}, bf16[2,32,1024]{2,1,0:T(8,128)(2,1)S(1)}, u32[]{:S(2)}, u32[]{:S(2)}) collective-permute-start(bf16[2,32,1024]{2,1,0:T(8,128)(2,1)S(1)} %get-tuple-element.53), channel_id=1, source_target_pairs={{0,1},{1,0},{2,3},{3,2},{4,5},{5,4},{6,7},{7,6},{8,9},{9,8},{10,11... | collective-permute-start | bytes 393224 | tf_op jit(solution)/shard_map/ppermute | solution.py:317
  88.0 12.0 %collective-permute-start.25 = (bf16[2,32,1024]{2,1,0:T(8,128)(2,1)S(1)}, bf16[2,32,1024]{2,1,0:T(8,128)(2,1)S(1)}, u32[]{:S(2)}, u32[]{:S(2)}) collective-permute-start(bf16[2,32,1024]{2,1,0:T(8,128)(2,1)S(1)} %get-tuple-element.62), channel_id=1, source_target_pairs={{0,2},{1,3},{2,0},{3,1},{4,6},{5,7},{6,4},{7,5},{8,10},{9,11},{10,... | collective-permute-start | bytes 393224 | tf_op jit(solution)/shard_map/ppermute | solution.py:317
  91.4 15.8 %collective-permute-start.26 = (bf16[2,32,1024]{2,1,0:T(8,128)(2,1)S(1)}, bf16[2,32,1024]{2,1,0:T(8,128)(2,1)S(1)}, u32[]{:S(2)}, u32[]{:S(2)}) collective-permute-start(bf16[2,32,1024]{2,1,0:T(8,128)(2,1)S(1)} %get-tuple-element.63), channel_id=1, source_target_pairs={{0,4},{1,5},{2,6},{3,7},{4,0},{5,1},{6,2},{7,3},{8,12},{9,13},{10,... | collective-permute-start | bytes 393224 | tf_op jit(solution)/shard_map/ppermute | solution.py:317
  91.7 18.3 %collective-permute-start.27 = (bf16[2,32,1024]{2,1,0:T(8,128)(2,1)S(1)}, bf16[2,32,1024]{2,1,0:T(8,128)(2,1)S(1)}, u32[]{:S(2)}, u32[]{:S(2)}) collective-permute-start(bf16[2,32,1024]{2,1,0:T(8,128)(2,1)S(1)} %get-tuple-element.64), channel_id=1, source_target_pairs={{0,5},{1,4},{2,7},{3,6},{4,1},{5,0},{6,3},{7,2},{8,13},{9,12},{10,... | collective-permute-start | bytes 393224 | tf_op jit(solution)/shard_map/ppermute | solution.py:317
  95.3 14.7 %collective-permute-start.28 = (bf16[2,32,1024]{2,1,0:T(8,128)(2,1)S(1)}, bf16[2,32,1024]{2,1,0:T(8,128)(2,1)S(1)}, u32[]{:S(2)}, u32[]{:S(2)}) collective-permute-start(bf16[2,32,1024]{2,1,0:T(8,128)(2,1)S(1)} %get-tuple-element.65), channel_id=1, source_target_pairs={{0,6},{1,7},{2,4},{3,5},{4,2},{5,3},{6,0},{7,1},{8,14},{9,15},{10,... | collective-permute-start | bytes 393224 | tf_op jit(solution)/shard_map/ppermute | solution.py:317
  98.4 11.6 %collective-permute-start.29 = (bf16[2,32,1024]{2,1,0:T(8,128)(2,1)S(1)}, bf16[2,32,1024]{2,1,0:T(8,128)(2,1)S(1)}, u32[]{:S(2)}, u32[]{:S(2)}) collective-permute-start(bf16[2,32,1024]{2,1,0:T(8,128)(2,1)S(1)} %get-tuple-element.66), channel_id=1, source_target_pairs={{0,7},{1,6},{2,5},{3,4},{4,3},{5,2},{6,1},{7,0},{8,15},{9,14},{10,... | collective-permute-start | bytes 393224 | tf_op jit(solution)/shard_map/ppermute | solution.py:317
  100.0 9.9 %collective-permute-start.30 = (bf16[2,32,1024]{2,1,0:T(8,128)(2,1)S(1)}, bf16[2,32,1024]{2,1,0:T(8,128)(2,1)S(1)}, u32[]{:S(2)}, u32[]{:S(2)}) collective-permute-start(bf16[2,32,1024]{2,1,0:T(8,128)(2,1)S(1)} %get-tuple-element.67), channel_id=1, source_target_pairs={{0,3},{1,2},{2,1},{3,0},{4,7},{5,6},{6,5},{7,4},{8,11},{9,10},{10,... | collective-permute-start | bytes 393224 | tf_op jit(solution)/shard_map/ppermute | solution.py:317
  107.2 5.0 %collective-permute-start.31 = (bf16[2,32,1024]{2,1,0:T(8,128)(2,1)S(1)}, bf16[2,32,1024]{2,1,0:T(8,128)(2,1)S(1)}, u32[]{:S(2)}, u32[]{:S(2)}) collective-permute-start(bf16[2,32,1024]{2,1,0:T(8,128)(2,1)S(1)} %get-tuple-element.68), channel_id=1, source_target_pairs={{0,1},{1,0},{2,3},{3,2},{4,5},{5,4},{6,7},{7,6},{8,9},{9,8},{10,11... | collective-permute-start | bytes 393224 | tf_op jit(solution)/shard_map/ppermute | solution.py:317

commit v5 on v4

--- a/solution.py
+++ b/solution.py
@@ -330,7 +330,8 @@
 
     far = count // 2
     order = list(dict.fromkeys(k for k in [0, far, 2, 1, far + 1, far + 2, *range(count)] if k < count))
-    order_back = list(dict.fromkeys(k for k in [0, 2, *range(far, count), *range(far - 1, 0, -1)] if k < count))
+    order_back = [0, 2, far, far + 1, far + 3, *range(far, count), *range(far - 1, 0, -1)]
+    order_back = list(dict.fromkeys(k for k in order_back if k < count))
 
     tiles = orbitals.reshape(1, bands, 2, all_cells // LANES, LANES).transpose(0, 3, 1, 2, 4)
     tiles = lax.optimization_barrier(tiles.reshape(all_cells // LANES, rows, LANES))

time: 116 us -> 115 us (level)
  no operation moved by 1% of the time
where the time goes in v5:
time: 115 us
  starting transfers between devices  53.4 us (46%)
  waiting for transfers between devices  28.7 us (25%)
  Pallas kernels  23 us (20%)
  blocking collectives  6.61 us (6%)
  local copies, waits for them, and re-layouts  3.06 us (3%)
    ppermute x32, starting transfers between devices, hop(): lax.ppermute(array, 'band', [(i, i ^ distance) for i in range(count)])  53.4 us
    ppermute x32, waiting for transfers between devices, hop(): lax.ppermute(array, 'band', [(i, i ^ distance) for i in range(count)])  28.7 us
    pallas_call x2, Pallas kernels, exchange(): pl.pallas_call(lambda *refs: exchange_kernel(first_plane, planes, places,...  13.4 us
    all_gather x1, blocking collectives, body(): everyone = lax.all_gather(own_values, 'kgrp', axis=0, tiled=False)  6.61 us
    pallas_call x1, Pallas kernels, line_pass(): pl.pallas_call(lambda *refs: line_kernel(factor, group_rows, count, *refs...  3.49 us
    pallas_call x3, Pallas kernels, send_blocks(): pl.pallas_call(lambda *refs: send_kernel(leads, *refs), in_specs=[pl.Bloc...  3.13 us
  transfers between devices with their start and end apart: 32, of which 11 were waited for; matrix products, arithmetic and copies ran while one was open for 0% of the time, Pallas kernels for 14%

profile of v5, /device:TPU:0, one launch (start us, length us, event | category | flops | bytes accessed | tf_op | source)
XLA Modules:
  0.0 115.1 jit_solution(1632290718943083171)
XLA Ops:
  0.0 1.6 %copy-done = bf16[1,16,2,32768]{3,2,1,0:T(2,128)(2,1)S(1)} copy-done((bf16[1,16,2,32768]{3,2,1,0:T(2,128)(2,1)S(1)}, bf16[1,16,2,32768]{3,2,1,0:T(2,128)(2,1)}, u32[]{:S(2)}) %copy-start) | copy-done | bytes 2097176
  1.6 1.4 %copy_bitcast_fusion = bf16[1,16,2,256,128]{4,2,1,3,0:T(2,128)(2,1)S(1)} fusion(bf16[1,16,2,32768]{3,2,1,0:T(2,128)(2,1)S(1)} %copy-done), kind=kLoop, calls=%fused_computation | loop fusion | bytes 4194304 | tf_op jit(solution)/shard_map/reshape | solution.py:336
  3.0 1.3 %send_blocks.3 = (bf16[1,16,32,128]{3,2,1,0:T(8,128)(2,1)S(1)}, bf16[1,16,32,128]{3,2,1,0:T(8,128)(2,1)S(1)}, bf16[1,16,32,128]{3,2,1,0:T(8,128)(2,1)S(1)}, bf16...) custom-call(s32[1]{0:T(128)} %bitcast.refs_0_, ...), custom_call_target="tpu_custom_call" | custom-call | flops 1 | bytes 1 | tf_op jit(solution)/shard_map/send_blocks/pallas_call | solution.py:237
  4.4 2.0 %pick_points.1 = bf16[4,32,128]{2,1,0:T(8,128)(2,1)S(1)} custom-call(s32[512]{0:T(512)S(1)} %copy-done.5, bf16[256,32,128]{2,1,0:T(8,128)(2,1)S(1)} %bitcast.35, bf16[1,16,32,128]{3,2,1,0:T(8,128)(2,1)S(1)} %get-tuple-element.37.refs_0_, bf16[1,16,32,128]{3,2,1,0:T(8,128)(2,1)S(1)} %get-tuple-element.40.refs_1_, ...), custom_call_target="tpu_custom_call" | custom-call | tf_op jit(solution)/shard_map/pick_points/pallas_call | solution.py:89
  6.3 6.6 %all-gather = bf16[16,32,128]{2,1,0:T(8,128)(2,1)S(1)} all-gather(bf16[4,32,128]{2,1,0:T(8,128)(2,1)S(1)} %pick_points.1), channel_id=2, replica_groups=mesh['kgrp'=4,'band'=8] {'kgrp'}, dimensions={0}, use_global_device_ids=true | all-gather | bytes 163840 | tf_op jit(solution)/shard_map/all_gather | solution.py:353
  13.1 4.1 %collective-permute-start.9 = (bf16[1,8,32,128]{3,2,1,0:T(8,128)(2,1)S(1)}, bf16[1,8,32,128]{3,2,1,0:T(8,128)(2,1)S(1)}, u32[]{:S(2)}, u32[]{:S(2)}) collective-permute-start(bf16[1,8,32,128]{3,2,1,0:T(8,128)(2,1)S(1)} %maximum_bitcast_fusion.refs_1_), channel_id=1, source_target_pairs={{0,6},{1,7},{2,4},{3,5},{4,2},{5,3},{6,0},{7,1},{8,14},{9,15},{10,... | collective-permute-start | bytes 196616 | tf_op jit(solution)/shard_map/ppermute | solution.py:317
  17.1 0.6 collective-permute-start.7
  17.8 1.0 send_blocks.4
  18.8 2.4 %collective-permute-start.18 = (bf16[1,16,32,128]{3,2,1,0:T(8,128)(2,1)S(1)}, bf16[1,16,32,128]{3,2,1,0:T(8,128)(2,1)S(1)}, u32[]{:S(2)}, u32[]{:S(2)}) collective-permute-start(bf16[1,16,32,128]{3,2,1,0:T(8,128)(2,1)S(1)} %get-tuple-element.54), channel_id=1, source_target_pairs={{0,4},{1,5},{2,6},{3,7},{4,0},{5,1},{6,2},{7,3},{8,12},{9,13},{10,... | collective-permute-start | bytes 393224 | tf_op jit(solution)/shard_map/ppermute | solution.py:317
  21.2 0.6 collective-permute-start
  21.8 1.5 %collective-permute-start.1 = (bf16[1,16,32,128]{3,2,1,0:T(8,128)(2,1)S(1)}, bf16[1,16,32,128]{3,2,1,0:T(8,128)(2,1)S(1)}, u32[]{:S(2)}, u32[]{:S(2)}) collective-permute-start(bf16[1,16,32,128]{3,2,1,0:T(8,128)(2,1)S(1)} %get-tuple-element.38.refs_5_), channel_id=1, source_target_pairs={{0,2},{1,3},{2,0},{3,1},{4,6},{5,7},{6,4},{7,5},{8,10},{9,11},{10,... | collective-permute-start | bytes 393224 | tf_op jit(solution)/shard_map/ppermute | solution.py:317
  23.3 0.8 collective-permute-done.8.refs_3_
  24.1 1.5 %collective-permute-start.2 = (bf16[1,16,32,128]{3,2,1,0:T(8,128)(2,1)S(1)}, bf16[1,16,32,128]{3,2,1,0:T(8,128)(2,1)S(1)}, u32[]{:S(2)}, u32[]{:S(2)}) collective-permute-start(bf16[1,16,32,128]{3,2,1,0:T(8,128)(2,1)S(1)} %get-tuple-element.39.refs_4_), channel_id=1, source_target_pairs={{0,1},{1,0},{2,3},{3,2},{4,5},{5,4},{6,7},{7,6},{8,9},{9,8},{10,11... | collective-permute-start | bytes 393224 | tf_op jit(solution)/shard_map/ppermute | solution.py:317
  25.6 0.7 collect_blocks.1.refs_1_
  26.3 0.6 collective-permute-start.10
  26.9 5.0 %collective-permute-done.18.refs_2_ = bf16[1,16,32,128]{3,2,1,0:T(8,128)(2,1)S(1)} collective-permute-done((bf16[1,16,32,128]{3,2,1,0:T(8,128)(2,1)S(1)}, bf16[1,16,32,128]{3,2,1,0:T(8,128)(2,1)S(1)}, u32[]{:S(2)}, u32[]{:S(2)}) %collective-permute-start.18) | collective-permute-done | bytes 131104 | tf_op jit(solution)/shard_map/ppermute | solution.py:317
  31.9 0.5 collective-permute-start.3
  32.4 1.9 %collective-permute-done.refs_2_ = bf16[1,16,32,128]{3,2,1,0:T(8,128)(2,1)S(1)} collective-permute-done((bf16[1,16,32,128]{3,2,1,0:T(8,128)(2,1)S(1)}, bf16[1,16,32,128]{3,2,1,0:T(8,128)(2,1)S(1)}, u32[]{:S(2)}, u32[]{:S(2)}) %collective-permute-start) | collective-permute-done | bytes 131104 | tf_op jit(solution)/shard_map/ppermute | solution.py:317
  34.3 5.7 %collective-permute-start.4 = (bf16[1,16,32,128]{3,2,1,0:T(8,128)(2,1)S(1)}, bf16[1,16,32,128]{3,2,1,0:T(8,128)(2,1)S(1)}, u32[]{:S(2)}, u32[]{:S(2)}) collective-permute-start(bf16[1,16,32,128]{3,2,1,0:T(8,128)(2,1)S(1)} %get-tuple-element.41.refs_2_), channel_id=1, source_target_pairs={{0,6},{1,7},{2,4},{3,5},{4,2},{5,3},{6,0},{7,1},{8,14},{9,15},{10,... | collective-permute-start | bytes 393224 | tf_op jit(solution)/shard_map/ppermute | solution.py:317
  40.0 1.2 %collective-permute-start.6 = (bf16[1,16,32,128]{3,2,1,0:T(8,128)(2,1)S(1)}, bf16[1,16,32,128]{3,2,1,0:T(8,128)(2,1)S(1)}, u32[]{:S(2)}, u32[]{:S(2)}) collective-permute-start(bf16[1,16,32,128]{3,2,1,0:T(8,128)(2,1)S(1)} %get-tuple-element.43.refs_3_), channel_id=1, source_target_pairs={{0,7},{1,6},{2,5},{3,4},{4,3},{5,2},{6,1},{7,0},{8,15},{9,14},{10,... | collective-permute-start | bytes 393224 | tf_op jit(solution)/shard_map/ppermute | solution.py:317
  41.3 1.5 %collective-permute-done.3.refs_5_ = bf16[1,16,32,128]{3,2,1,0:T(8,128)(2,1)S(1)} collective-permute-done((bf16[1,16,32,128]{3,2,1,0:T(8,128)(2,1)S(1)}, bf16[1,16,32,128]{3,2,1,0:T(8,128)(2,1)S(1)}, u32[]{:S(2)}, u32[]{:S(2)}) %collective-permute-start.3) | collective-permute-done | bytes 131104 | tf_op jit(solution)/shard_map/ppermute | solution.py:317
  42.8 0.5 collective-permute-start.19
  43.3 0.7 collective-permute-done.4.refs_6_
  44.0 2.2 %collective-permute-start.20 = (bf16[1,16,32,128]{3,2,1,0:T(8,128)(2,1)S(1)}, bf16[1,16,32,128]{3,2,1,0:T(8,128)(2,1)S(1)}, u32[]{:S(2)}, u32[]{:S(2)}) collective-permute-start(bf16[1,16,32,128]{3,2,1,0:T(8,128)(2,1)S(1)} %get-tuple-element.56), channel_id=1, source_target_pairs={{0,1},{1,0},{2,3},{3,2},{4,5},{5,4},{6,7},{7,6},{8,9},{9,8},{10,11... | collective-permute-start | bytes 393224 | tf_op jit(solution)/shard_map/ppermute | solution.py:317
  46.2 4.0 %collective-permute-done.5.refs_7_ = bf16[1,16,32,128]{3,2,1,0:T(8,128)(2,1)S(1)} collective-permute-done((bf16[1,16,32,128]{3,2,1,0:T(8,128)(2,1)S(1)}, bf16[1,16,32,128]{3,2,1,0:T(8,128)(2,1)S(1)}, u32[]{:S(2)}, u32[]{:S(2)}) %collective-permute-start.5) | collective-permute-done | bytes 131104 | tf_op jit(solution)/shard_map/ppermute | solution.py:317
  50.5 0.5 collective-permute-done.6.refs_8_
  51.0 4.2 %collective-permute-start.22 = (bf16[1,16,32,128]{3,2,1,0:T(8,128)(2,1)S(1)}, bf16[1,16,32,128]{3,2,1,0:T(8,128)(2,1)S(1)}, u32[]{:S(2)}, u32[]{:S(2)}) collective-permute-start(bf16[1,16,32,128]{3,2,1,0:T(8,128)(2,1)S(1)} %get-tuple-element.58), channel_id=1, source_target_pairs={{0,6},{1,7},{2,4},{3,5},{4,2},{5,3},{6,0},{7,1},{8,14},{9,15},{10,... | collective-permute-start | bytes 393224 | tf_op jit(solution)/shard_map/ppermute | solution.py:317
  55.4 0.3 coefficients.1
  55.8 6.7 %exchange_planes.2 = (bf16[2,32,1024]{2,1,0:T(8,128)(2,1)S(1)}, bf16[2,32,1024]{2,1,0:T(8,128)(2,1)S(1)}, bf16[2,32,1024]{2,1,0:T(8,128)(2,1)S(1)}, bf16[2,32,10...) custom-call(s32[1]{0:T(128)} %bitcast.refs_0_, ...), custom_call_target="tpu_custom_call" | custom-call | flops 1 | bytes 1 | tf_op jit(solution)/shard_map/exchange_planes/pallas_call | solution.py:181
  62.5 0.8 send_blocks.5
  63.3 7.8 %collective-permute-start.23 = (bf16[1,16,32,128]{3,2,1,0:T(8,128)(2,1)S(1)}, bf16[1,16,32,128]{3,2,1,0:T(8,128)(2,1)S(1)}, u32[]{:S(2)}, u32[]{:S(2)}) collective-permute-start(bf16[1,16,32,128]{3,2,1,0:T(8,128)(2,1)S(1)} %send_blocks.5), channel_id=1, source_target_pairs={{0,3},{1,2},{2,1},{3,0},{4,7},{5,6},{6,5},{7,4},{8,11},{9,10},{10,... | collective-permute-start | bytes 393224 | tf_op jit(solution)/shard_map/ppermute | solution.py:317
  71.1 1.5 %collective-permute-start.12 = (bf16[2,32,1024]{2,1,0:T(8,128)(2,1)S(1)}, bf16[2,32,1024]{2,1,0:T(8,128)(2,1)S(1)}, u32[]{:S(2)}, u32[]{:S(2)}) collective-permute-start(bf16[2,32,1024]{2,1,0:T(8,128)(2,1)S(1)} %get-tuple-element.48), channel_id=1, source_target_pairs={{0,4},{1,5},{2,6},{3,7},{4,0},{5,1},{6,2},{7,3},{8,12},{9,13},{10,... | collective-permute-start | bytes 393224 | tf_op jit(solution)/shard_map/ppermute | solution.py:317
  72.6 1.5 %collective-permute-start.13 = (bf16[2,32,1024]{2,1,0:T(8,128)(2,1)S(1)}, bf16[2,32,1024]{2,1,0:T(8,128)(2,1)S(1)}, u32[]{:S(2)}, u32[]{:S(2)}) collective-permute-start(bf16[2,32,1024]{2,1,0:T(8,128)(2,1)S(1)} %get-tuple-element.49), channel_id=1, source_target_pairs={{0,5},{1,4},{2,7},{3,6},{4,1},{5,0},{6,3},{7,2},{8,13},{9,12},{10,... | collective-permute-start | bytes 393224 | tf_op jit(solution)/shard_map/ppermute | solution.py:317
  74.1 2.3 %collective-permute-start.14 = (bf16[2,32,1024]{2,1,0:T(8,128)(2,1)S(1)}, bf16[2,32,1024]{2,1,0:T(8,128)(2,1)S(1)}, u32[]{:S(2)}, u32[]{:S(2)}) collective-permute-start(bf16[2,32,1024]{2,1,0:T(8,128)(2,1)S(1)} %get-tuple-element.50), channel_id=1, source_target_pairs={{0,7},{1,6},{2,5},{3,4},{4,3},{5,2},{6,1},{7,0},{8,15},{9,14},{10,... | collective-permute-start | bytes 393224 | tf_op jit(solution)/shard_map/ppermute | solution.py:317
  76.5 2.8 %collective-permute-done.23.refs_7_ = bf16[1,16,32,128]{3,2,1,0:T(8,128)(2,1)S(1)} collective-permute-done((bf16[1,16,32,128]{3,2,1,0:T(8,128)(2,1)S(1)}, bf16[1,16,32,128]{3,2,1,0:T(8,128)(2,1)S(1)}, u32[]{:S(2)}, u32[]{:S(2)}) %collective-permute-start.23) | collective-permute-done | bytes 131104 | tf_op jit(solution)/shard_map/ppermute | solution.py:317
  79.3 1.0 collective-permute-start.15
  80.2 6.7 %exchange_planes.3 = (bf16[2,32,1024]{2,1,0:T(8,128)(2,1)S(1)}, bf16[2,32,1024]{2,1,0:T(8,128)(2,1)S(1)}, bf16[2,32,1024]{2,1,0:T(8,128)(2,1)S(1)}, bf16[2,32,10...) custom-call(s32[1]{0:T(128)} %bitcast.refs_0_, ...), custom_call_target="tpu_custom_call" | custom-call | flops 1 | bytes 1 | tf_op jit(solution)/shard_map/exchange_planes/pallas_call | solution.py:181
  87.0 1.5 %collective-permute-start.17 = (bf16[2,32,1024]{2,1,0:T(8,128)(2,1)S(1)}, bf16[2,32,1024]{2,1,0:T(8,128)(2,1)S(1)}, u32[]{:S(2)}, u32[]{:S(2)}) collective-permute-start(bf16[2,32,1024]{2,1,0:T(8,128)(2,1)S(1)} %get-tuple-element.53), channel_id=1, source_target_pairs={{0,1},{1,0},{2,3},{3,2},{4,5},{5,4},{6,7},{7,6},{8,9},{9,8},{10,11... | collective-permute-start | bytes 393224 | tf_op jit(solution)/shard_map/ppermute | solution.py:317
  88.5 2.0 %collective-permute-start.25 = (bf16[2,32,1024]{2,1,0:T(8,128)(2,1)S(1)}, bf16[2,32,1024]{2,1,0:T(8,128)(2,1)S(1)}, u32[]{:S(2)}, u32[]{:S(2)}) collective-permute-start(bf16[2,32,1024]{2,1,0:T(8,128)(2,1)S(1)} %get-tuple-element.62), channel_id=1, source_target_pairs={{0,2},{1,3},{2,0},{3,1},{4,6},{5,7},{6,4},{7,5},{8,10},{9,11},{10,... | collective-permute-start | bytes 393224 | tf_op jit(solution)/shard_map/ppermute | solution.py:317
  90.5 1.5 %collective-permute-start.26 = (bf16[2,32,1024]{2,1,0:T(8,128)(2,1)S(1)}, bf16[2,32,1024]{2,1,0:T(8,128)(2,1)S(1)}, u32[]{:S(2)}, u32[]{:S(2)}) collective-permute-start(bf16[2,32,1024]{2,1,0:T(8,128)(2,1)S(1)} %get-tuple-element.63), channel_id=1, source_target_pairs={{0,4},{1,5},{2,6},{3,7},{4,0},{5,1},{6,2},{7,3},{8,12},{9,13},{10,... | collective-permute-start | bytes 393224 | tf_op jit(solution)/shard_map/ppermute | solution.py:317
  92.0 3.3 %collective-permute-start.27 = (bf16[2,32,1024]{2,1,0:T(8,128)(2,1)S(1)}, bf16[2,32,1024]{2,1,0:T(8,128)(2,1)S(1)}, u32[]{:S(2)}, u32[]{:S(2)}) collective-permute-start(bf16[2,32,1024]{2,1,0:T(8,128)(2,1)S(1)} %get-tuple-element.64), channel_id=1, source_target_pairs={{0,5},{1,4},{2,7},{3,6},{4,1},{5,0},{6,3},{7,2},{8,13},{9,12},{10,... | collective-permute-start | bytes 393224 | tf_op jit(solution)/shard_map/ppermute | solution.py:317
  95.3 1.9 %collective-permute-start.28 = (bf16[2,32,1024]{2,1,0:T(8,128)(2,1)S(1)}, bf16[2,32,1024]{2,1,0:T(8,128)(2,1)S(1)}, u32[]{:S(2)}, u32[]{:S(2)}) collective-permute-start(bf16[2,32,1024]{2,1,0:T(8,128)(2,1)S(1)} %get-tuple-element.65), channel_id=1, source_target_pairs={{0,7},{1,6},{2,5},{3,4},{4,3},{5,2},{6,1},{7,0},{8,15},{9,14},{10,... | collective-permute-start | bytes 393224 | tf_op jit(solution)/shard_map/ppermute | solution.py:317
  97.2 1.7 %collective-permute-start.29 = (bf16[2,32,1024]{2,1,0:T(8,128)(2,1)S(1)}, bf16[2,32,1024]{2,1,0:T(8,128)(2,1)S(1)}, u32[]{:S(2)}, u32[]{:S(2)}) collective-permute-start(bf16[2,32,1024]{2,1,0:T(8,128)(2,1)S(1)} %get-tuple-element.66), channel_id=1, source_target_pairs={{0,6},{1,7},{2,4},{3,5},{4,2},{5,3},{6,0},{7,1},{8,14},{9,15},{10,... | collective-permute-start | bytes 393224 | tf_op jit(solution)/shard_map/ppermute | solution.py:317
  98.9 7.7 %collective-permute-done.26 = bf16[2,32,1024]{2,1,0:T(8,128)(2,1)S(1)} collective-permute-done((bf16[2,32,1024]{2,1,0:T(8,128)(2,1)S(1)}, bf16[2,32,1024]{2,1,0:T(8,128)(2,1)S(1)}, u32[]{:S(2)}, u32[]{:S(2)}) %collective-permute-start.26) | collective-permute-done | bytes 131104 | tf_op jit(solution)/shard_map/ppermute | solution.py:317
  106.6 1.2 %collective-permute-start.31 = (bf16[2,32,1024]{2,1,0:T(8,128)(2,1)S(1)}, bf16[2,32,1024]{2,1,0:T(8,128)(2,1)S(1)}, u32[]{:S(2)}, u32[]{:S(2)}) collective-permute-start(bf16[2,32,1024]{2,1,0:T(8,128)(2,1)S(1)} %get-tuple-element.68), channel_id=1, source_target_pairs={{0,1},{1,0},{2,3},{3,2},{4,5},{5,4},{6,7},{7,6},{8,9},{9,8},{10,11... | collective-permute-start | bytes 393224 | tf_op jit(solution)/shard_map/ppermute | solution.py:317
  107.8 2.2 %collective-permute-done.27 = bf16[2,32,1024]{2,1,0:T(8,128)(2,1)S(1)} collective-permute-done((bf16[2,32,1024]{2,1,0:T(8,128)(2,1)S(1)}, bf16[2,32,1024]{2,1,0:T(8,128)(2,1)S(1)}, u32[]{:S(2)}, u32[]{:S(2)}) %collective-permute-start.27) | collective-permute-done | bytes 131104 | tf_op jit(solution)/shard_map/ppermute | solution.py:317
  110.1 1.5 %collective-permute-done.31 = bf16[2,32,1024]{2,1,0:T(8,128)(2,1)S(1)} collective-permute-done((bf16[2,32,1024]{2,1,0:T(8,128)(2,1)S(1)}, bf16[2,32,1024]{2,1,0:T(8,128)(2,1)S(1)}, u32[]{:S(2)}, u32[]{:S(2)}) %collective-permute-start.31) | collective-permute-done | bytes 131104 | tf_op jit(solution)/shard_map/ppermute | solution.py:317
  111.6 3.5 %line_pass.1 = bf16[512,8,2,128]{3,2,1,0:T(2,128)(2,1)} custom-call(s32[1]{0:T(128)} %bitcast.refs_0_, bf16[1,2,32,1024]{3,2,1,0:T(8,128)(2,1)S(1)} %bitcast.40, bf16[1,2,32,1024]{3,2,1,0:T(8,128)(2,1)S(1)} %bitcast.41, bf16[1,2,32,1024]{3,2,1,0:T(8,128)(2,1)S(1)} %bitcast.42, bf16[1,2,32,1024]{3,2,1,0:T(8,128)(2,1)S(1)} %bitcast.43, ...), custom_call_target="tpu_custom_call" | custom-call | flops 1 | bytes 1 | tf_op jit(solution)/shard_map/line_pass/pallas_call | solution.py:306
  (44 shorter events, 0.8 us)
Async XLA Ops:
  0.0 1.6 %copy-start = (bf16[1,16,2,32768]{3,2,1,0:T(2,128)(2,1)S(1)}, bf16[1,16,2,32768]{3,2,1,0:T(2,128)(2,1)}, u32[]{:S(2)}) copy-start(bf16[1,16,2,32768]{3,2,1,0:T(2,128)(2,1)} %param.7) | copy-start | bytes 6291460
  1.6 53.8 %copy-start.2 = (bf16[2,1024,1024]{2,1,0:T(8,128)(2,1)S(1)}, bf16[2,1024,1024]{2,1,0:T(8,128)(2,1)}, u32[]{:S(2)}) copy-start(bf16[2,1024,1024]{2,1,0:T(8,128)(2,1)} %constant.19.clone.refs_5_.refs_12_) | copy-start | bytes 12582916
  3.0 1.3 %copy-start.5 = (s32[512]{0:T(512)S(1)}, s32[512]{0:T(512)}, u32[]{:S(2)}) copy-start(s32[512]{0:T(512)} %points_ref.1) | copy-start | bytes 6148
  4.3 8.6 %copy-start.6 = (s32[4]{0:T(128)S(1)}, s32[4]{0:T(128)}, u32[]{:S(2)}) copy-start(s32[4]{0:T(128)} %param.9) | copy-start | bytes 52
  4.3 51.1 %copy-start.1 = (bf16[512,4096]{1,0:T(8,128)(2,1)S(1)}, bf16[512,4096]{1,0:T(8,128)(2,1)}, u32[]{:S(2)}) copy-start(bf16[512,4096]{1,0:T(8,128)(2,1)} %refs_11_.3) | copy-start | bytes 12582916
  6.3 49.1 %copy-start.4 = (bf16[256,256]{1,0:T(8,128)(2,1)S(1)}, bf16[256,256]{1,0:T(8,128)(2,1)}, u32[]{:S(2)}) copy-start(bf16[256,256]{1,0:T(8,128)(2,1)} %constant.18.clone.refs_3_.refs_13_) | copy-start | bytes 393220
  13.1 8.7 %collective-permute-start.9 = (bf16[1,8,32,128]{3,2,1,0:T(8,128)(2,1)S(1)}, bf16[1,8,32,128]{3,2,1,0:T(8,128)(2,1)S(1)}, u32[]{:S(2)}, u32[]{:S(2)}) collective-permute-start(bf16[1,8,32,128]{3,2,1,0:T(8,128)(2,1)S(1)} %maximum_bitcast_fusion.refs_1_), channel_id=1, source_target_pairs={{0,6},{1,7},{2,4},{3,5},{4,2},{5,3},{6,0},{7,1},{8,14},{9,15},{10,... | collective-permute-start | bytes 196616 | tf_op jit(solution)/shard_map/ppermute | solution.py:317
  17.1 6.9 %collective-permute-start.8 = (bf16[1,8,32,128]{3,2,1,0:T(8,128)(2,1)S(1)}, bf16[1,8,32,128]{3,2,1,0:T(8,128)(2,1)S(1)}, u32[]{:S(2)}, u32[]{:S(2)}) collective-permute-start(bf16[1,8,32,128]{3,2,1,0:T(8,128)(2,1)S(1)} %maximum_bitcast_fusion.refs_1_), channel_id=1, source_target_pairs={{0,4},{1,5},{2,6},{3,7},{4,0},{5,1},{6,2},{7,3},{8,12},{9,13},{10,... | collective-permute-start | bytes 196616 | tf_op jit(solution)/shard_map/ppermute | solution.py:317
  17.1 8.4 %collective-permute-start.7 = (bf16[1,8,32,128]{3,2,1,0:T(8,128)(2,1)S(1)}, bf16[1,8,32,128]{3,2,1,0:T(8,128)(2,1)S(1)}, u32[]{:S(2)}, u32[]{:S(2)}) collective-permute-start(bf16[1,8,32,128]{3,2,1,0:T(8,128)(2,1)S(1)} %maximum_bitcast_fusion.refs_1_), channel_id=1, source_target_pairs={{0,2},{1,3},{2,0},{3,1},{4,6},{5,7},{6,4},{7,5},{8,10},{9,11},{10,... | collective-permute-start | bytes 196616 | tf_op jit(solution)/shard_map/ppermute | solution.py:317
  18.8 13.1 %collective-permute-start.18 = (bf16[1,16,32,128]{3,2,1,0:T(8,128)(2,1)S(1)}, bf16[1,16,32,128]{3,2,1,0:T(8,128)(2,1)S(1)}, u32[]{:S(2)}, u32[]{:S(2)}) collective-permute-start(bf16[1,16,32,128]{3,2,1,0:T(8,128)(2,1)S(1)} %get-tuple-element.54), channel_id=1, source_target_pairs={{0,4},{1,5},{2,6},{3,7},{4,0},{5,1},{6,2},{7,3},{8,12},{9,13},{10,... | collective-permute-start | bytes 393224 | tf_op jit(solution)/shard_map/ppermute | solution.py:317
  21.2 13.1 %collective-permute-start = (bf16[1,16,32,128]{3,2,1,0:T(8,128)(2,1)S(1)}, bf16[1,16,32,128]{3,2,1,0:T(8,128)(2,1)S(1)}, u32[]{:S(2)}, u32[]{:S(2)}) collective-permute-start(bf16[1,16,32,128]{3,2,1,0:T(8,128)(2,1)S(1)} %get-tuple-element.37.refs_0_), channel_id=1, source_target_pairs={{0,4},{1,5},{2,6},{3,7},{4,0},{5,1},{6,2},{7,3},{8,12},{9,13},{10,... | collective-permute-start | bytes 393224 | tf_op jit(solution)/shard_map/ppermute | solution.py:317
  21.8 18.2 %collective-permute-start.1 = (bf16[1,16,32,128]{3,2,1,0:T(8,128)(2,1)S(1)}, bf16[1,16,32,128]{3,2,1,0:T(8,128)(2,1)S(1)}, u32[]{:S(2)}, u32[]{:S(2)}) collective-permute-start(bf16[1,16,32,128]{3,2,1,0:T(8,128)(2,1)S(1)} %get-tuple-element.38.refs_5_), channel_id=1, source_target_pairs={{0,2},{1,3},{2,0},{3,1},{4,6},{5,7},{6,4},{7,5},{8,10},{9,11},{10,... | collective-permute-start | bytes 393224 | tf_op jit(solution)/shard_map/ppermute | solution.py:317
  24.1 16.0 %collective-permute-start.2 = (bf16[1,16,32,128]{3,2,1,0:T(8,128)(2,1)S(1)}, bf16[1,16,32,128]{3,2,1,0:T(8,128)(2,1)S(1)}, u32[]{:S(2)}, u32[]{:S(2)}) collective-permute-start(bf16[1,16,32,128]{3,2,1,0:T(8,128)(2,1)S(1)} %get-tuple-element.39.refs_4_), channel_id=1, source_target_pairs={{0,1},{1,0},{2,3},{3,2},{4,5},{5,4},{6,7},{7,6},{8,9},{9,8},{10,11... | collective-permute-start | bytes 393224 | tf_op jit(solution)/shard_map/ppermute | solution.py:317
  26.3 28.9 %collective-permute-start.10 = (bf16[4,8,32,128]{3,2,1,0:T(8,128)(2,1)S(1)}, bf16[4,8,32,128]{3,2,1,0:T(8,128)(2,1)S(1)}, u32[]{:S(2)}, u32[]{:S(2)}) collective-permute-start(bf16[4,8,32,128]{3,2,1,0:T(8,128)(2,1)S(1)} %collect_blocks.1.refs_1_), channel_id=1, source_target_pairs={{0,1},{1,0},{2,3},{3,2},{4,5},{5,4},{6,7},{7,6},{8,9},{9,8},{10,11... | collective-permute-start | bytes 786440 | tf_op jit(solution)/shard_map/ppermute | solution.py:317
  31.9 10.9 %collective-permute-start.3 = (bf16[1,16,32,128]{3,2,1,0:T(8,128)(2,1)S(1)}, bf16[1,16,32,128]{3,2,1,0:T(8,128)(2,1)S(1)}, u32[]{:S(2)}, u32[]{:S(2)}) collective-permute-start(bf16[1,16,32,128]{3,2,1,0:T(8,128)(2,1)S(1)} %get-tuple-element.40.refs_1_), channel_id=1, source_target_pairs={{0,5},{1,4},{2,7},{3,6},{4,1},{5,0},{6,3},{7,2},{8,13},{9,12},{10,... | collective-permute-start | bytes 393224 | tf_op jit(solution)/shard_map/ppermute | solution.py:317
  34.3 9.7 %collective-permute-start.4 = (bf16[1,16,32,128]{3,2,1,0:T(8,128)(2,1)S(1)}, bf16[1,16,32,128]{3,2,1,0:T(8,128)(2,1)S(1)}, u32[]{:S(2)}, u32[]{:S(2)}) collective-permute-start(bf16[1,16,32,128]{3,2,1,0:T(8,128)(2,1)S(1)} %get-tuple-element.41.refs_2_), channel_id=1, source_target_pairs={{0,6},{1,7},{2,4},{3,5},{4,2},{5,3},{6,0},{7,1},{8,14},{9,15},{10,... | collective-permute-start | bytes 393224 | tf_op jit(solution)/shard_map/ppermute | solution.py:317
  40.0 10.2 %collective-permute-start.5 = (bf16[1,16,32,128]{3,2,1,0:T(8,128)(2,1)S(1)}, bf16[1,16,32,128]{3,2,1,0:T(8,128)(2,1)S(1)}, u32[]{:S(2)}, u32[]{:S(2)}) collective-permute-start(bf16[1,16,32,128]{3,2,1,0:T(8,128)(2,1)S(1)} %get-tuple-element.42.refs_6_), channel_id=1, source_target_pairs={{0,3},{1,2},{2,1},{3,0},{4,7},{5,6},{6,5},{7,4},{8,11},{9,10},{10,... | collective-permute-start | bytes 393224 | tf_op jit(solution)/shard_map/ppermute | solution.py:317
  40.0 11.0 %collective-permute-start.6 = (bf16[1,16,32,128]{3,2,1,0:T(8,128)(2,1)S(1)}, bf16[1,16,32,128]{3,2,1,0:T(8,128)(2,1)S(1)}, u32[]{:S(2)}, u32[]{:S(2)}) collective-permute-start(bf16[1,16,32,128]{3,2,1,0:T(8,128)(2,1)S(1)} %get-tuple-element.43.refs_3_), channel_id=1, source_target_pairs={{0,7},{1,6},{2,5},{3,4},{4,3},{5,2},{6,1},{7,0},{8,15},{9,14},{10,... | collective-permute-start | bytes 393224 | tf_op jit(solution)/shard_map/ppermute | solution.py:317
  42.8 20.5 %collective-permute-start.19 = (bf16[1,16,32,128]{3,2,1,0:T(8,128)(2,1)S(1)}, bf16[1,16,32,128]{3,2,1,0:T(8,128)(2,1)S(1)}, u32[]{:S(2)}, u32[]{:S(2)}) collective-permute-start(bf16[1,16,32,128]{3,2,1,0:T(8,128)(2,1)S(1)} %get-tuple-element.55), channel_id=1, source_target_pairs={{0,2},{1,3},{2,0},{3,1},{4,6},{5,7},{6,4},{7,5},{8,10},{9,11},{10,... | collective-permute-start | bytes 393224 | tf_op jit(solution)/shard_map/ppermute | solution.py:317
  44.0 27.1 %collective-permute-start.20 = (bf16[1,16,32,128]{3,2,1,0:T(8,128)(2,1)S(1)}, bf16[1,16,32,128]{3,2,1,0:T(8,128)(2,1)S(1)}, u32[]{:S(2)}, u32[]{:S(2)}) collective-permute-start(bf16[1,16,32,128]{3,2,1,0:T(8,128)(2,1)S(1)} %get-tuple-element.56), channel_id=1, source_target_pairs={{0,1},{1,0},{2,3},{3,2},{4,5},{5,4},{6,7},{7,6},{8,9},{9,8},{10,11... | collective-permute-start | bytes 393224 | tf_op jit(solution)/shard_map/ppermute | solution.py:317
  50.2 20.9 %collective-permute-start.21 = (bf16[1,16,32,128]{3,2,1,0:T(8,128)(2,1)S(1)}, bf16[1,16,32,128]{3,2,1,0:T(8,128)(2,1)S(1)}, u32[]{:S(2)}, u32[]{:S(2)}) collective-permute-start(bf16[1,16,32,128]{3,2,1,0:T(8,128)(2,1)S(1)} %get-tuple-element.57), channel_id=1, source_target_pairs={{0,5},{1,4},{2,7},{3,6},{4,1},{5,0},{6,3},{7,2},{8,13},{9,12},{10,... | collective-permute-start | bytes 393224 | tf_op jit(solution)/shard_map/ppermute | solution.py:317
  51.0 21.6 %collective-permute-start.22 = (bf16[1,16,32,128]{3,2,1,0:T(8,128)(2,1)S(1)}, bf16[1,16,32,128]{3,2,1,0:T(8,128)(2,1)S(1)}, u32[]{:S(2)}, u32[]{:S(2)}) collective-permute-start(bf16[1,16,32,128]{3,2,1,0:T(8,128)(2,1)S(1)} %get-tuple-element.58), channel_id=1, source_target_pairs={{0,6},{1,7},{2,4},{3,5},{4,2},{5,3},{6,0},{7,1},{8,14},{9,15},{10,... | collective-permute-start | bytes 393224 | tf_op jit(solution)/shard_map/ppermute | solution.py:317
  55.2 18.9 %collective-permute-start.24 = (bf16[1,16,32,128]{3,2,1,0:T(8,128)(2,1)S(1)}, bf16[1,16,32,128]{3,2,1,0:T(8,128)(2,1)S(1)}, u32[]{:S(2)}, u32[]{:S(2)}) collective-permute-start(bf16[1,16,32,128]{3,2,1,0:T(8,128)(2,1)S(1)} %get-tuple-element.60), channel_id=1, source_target_pairs={{0,7},{1,6},{2,5},{3,4},{4,3},{5,2},{6,1},{7,0},{8,15},{9,14},{10,... | collective-permute-start | bytes 393224 | tf_op jit(solution)/shard_map/ppermute | solution.py:317
  63.3 15.9 %collective-permute-start.23 = (bf16[1,16,32,128]{3,2,1,0:T(8,128)(2,1)S(1)}, bf16[1,16,32,128]{3,2,1,0:T(8,128)(2,1)S(1)}, u32[]{:S(2)}, u32[]{:S(2)}) collective-permute-start(bf16[1,16,32,128]{3,2,1,0:T(8,128)(2,1)S(1)} %send_blocks.5), channel_id=1, source_target_pairs={{0,3},{1,2},{2,1},{3,0},{4,7},{5,6},{6,5},{7,4},{8,11},{9,10},{10,... | collective-permute-start | bytes 393224 | tf_op jit(solution)/shard_map/ppermute | solution.py:317
  71.1 15.8 %collective-permute-start.11 = (bf16[2,32,1024]{2,1,0:T(8,128)(2,1)S(1)}, bf16[2,32,1024]{2,1,0:T(8,128)(2,1)S(1)}, u32[]{:S(2)}, u32[]{:S(2)}) collective-permute-start(bf16[2,32,1024]{2,1,0:T(8,128)(2,1)S(1)} %get-tuple-element.47), channel_id=1, source_target_pairs={{0,2},{1,3},{2,0},{3,1},{4,6},{5,7},{6,4},{7,5},{8,10},{9,11},{10,... | collective-permute-start | bytes 393224 | tf_op jit(solution)/shard_map/ppermute | solution.py:317
  71.1 15.9 %collective-permute-start.12 = (bf16[2,32,1024]{2,1,0:T(8,128)(2,1)S(1)}, bf16[2,32,1024]{2,1,0:T(8,128)(2,1)S(1)}, u32[]{:S(2)}, u32[]{:S(2)}) collective-permute-start(bf16[2,32,1024]{2,1,0:T(8,128)(2,1)S(1)} %get-tuple-element.48), channel_id=1, source_target_pairs={{0,4},{1,5},{2,6},{3,7},{4,0},{5,1},{6,2},{7,3},{8,12},{9,13},{10,... | collective-permute-start | bytes 393224 | tf_op jit(solution)/shard_map/ppermute | solution.py:317
  72.6 15.9 %collective-permute-start.13 = (bf16[2,32,1024]{2,1,0:T(8,128)(2,1)S(1)}, bf16[2,32,1024]{2,1,0:T(8,128)(2,1)S(1)}, u32[]{:S(2)}, u32[]{:S(2)}) collective-permute-start(bf16[2,32,1024]{2,1,0:T(8,128)(2,1)S(1)} %get-tuple-element.49), channel_id=1, source_target_pairs={{0,5},{1,4},{2,7},{3,6},{4,1},{5,0},{6,3},{7,2},{8,13},{9,12},{10,... | collective-permute-start | bytes 393224 | tf_op jit(solution)/shard_map/ppermute | solution.py:317
  74.1 16.4 %collective-permute-start.14 = (bf16[2,32,1024]{2,1,0:T(8,128)(2,1)S(1)}, bf16[2,32,1024]{2,1,0:T(8,128)(2,1)S(1)}, u32[]{:S(2)}, u32[]{:S(2)}) collective-permute-start(bf16[2,32,1024]{2,1,0:T(8,128)(2,1)S(1)} %get-tuple-element.50), channel_id=1, source_target_pairs={{0,7},{1,6},{2,5},{3,4},{4,3},{5,2},{6,1},{7,0},{8,15},{9,14},{10,... | collective-permute-start | bytes 393224 | tf_op jit(solution)/shard_map/ppermute | solution.py:317
  79.3 12.7 %collective-permute-start.15 = (bf16[2,32,1024]{2,1,0:T(8,128)(2,1)S(1)}, bf16[2,32,1024]{2,1,0:T(8,128)(2,1)S(1)}, u32[]{:S(2)}, u32[]{:S(2)}) collective-permute-start(bf16[2,32,1024]{2,1,0:T(8,128)(2,1)S(1)} %get-tuple-element.51), channel_id=1, source_target_pairs={{0,6},{1,7},{2,4},{3,5},{4,2},{5,3},{6,0},{7,1},{8,14},{9,15},{10,... | collective-permute-start | bytes 393224 | tf_op jit(solution)/shard_map/ppermute | solution.py:317
  80.2 31.4 %copy-start.3 = (bf16[8,512,512]{2,1,0:T(8,128)(2,1)S(1)}, bf16[8,512,512]{2,1,0:T(8,128)(2,1)}, u32[]{:S(2)}) copy-start(bf16[8,512,512]{2,1,0:T(8,128)(2,1)} %constant.20.clone.refs_17_) | copy-start | bytes 12582916
  86.9 8.4 %collective-permute-start.16 = (bf16[2,32,1024]{2,1,0:T(8,128)(2,1)S(1)}, bf16[2,32,1024]{2,1,0:T(8,128)(2,1)S(1)}, u32[]{:S(2)}, u32[]{:S(2)}) collective-permute-start(bf16[2,32,1024]{2,1,0:T(8,128)(2,1)S(1)} %get-tuple-element.52), channel_id=1, source_target_pairs={{0,3},{1,2},{2,1},{3,0},{4,7},{5,6},{6,5},{7,4},{8,11},{9,10},{10,... | collective-permute-start | bytes 393224 | tf_op jit(solution)/shard_map/ppermute | solution.py:317
  87.0 10.2 %collective-permute-start.17 = (bf16[2,32,1024]{2,1,0:T(8,128)(2,1)S(1)}, bf16[2,32,1024]{2,1,0:T(8,128)(2,1)S(1)}, u32[]{:S(2)}, u32[]{:S(2)}) collective-permute-start(bf16[2,32,1024]{2,1,0:T(8,128)(2,1)S(1)} %get-tuple-element.53), channel_id=1, source_target_pairs={{0,1},{1,0},{2,3},{3,2},{4,5},{5,4},{6,7},{7,6},{8,9},{9,8},{10,11... | collective-permute-start | bytes 393224 | tf_op jit(solution)/shard_map/ppermute | solution.py:317
  88.5 10.4 %collective-permute-start.25 = (bf16[2,32,1024]{2,1,0:T(8,128)(2,1)S(1)}, bf16[2,32,1024]{2,1,0:T(8,128)(2,1)S(1)}, u32[]{:S(2)}, u32[]{:S(2)}) collective-permute-start(bf16[2,32,1024]{2,1,0:T(8,128)(2,1)S(1)} %get-tuple-element.62), channel_id=1, source_target_pairs={{0,2},{1,3},{2,0},{3,1},{4,6},{5,7},{6,4},{7,5},{8,10},{9,11},{10,... | collective-permute-start | bytes 393224 | tf_op jit(solution)/shard_map/ppermute | solution.py:317
  90.5 16.1 %collective-permute-start.26 = (bf16[2,32,1024]{2,1,0:T(8,128)(2,1)S(1)}, bf16[2,32,1024]{2,1,0:T(8,128)(2,1)S(1)}, u32[]{:S(2)}, u32[]{:S(2)}) collective-permute-start(bf16[2,32,1024]{2,1,0:T(8,128)(2,1)S(1)} %get-tuple-element.63), channel_id=1, source_target_pairs={{0,4},{1,5},{2,6},{3,7},{4,0},{5,1},{6,2},{7,3},{8,12},{9,13},{10,... | collective-permute-start | bytes 393224 | tf_op jit(solution)/shard_map/ppermute | solution.py:317
  92.0 18.1 %collective-permute-start.27 = (bf16[2,32,1024]{2,1,0:T(8,128)(2,1)S(1)}, bf16[2,32,1024]{2,1,0:T(8,128)(2,1)S(1)}, u32[]{:S(2)}, u32[]{:S(2)}) collective-permute-start(bf16[2,32,1024]{2,1,0:T(8,128)(2,1)S(1)} %get-tuple-element.64), channel_id=1, source_target_pairs={{0,5},{1,4},{2,7},{3,6},{4,1},{5,0},{6,3},{7,2},{8,13},{9,12},{10,... | collective-permute-start | bytes 393224 | tf_op jit(solution)/shard_map/ppermute | solution.py:317
  95.3 14.8 %collective-permute-start.28 = (bf16[2,32,1024]{2,1,0:T(8,128)(2,1)S(1)}, bf16[2,32,1024]{2,1,0:T(8,128)(2,1)S(1)}, u32[]{:S(2)}, u32[]{:S(2)}) collective-permute-start(bf16[2,32,1024]{2,1,0:T(8,128)(2,1)S(1)} %get-tuple-element.65), channel_id=1, source_target_pairs={{0,7},{1,6},{2,5},{3,4},{4,3},{5,2},{6,1},{7,0},{8,15},{9,14},{10,... | collective-permute-start | bytes 393224 | tf_op jit(solution)/shard_map/ppermute | solution.py:317
  97.2 12.9 %collective-permute-start.29 = (bf16[2,32,1024]{2,1,0:T(8,128)(2,1)S(1)}, bf16[2,32,1024]{2,1,0:T(8,128)(2,1)S(1)}, u32[]{:S(2)}, u32[]{:S(2)}) collective-permute-start(bf16[2,32,1024]{2,1,0:T(8,128)(2,1)S(1)} %get-tuple-element.66), channel_id=1, source_target_pairs={{0,6},{1,7},{2,4},{3,5},{4,2},{5,3},{6,0},{7,1},{8,14},{9,15},{10,... | collective-permute-start | bytes 393224 | tf_op jit(solution)/shard_map/ppermute | solution.py:317
  98.9 11.2 %collective-permute-start.30 = (bf16[2,32,1024]{2,1,0:T(8,128)(2,1)S(1)}, bf16[2,32,1024]{2,1,0:T(8,128)(2,1)S(1)}, u32[]{:S(2)}, u32[]{:S(2)}) collective-permute-start(bf16[2,32,1024]{2,1,0:T(8,128)(2,1)S(1)} %get-tuple-element.67), channel_id=1, source_target_pairs={{0,3},{1,2},{2,1},{3,0},{4,7},{5,6},{6,5},{7,4},{8,11},{9,10},{10,... | collective-permute-start | bytes 393224 | tf_op jit(solution)/shard_map/ppermute | solution.py:317
  106.6 5.0 %collective-permute-start.31 = (bf16[2,32,1024]{2,1,0:T(8,128)(2,1)S(1)}, bf16[2,32,1024]{2,1,0:T(8,128)(2,1)S(1)}, u32[]{:S(2)}, u32[]{:S(2)}) collective-permute-start(bf16[2,32,1024]{2,1,0:T(8,128)(2,1)S(1)} %get-tuple-element.68), channel_id=1, source_target_pairs={{0,1},{1,0},{2,3},{3,2},{4,5},{5,4},{6,7},{7,6},{8,9},{9,8},{10,11... | collective-permute-start | bytes 393224 | tf_op jit(solution)/shard_map/ppermute | solution.py:317

commit v6 on v5

--- a/solution.py
+++ b/solution.py
@@ -132,6 +132,9 @@
     outs, after_ref, grid_ref, turned_ref = refs[inputs + 5 : -3], refs[-3], refs[-2], refs[-1]
     me = me_ref[0]
     after_ref[0] = me
+    for extra, (array, lead) in zip(outs[len(pairs) :], cells[len(pairs) :]):
+        extra[0] = arrays[array][lead(me)]
+    cells = cells[: len(pairs)]
     nu = coulomb_ref.shape[0]
     rows = arrays[0].shape[2]
     high = len(cells) * rows
@@ -172,7 +175,7 @@
 def exchange(me, cells, own, src, coulomb, table, turn, first_plane, planes, pairs):
     arrays, places = distinct(cells)
     rows = arrays[0].shape[2]
-    high = len(cells) * rows
+    high = len(pairs) * rows
     area = GY * GZ
     outs = 1 + max(out for out, _ in pairs)
     halves = () if pairs[0][1] is None else (2,)
@@ -181,8 +184,9 @@
     *sent, after = pl.pallas_call(
         lambda *refs: exchange_kernel(first_plane, planes, places, pairs, len(arrays), *refs),
         in_specs=[smem] + [vmem] * (len(arrays) + 5),
-        out_specs=[vmem] * outs + [smem],
+        out_specs=[vmem] * (outs + len(cells) - len(pairs)) + [smem],
         out_shape=[jax.ShapeDtypeStruct(halves + (planes, rows, area), BF16)] * outs
+        + [jax.ShapeDtypeStruct((1,) + a.shape[1:], BF16) for a, _ in cells[len(pairs) :]]
         + [jax.ShapeDtypeStruct((1,), jnp.int32)],
         scratch_shapes=[pltpu.VMEM((planes * high, area), BF16)] * 2,
         compiler_params=pltpu.CompilerParams(vmem_limit_bytes=VMEM_BYTES),
@@ -376,9 +380,11 @@
     for c in range(chunks):
         arrived = received[c]
         if c:
-            arrived.update({d: hop(block, d, count) for d, block in zip(late, blocks_for(c, late, after))})
+            arrived.update({d: hop(block, d, count) for d, block in zip(late, sent[count:])})
         here = [(arrived[k], first) if k else (blocks, lambda me, c=c: me * chunks + c) for k in order]
-        sent, after = exchange(
+        if c < chunks - 1:
+            here += [(blocks, lambda me, c=c, d=d: (me ^ d) * chunks + c + 1) for d in late]
+        sent, _ = exchange(
             device, here, own_coef, src_coef, coulomb, plane_t, turn, c * chunk_planes, chunk_planes,
             [(at, None) for at in range(count)],
         )

time: 115 us -> 115 us (level)
  waiting for transfers between devices: 28.7 us -> 31.9 us
  starting transfers between devices: 53.4 us -> 50.9 us
    ppermute x32, waiting for transfers between devices: 28.7 us -> 31.9 us  [hop(): lax.ppermute(array, 'band', [(i, i ^ distance) for i in range(count)])]
    ppermute x32, starting transfers between devices: 53.4 us -> 50.9 us  [hop(): lax.ppermute(array, 'band', [(i, i ^ distance) for i in range(count)])]
    pallas_call x3 -> x2, Pallas kernels: 3.13 us -> 2.31 us  [send_blocks(): pl.pallas_call(lambda *refs: send_kernel(leads, *refs), in_specs=[pl.Bloc...]
  transfers between devices with their start and end apart: 32 -> 32, of which waited for: 11 -> 13; matrix products, arithmetic and copies ran while one was open for 0% -> 0% of each run, Pallas kernels for 14% -> 13%
where the time goes in v6:
time: 115 us
  starting transfers between devices  50.9 us (44%)
  waiting for transfers between devices  31.9 us (28%)
  Pallas kernels  22.2 us (19%)
  blocking collectives  6.61 us (6%)
  local copies, waits for them, and re-layouts  3.06 us (3%)
    ppermute x32, starting transfers between devices, hop(): lax.ppermute(array, 'band', [(i, i ^ distance) for i in range(count)])  50.9 us
    ppermute x32, waiting for transfers between devices, hop(): lax.ppermute(array, 'band', [(i, i ^ distance) for i in range(count)])  31.9 us
    pallas_call x2, Pallas kernels, exchange(): pl.pallas_call(lambda *refs: exchange_kernel(first_plane, planes, places,...  13.4 us
    all_gather x1, blocking collectives, body(): everyone = lax.all_gather(own_values, 'kgrp', axis=0, tiled=False)  6.61 us
    pallas_call x1, Pallas kernels, line_pass(): pl.pallas_call(lambda *refs: line_kernel(factor, group_rows, count, *refs...  3.49 us
    pallas_call x2, Pallas kernels, send_blocks(): pl.pallas_call(lambda *refs: send_kernel(leads, *refs), in_specs=[pl.Bloc...  2.31 us
  transfers between devices with their start and end apart: 32, of which 13 were waited for; matrix products, arithmetic and copies ran while one was open for 0% of the time, Pallas kernels for 13%

profile of v6, /device:TPU:0, one launch (start us, length us, event | category | flops | bytes accessed | tf_op | source)
XLA Modules:
  0.0 115.0 jit_solution(2766084863552365245)
XLA Ops:
  0.0 1.6 %copy-done = bf16[1,16,2,32768]{3,2,1,0:T(2,128)(2,1)S(1)} copy-done((bf16[1,16,2,32768]{3,2,1,0:T(2,128)(2,1)S(1)}, bf16[1,16,2,32768]{3,2,1,0:T(2,128)(2,1)}, u32[]{:S(2)}) %copy-start) | copy-done | bytes 2097176
  1.6 1.4 %copy_bitcast_fusion = bf16[1,16,2,256,128]{4,2,1,3,0:T(2,128)(2,1)S(1)} fusion(bf16[1,16,2,32768]{3,2,1,0:T(2,128)(2,1)S(1)} %copy-done), kind=kLoop, calls=%fused_computation | loop fusion | bytes 4194304 | tf_op jit(solution)/shard_map/reshape | solution.py:340
  3.0 1.3 %send_blocks.2 = (bf16[1,16,32,128]{3,2,1,0:T(8,128)(2,1)S(1)}, bf16[1,16,32,128]{3,2,1,0:T(8,128)(2,1)S(1)}, bf16[1,16,32,128]{3,2,1,0:T(8,128)(2,1)S(1)}, bf16...) custom-call(s32[1]{0:T(128)} %bitcast.refs_0_, ...), custom_call_target="tpu_custom_call" | custom-call | flops 1 | bytes 1 | tf_op jit(solution)/shard_map/send_blocks/pallas_call | solution.py:241
  4.4 2.0 %pick_points.1 = bf16[4,32,128]{2,1,0:T(8,128)(2,1)S(1)} custom-call(s32[512]{0:T(512)S(1)} %copy-done.5, bf16[256,32,128]{2,1,0:T(8,128)(2,1)S(1)} %bitcast.35, bf16[1,16,32,128]{3,2,1,0:T(8,128)(2,1)S(1)} %get-tuple-element.37.refs_0_, bf16[1,16,32,128]{3,2,1,0:T(8,128)(2,1)S(1)} %get-tuple-element.40.refs_1_, ...), custom_call_target="tpu_custom_call" | custom-call | tf_op jit(solution)/shard_map/pick_points/pallas_call | solution.py:89
  6.3 6.6 %all-gather = bf16[16,32,128]{2,1,0:T(8,128)(2,1)S(1)} all-gather(bf16[4,32,128]{2,1,0:T(8,128)(2,1)S(1)} %pick_points.1), channel_id=2, replica_groups=mesh['kgrp'=4,'band'=8] {'kgrp'}, dimensions={0}, use_global_device_ids=true | all-gather | bytes 163840 | tf_op jit(solution)/shard_map/all_gather | solution.py:357
  13.1 4.1 %collective-permute-start.9 = (bf16[1,8,32,128]{3,2,1,0:T(8,128)(2,1)S(1)}, bf16[1,8,32,128]{3,2,1,0:T(8,128)(2,1)S(1)}, u32[]{:S(2)}, u32[]{:S(2)}) collective-permute-start(bf16[1,8,32,128]{3,2,1,0:T(8,128)(2,1)S(1)} %maximum_bitcast_fusion.refs_1_), channel_id=1, source_target_pairs={{0,6},{1,7},{2,4},{3,5},{4,2},{5,3},{6,0},{7,1},{8,14},{9,15},{10,... | collective-permute-start | bytes 196616 | tf_op jit(solution)/shard_map/ppermute | solution.py:321
  17.1 0.6 collective-permute-start.7
  17.8 1.0 send_blocks.3
  18.8 2.4 %collective-permute-start.18 = (bf16[1,16,32,128]{3,2,1,0:T(8,128)(2,1)S(1)}, bf16[1,16,32,128]{3,2,1,0:T(8,128)(2,1)S(1)}, u32[]{:S(2)}, u32[]{:S(2)}) collective-permute-start(bf16[1,16,32,128]{3,2,1,0:T(8,128)(2,1)S(1)} %get-tuple-element.54), channel_id=1, source_target_pairs={{0,4},{1,5},{2,6},{3,7},{4,0},{5,1},{6,2},{7,3},{8,12},{9,13},{10,... | collective-permute-start | bytes 393224 | tf_op jit(solution)/shard_map/ppermute | solution.py:321
  21.2 0.6 collective-permute-start
  21.8 1.5 %collective-permute-start.1 = (bf16[1,16,32,128]{3,2,1,0:T(8,128)(2,1)S(1)}, bf16[1,16,32,128]{3,2,1,0:T(8,128)(2,1)S(1)}, u32[]{:S(2)}, u32[]{:S(2)}) collective-permute-start(bf16[1,16,32,128]{3,2,1,0:T(8,128)(2,1)S(1)} %get-tuple-element.38.refs_5_), channel_id=1, source_target_pairs={{0,2},{1,3},{2,0},{3,1},{4,6},{5,7},{6,4},{7,5},{8,10},{9,11},{10,... | collective-permute-start | bytes 393224 | tf_op jit(solution)/shard_map/ppermute | solution.py:321
  23.3 0.8 collective-permute-done.8.refs_3_
  24.1 1.5 %collective-permute-start.2 = (bf16[1,16,32,128]{3,2,1,0:T(8,128)(2,1)S(1)}, bf16[1,16,32,128]{3,2,1,0:T(8,128)(2,1)S(1)}, u32[]{:S(2)}, u32[]{:S(2)}) collective-permute-start(bf16[1,16,32,128]{3,2,1,0:T(8,128)(2,1)S(1)} %get-tuple-element.39.refs_4_), channel_id=1, source_target_pairs={{0,1},{1,0},{2,3},{3,2},{4,5},{5,4},{6,7},{7,6},{8,9},{9,8},{10,11... | collective-permute-start | bytes 393224 | tf_op jit(solution)/shard_map/ppermute | solution.py:321
  25.6 0.7 collect_blocks.1.refs_1_
  26.3 0.6 collective-permute-start.10
  26.9 5.0 %collective-permute-done.18.refs_2_ = bf16[1,16,32,128]{3,2,1,0:T(8,128)(2,1)S(1)} collective-permute-done((bf16[1,16,32,128]{3,2,1,0:T(8,128)(2,1)S(1)}, bf16[1,16,32,128]{3,2,1,0:T(8,128)(2,1)S(1)}, u32[]{:S(2)}, u32[]{:S(2)}) %collective-permute-start.18) | collective-permute-done | bytes 131104 | tf_op jit(solution)/shard_map/ppermute | solution.py:321
  31.9 0.5 collective-permute-start.3
  32.4 1.9 %collective-permute-done.refs_2_ = bf16[1,16,32,128]{3,2,1,0:T(8,128)(2,1)S(1)} collective-permute-done((bf16[1,16,32,128]{3,2,1,0:T(8,128)(2,1)S(1)}, bf16[1,16,32,128]{3,2,1,0:T(8,128)(2,1)S(1)}, u32[]{:S(2)}, u32[]{:S(2)}) %collective-permute-start) | collective-permute-done | bytes 131104 | tf_op jit(solution)/shard_map/ppermute | solution.py:321
  34.3 5.7 %collective-permute-start.4 = (bf16[1,16,32,128]{3,2,1,0:T(8,128)(2,1)S(1)}, bf16[1,16,32,128]{3,2,1,0:T(8,128)(2,1)S(1)}, u32[]{:S(2)}, u32[]{:S(2)}) collective-permute-start(bf16[1,16,32,128]{3,2,1,0:T(8,128)(2,1)S(1)} %get-tuple-element.41.refs_2_), channel_id=1, source_target_pairs={{0,6},{1,7},{2,4},{3,5},{4,2},{5,3},{6,0},{7,1},{8,14},{9,15},{10,... | collective-permute-start | bytes 393224 | tf_op jit(solution)/shard_map/ppermute | solution.py:321
  40.0 1.2 %collective-permute-start.6 = (bf16[1,16,32,128]{3,2,1,0:T(8,128)(2,1)S(1)}, bf16[1,16,32,128]{3,2,1,0:T(8,128)(2,1)S(1)}, u32[]{:S(2)}, u32[]{:S(2)}) collective-permute-start(bf16[1,16,32,128]{3,2,1,0:T(8,128)(2,1)S(1)} %get-tuple-element.43.refs_3_), channel_id=1, source_target_pairs={{0,7},{1,6},{2,5},{3,4},{4,3},{5,2},{6,1},{7,0},{8,15},{9,14},{10,... | collective-permute-start | bytes 393224 | tf_op jit(solution)/shard_map/ppermute | solution.py:321
  41.3 1.5 %collective-permute-done.3.refs_5_ = bf16[1,16,32,128]{3,2,1,0:T(8,128)(2,1)S(1)} collective-permute-done((bf16[1,16,32,128]{3,2,1,0:T(8,128)(2,1)S(1)}, bf16[1,16,32,128]{3,2,1,0:T(8,128)(2,1)S(1)}, u32[]{:S(2)}, u32[]{:S(2)}) %collective-permute-start.3) | collective-permute-done | bytes 131104 | tf_op jit(solution)/shard_map/ppermute | solution.py:321
  42.8 0.5 collective-permute-start.19
  43.3 0.7 collective-permute-done.4.refs_6_
  44.0 2.2 %collective-permute-start.20 = (bf16[1,16,32,128]{3,2,1,0:T(8,128)(2,1)S(1)}, bf16[1,16,32,128]{3,2,1,0:T(8,128)(2,1)S(1)}, u32[]{:S(2)}, u32[]{:S(2)}) collective-permute-start(bf16[1,16,32,128]{3,2,1,0:T(8,128)(2,1)S(1)} %get-tuple-element.56), channel_id=1, source_target_pairs={{0,1},{1,0},{2,3},{3,2},{4,5},{5,4},{6,7},{7,6},{8,9},{9,8},{10,11... | collective-permute-start | bytes 393224 | tf_op jit(solution)/shard_map/ppermute | solution.py:321
  46.2 4.0 %collective-permute-done.5.refs_7_ = bf16[1,16,32,128]{3,2,1,0:T(8,128)(2,1)S(1)} collective-permute-done((bf16[1,16,32,128]{3,2,1,0:T(8,128)(2,1)S(1)}, bf16[1,16,32,128]{3,2,1,0:T(8,128)(2,1)S(1)}, u32[]{:S(2)}, u32[]{:S(2)}) %collective-permute-start.5) | collective-permute-done | bytes 131104 | tf_op jit(solution)/shard_map/ppermute | solution.py:321
  50.5 0.5 collective-permute-done.6.refs_8_
  51.0 4.2 %collective-permute-start.22 = (bf16[1,16,32,128]{3,2,1,0:T(8,128)(2,1)S(1)}, bf16[1,16,32,128]{3,2,1,0:T(8,128)(2,1)S(1)}, u32[]{:S(2)}, u32[]{:S(2)}) collective-permute-start(bf16[1,16,32,128]{3,2,1,0:T(8,128)(2,1)S(1)} %get-tuple-element.58), channel_id=1, source_target_pairs={{0,6},{1,7},{2,4},{3,5},{4,2},{5,3},{6,0},{7,1},{8,14},{9,15},{10,... | collective-permute-start | bytes 393224 | tf_op jit(solution)/shard_map/ppermute | solution.py:321
  55.4 0.3 coefficients.1
  55.8 6.7 %exchange_planes.2 = (bf16[2,32,1024]{2,1,0:T(8,128)(2,1)S(1)}, bf16[2,32,1024]{2,1,0:T(8,128)(2,1)S(1)}, bf16[2,32,1024]{2,1,0:T(8,128)(2,1)S(1)}, bf16[2,32,10...) custom-call(s32[1]{0:T(128)} %bitcast.refs_0_, ...), custom_call_target="tpu_custom_call" | custom-call | flops 1 | bytes 1 | tf_op jit(solution)/shard_map/exchange_planes/pallas_call | solution.py:184
  62.5 7.8 %collective-permute-start.23 = (bf16[1,16,32,128]{3,2,1,0:T(8,128)(2,1)S(1)}, bf16[1,16,32,128]{3,2,1,0:T(8,128)(2,1)S(1)}, u32[]{:S(2)}, u32[]{:S(2)}) collective-permute-start(bf16[1,16,32,128]{3,2,1,0:T(8,128)(2,1)S(1)} %get-tuple-element.59), channel_id=1, source_target_pairs={{0,3},{1,2},{2,1},{3,0},{4,7},{5,6},{6,5},{7,4},{8,11},{9,10},{10,... | collective-permute-start | bytes 393224 | tf_op jit(solution)/shard_map/ppermute | solution.py:321
  70.3 1.5 %collective-permute-start.12 = (bf16[2,32,1024]{2,1,0:T(8,128)(2,1)S(1)}, bf16[2,32,1024]{2,1,0:T(8,128)(2,1)S(1)}, u32[]{:S(2)}, u32[]{:S(2)}) collective-permute-start(bf16[2,32,1024]{2,1,0:T(8,128)(2,1)S(1)} %get-tuple-element.48), channel_id=1, source_target_pairs={{0,4},{1,5},{2,6},{3,7},{4,0},{5,1},{6,2},{7,3},{8,12},{9,13},{10,... | collective-permute-start | bytes 393224 | tf_op jit(solution)/shard_map/ppermute | solution.py:321
  71.7 1.5 %collective-permute-start.13 = (bf16[2,32,1024]{2,1,0:T(8,128)(2,1)S(1)}, bf16[2,32,1024]{2,1,0:T(8,128)(2,1)S(1)}, u32[]{:S(2)}, u32[]{:S(2)}) collective-permute-start(bf16[2,32,1024]{2,1,0:T(8,128)(2,1)S(1)} %get-tuple-element.49), channel_id=1, source_target_pairs={{0,5},{1,4},{2,7},{3,6},{4,1},{5,0},{6,3},{7,2},{8,13},{9,12},{10,... | collective-permute-start | bytes 393224 | tf_op jit(solution)/shard_map/ppermute | solution.py:321
  73.3 2.3 %collective-permute-start.14 = (bf16[2,32,1024]{2,1,0:T(8,128)(2,1)S(1)}, bf16[2,32,1024]{2,1,0:T(8,128)(2,1)S(1)}, u32[]{:S(2)}, u32[]{:S(2)}) collective-permute-start(bf16[2,32,1024]{2,1,0:T(8,128)(2,1)S(1)} %get-tuple-element.50), channel_id=1, source_target_pairs={{0,7},{1,6},{2,5},{3,4},{4,3},{5,2},{6,1},{7,0},{8,15},{9,14},{10,... | collective-permute-start | bytes 393224 | tf_op jit(solution)/shard_map/ppermute | solution.py:321
  75.6 3.4 %collective-permute-done.23.refs_7_ = bf16[1,16,32,128]{3,2,1,0:T(8,128)(2,1)S(1)} collective-permute-done((bf16[1,16,32,128]{3,2,1,0:T(8,128)(2,1)S(1)}, bf16[1,16,32,128]{3,2,1,0:T(8,128)(2,1)S(1)}, u32[]{:S(2)}, u32[]{:S(2)}) %collective-permute-start.23) | collective-permute-done | bytes 131104 | tf_op jit(solution)/shard_map/ppermute | solution.py:321
  79.0 6.7 %exchange_planes.3 = (bf16[2,32,1024]{2,1,0:T(8,128)(2,1)S(1)}, bf16[2,32,1024]{2,1,0:T(8,128)(2,1)S(1)}, bf16[2,32,1024]{2,1,0:T(8,128)(2,1)S(1)}, bf16[2,32,10...) custom-call(s32[1]{0:T(128)} %bitcast.refs_0_, ...), custom_call_target="tpu_custom_call" | custom-call | flops 1 | bytes 1 | tf_op jit(solution)/shard_map/exchange_planes/pallas_call | solution.py:184
  85.8 0.6 collective-permute-start.17
  86.4 1.0 collective-permute-done.13
  87.4 1.9 %collective-permute-start.25 = (bf16[2,32,1024]{2,1,0:T(8,128)(2,1)S(1)}, bf16[2,32,1024]{2,1,0:T(8,128)(2,1)S(1)}, u32[]{:S(2)}, u32[]{:S(2)}) collective-permute-start(bf16[2,32,1024]{2,1,0:T(8,128)(2,1)S(1)} %get-tuple-element.62), channel_id=1, source_target_pairs={{0,2},{1,3},{2,0},{3,1},{4,6},{5,7},{6,4},{7,5},{8,10},{9,11},{10,... | collective-permute-start | bytes 393224 | tf_op jit(solution)/shard_map/ppermute | solution.py:321
  89.3 2.4 %collective-permute-start.26 = (bf16[2,32,1024]{2,1,0:T(8,128)(2,1)S(1)}, bf16[2,32,1024]{2,1,0:T(8,128)(2,1)S(1)}, u32[]{:S(2)}, u32[]{:S(2)}) collective-permute-start(bf16[2,32,1024]{2,1,0:T(8,128)(2,1)S(1)} %get-tuple-element.63), channel_id=1, source_target_pairs={{0,4},{1,5},{2,6},{3,7},{4,0},{5,1},{6,2},{7,3},{8,12},{9,13},{10,... | collective-permute-start | bytes 393224 | tf_op jit(solution)/shard_map/ppermute | solution.py:321
  91.7 3.0 %collective-permute-start.27 = (bf16[2,32,1024]{2,1,0:T(8,128)(2,1)S(1)}, bf16[2,32,1024]{2,1,0:T(8,128)(2,1)S(1)}, u32[]{:S(2)}, u32[]{:S(2)}) collective-permute-start(bf16[2,32,1024]{2,1,0:T(8,128)(2,1)S(1)} %get-tuple-element.64), channel_id=1, source_target_pairs={{0,5},{1,4},{2,7},{3,6},{4,1},{5,0},{6,3},{7,2},{8,13},{9,12},{10,... | collective-permute-start | bytes 393224 | tf_op jit(solution)/shard_map/ppermute | solution.py:321
  94.8 2.2 %collective-permute-start.28 = (bf16[2,32,1024]{2,1,0:T(8,128)(2,1)S(1)}, bf16[2,32,1024]{2,1,0:T(8,128)(2,1)S(1)}, u32[]{:S(2)}, u32[]{:S(2)}) collective-permute-start(bf16[2,32,1024]{2,1,0:T(8,128)(2,1)S(1)} %get-tuple-element.65), channel_id=1, source_target_pairs={{0,7},{1,6},{2,5},{3,4},{4,3},{5,2},{6,1},{7,0},{8,15},{9,14},{10,... | collective-permute-start | bytes 393224 | tf_op jit(solution)/shard_map/ppermute | solution.py:321
  97.0 0.7 collective-permute-start.29
  97.7 8.8 %collective-permute-done.26 = bf16[2,32,1024]{2,1,0:T(8,128)(2,1)S(1)} collective-permute-done((bf16[2,32,1024]{2,1,0:T(8,128)(2,1)S(1)}, bf16[2,32,1024]{2,1,0:T(8,128)(2,1)S(1)}, u32[]{:S(2)}, u32[]{:S(2)}) %collective-permute-start.26) | collective-permute-done | bytes 131104 | tf_op jit(solution)/shard_map/ppermute | solution.py:321
  106.5 0.8 collective-permute-start.31
  107.3 2.2 %collective-permute-done.27 = bf16[2,32,1024]{2,1,0:T(8,128)(2,1)S(1)} collective-permute-done((bf16[2,32,1024]{2,1,0:T(8,128)(2,1)S(1)}, bf16[2,32,1024]{2,1,0:T(8,128)(2,1)S(1)}, u32[]{:S(2)}, u32[]{:S(2)}) %collective-permute-start.27) | collective-permute-done | bytes 131104 | tf_op jit(solution)/shard_map/ppermute | solution.py:321
  109.5 0.6 collective-permute-done.30
  110.1 1.4 %collective-permute-done.31 = bf16[2,32,1024]{2,1,0:T(8,128)(2,1)S(1)} collective-permute-done((bf16[2,32,1024]{2,1,0:T(8,128)(2,1)S(1)}, bf16[2,32,1024]{2,1,0:T(8,128)(2,1)S(1)}, u32[]{:S(2)}, u32[]{:S(2)}) %collective-permute-start.31) | collective-permute-done | bytes 131104 | tf_op jit(solution)/shard_map/ppermute | solution.py:321
  111.5 3.5 %line_pass.1 = bf16[512,8,2,128]{3,2,1,0:T(2,128)(2,1)} custom-call(s32[1]{0:T(128)} %bitcast.refs_0_, bf16[1,2,32,1024]{3,2,1,0:T(8,128)(2,1)S(1)} %bitcast.39, bf16[1,2,32,1024]{3,2,1,0:T(8,128)(2,1)S(1)} %bitcast.40, bf16[1,2,32,1024]{3,2,1,0:T(8,128)(2,1)S(1)} %bitcast.41, bf16[1,2,32,1024]{3,2,1,0:T(8,128)(2,1)S(1)} %bitcast.42, ...), custom_call_target="tpu_custom_call" | custom-call | flops 1 | bytes 1 | tf_op jit(solution)/shard_map/line_pass/pallas_call | solution.py:310
  (43 shorter events, 0.8 us)
Async XLA Ops:
  0.0 1.6 %copy-start = (bf16[1,16,2,32768]{3,2,1,0:T(2,128)(2,1)S(1)}, bf16[1,16,2,32768]{3,2,1,0:T(2,128)(2,1)}, u32[]{:S(2)}) copy-start(bf16[1,16,2,32768]{3,2,1,0:T(2,128)(2,1)} %param.7) | copy-start | bytes 6291460
  1.6 53.8 %copy-start.2 = (bf16[2,1024,1024]{2,1,0:T(8,128)(2,1)S(1)}, bf16[2,1024,1024]{2,1,0:T(8,128)(2,1)}, u32[]{:S(2)}) copy-start(bf16[2,1024,1024]{2,1,0:T(8,128)(2,1)} %constant.19.clone.refs_5_.refs_12_) | copy-start | bytes 12582916
  3.0 1.3 %copy-start.5 = (s32[512]{0:T(512)S(1)}, s32[512]{0:T(512)}, u32[]{:S(2)}) copy-start(s32[512]{0:T(512)} %points_ref.1) | copy-start | bytes 6148
  4.3 8.6 %copy-start.6 = (s32[4]{0:T(128)S(1)}, s32[4]{0:T(128)}, u32[]{:S(2)}) copy-start(s32[4]{0:T(128)} %param.9) | copy-start | bytes 52
  4.3 51.1 %copy-start.1 = (bf16[512,4096]{1,0:T(8,128)(2,1)S(1)}, bf16[512,4096]{1,0:T(8,128)(2,1)}, u32[]{:S(2)}) copy-start(bf16[512,4096]{1,0:T(8,128)(2,1)} %refs_11_.3) | copy-start | bytes 12582916
  6.3 49.1 %copy-start.4 = (bf16[256,256]{1,0:T(8,128)(2,1)S(1)}, bf16[256,256]{1,0:T(8,128)(2,1)}, u32[]{:S(2)}) copy-start(bf16[256,256]{1,0:T(8,128)(2,1)} %constant.18.clone.refs_3_.refs_13_) | copy-start | bytes 393220
  13.1 8.7 %collective-permute-start.9 = (bf16[1,8,32,128]{3,2,1,0:T(8,128)(2,1)S(1)}, bf16[1,8,32,128]{3,2,1,0:T(8,128)(2,1)S(1)}, u32[]{:S(2)}, u32[]{:S(2)}) collective-permute-start(bf16[1,8,32,128]{3,2,1,0:T(8,128)(2,1)S(1)} %maximum_bitcast_fusion.refs_1_), channel_id=1, source_target_pairs={{0,6},{1,7},{2,4},{3,5},{4,2},{5,3},{6,0},{7,1},{8,14},{9,15},{10,... | collective-permute-start | bytes 196616 | tf_op jit(solution)/shard_map/ppermute | solution.py:321
  17.1 6.9 %collective-permute-start.8 = (bf16[1,8,32,128]{3,2,1,0:T(8,128)(2,1)S(1)}, bf16[1,8,32,128]{3,2,1,0:T(8,128)(2,1)S(1)}, u32[]{:S(2)}, u32[]{:S(2)}) collective-permute-start(bf16[1,8,32,128]{3,2,1,0:T(8,128)(2,1)S(1)} %maximum_bitcast_fusion.refs_1_), channel_id=1, source_target_pairs={{0,4},{1,5},{2,6},{3,7},{4,0},{5,1},{6,2},{7,3},{8,12},{9,13},{10,... | collective-permute-start | bytes 196616 | tf_op jit(solution)/shard_map/ppermute | solution.py:321
  17.1 8.4 %collective-permute-start.7 = (bf16[1,8,32,128]{3,2,1,0:T(8,128)(2,1)S(1)}, bf16[1,8,32,128]{3,2,1,0:T(8,128)(2,1)S(1)}, u32[]{:S(2)}, u32[]{:S(2)}) collective-permute-start(bf16[1,8,32,128]{3,2,1,0:T(8,128)(2,1)S(1)} %maximum_bitcast_fusion.refs_1_), channel_id=1, source_target_pairs={{0,2},{1,3},{2,0},{3,1},{4,6},{5,7},{6,4},{7,5},{8,10},{9,11},{10,... | collective-permute-start | bytes 196616 | tf_op jit(solution)/shard_map/ppermute | solution.py:321
  18.8 13.1 %collective-permute-start.18 = (bf16[1,16,32,128]{3,2,1,0:T(8,128)(2,1)S(1)}, bf16[1,16,32,128]{3,2,1,0:T(8,128)(2,1)S(1)}, u32[]{:S(2)}, u32[]{:S(2)}) collective-permute-start(bf16[1,16,32,128]{3,2,1,0:T(8,128)(2,1)S(1)} %get-tuple-element.54), channel_id=1, source_target_pairs={{0,4},{1,5},{2,6},{3,7},{4,0},{5,1},{6,2},{7,3},{8,12},{9,13},{10,... | collective-permute-start | bytes 393224 | tf_op jit(solution)/shard_map/ppermute | solution.py:321
  21.2 13.1 %collective-permute-start = (bf16[1,16,32,128]{3,2,1,0:T(8,128)(2,1)S(1)}, bf16[1,16,32,128]{3,2,1,0:T(8,128)(2,1)S(1)}, u32[]{:S(2)}, u32[]{:S(2)}) collective-permute-start(bf16[1,16,32,128]{3,2,1,0:T(8,128)(2,1)S(1)} %get-tuple-element.37.refs_0_), channel_id=1, source_target_pairs={{0,4},{1,5},{2,6},{3,7},{4,0},{5,1},{6,2},{7,3},{8,12},{9,13},{10,... | collective-permute-start | bytes 393224 | tf_op jit(solution)/shard_map/ppermute | solution.py:321
  21.8 18.2 %collective-permute-start.1 = (bf16[1,16,32,128]{3,2,1,0:T(8,128)(2,1)S(1)}, bf16[1,16,32,128]{3,2,1,0:T(8,128)(2,1)S(1)}, u32[]{:S(2)}, u32[]{:S(2)}) collective-permute-start(bf16[1,16,32,128]{3,2,1,0:T(8,128)(2,1)S(1)} %get-tuple-element.38.refs_5_), channel_id=1, source_target_pairs={{0,2},{1,3},{2,0},{3,1},{4,6},{5,7},{6,4},{7,5},{8,10},{9,11},{10,... | collective-permute-start | bytes 393224 | tf_op jit(solution)/shard_map/ppermute | solution.py:321
  24.1 16.0 %collective-permute-start.2 = (bf16[1,16,32,128]{3,2,1,0:T(8,128)(2,1)S(1)}, bf16[1,16,32,128]{3,2,1,0:T(8,128)(2,1)S(1)}, u32[]{:S(2)}, u32[]{:S(2)}) collective-permute-start(bf16[1,16,32,128]{3,2,1,0:T(8,128)(2,1)S(1)} %get-tuple-element.39.refs_4_), channel_id=1, source_target_pairs={{0,1},{1,0},{2,3},{3,2},{4,5},{5,4},{6,7},{7,6},{8,9},{9,8},{10,11... | collective-permute-start | bytes 393224 | tf_op jit(solution)/shard_map/ppermute | solution.py:321
  26.3 28.9 %collective-permute-start.10 = (bf16[4,8,32,128]{3,2,1,0:T(8,128)(2,1)S(1)}, bf16[4,8,32,128]{3,2,1,0:T(8,128)(2,1)S(1)}, u32[]{:S(2)}, u32[]{:S(2)}) collective-permute-start(bf16[4,8,32,128]{3,2,1,0:T(8,128)(2,1)S(1)} %collect_blocks.1.refs_1_), channel_id=1, source_target_pairs={{0,1},{1,0},{2,3},{3,2},{4,5},{5,4},{6,7},{7,6},{8,9},{9,8},{10,11... | collective-permute-start | bytes 786440 | tf_op jit(solution)/shard_map/ppermute | solution.py:321
  31.9 10.9 %collective-permute-start.3 = (bf16[1,16,32,128]{3,2,1,0:T(8,128)(2,1)S(1)}, bf16[1,16,32,128]{3,2,1,0:T(8,128)(2,1)S(1)}, u32[]{:S(2)}, u32[]{:S(2)}) collective-permute-start(bf16[1,16,32,128]{3,2,1,0:T(8,128)(2,1)S(1)} %get-tuple-element.40.refs_1_), channel_id=1, source_target_pairs={{0,5},{1,4},{2,7},{3,6},{4,1},{5,0},{6,3},{7,2},{8,13},{9,12},{10,... | collective-permute-start | bytes 393224 | tf_op jit(solution)/shard_map/ppermute | solution.py:321
  34.3 9.7 %collective-permute-start.4 = (bf16[1,16,32,128]{3,2,1,0:T(8,128)(2,1)S(1)}, bf16[1,16,32,128]{3,2,1,0:T(8,128)(2,1)S(1)}, u32[]{:S(2)}, u32[]{:S(2)}) collective-permute-start(bf16[1,16,32,128]{3,2,1,0:T(8,128)(2,1)S(1)} %get-tuple-element.41.refs_2_), channel_id=1, source_target_pairs={{0,6},{1,7},{2,4},{3,5},{4,2},{5,3},{6,0},{7,1},{8,14},{9,15},{10,... | collective-permute-start | bytes 393224 | tf_op jit(solution)/shard_map/ppermute | solution.py:321
  40.0 10.2 %collective-permute-start.5 = (bf16[1,16,32,128]{3,2,1,0:T(8,128)(2,1)S(1)}, bf16[1,16,32,128]{3,2,1,0:T(8,128)(2,1)S(1)}, u32[]{:S(2)}, u32[]{:S(2)}) collective-permute-start(bf16[1,16,32,128]{3,2,1,0:T(8,128)(2,1)S(1)} %get-tuple-element.42.refs_6_), channel_id=1, source_target_pairs={{0,3},{1,2},{2,1},{3,0},{4,7},{5,6},{6,5},{7,4},{8,11},{9,10},{10,... | collective-permute-start | bytes 393224 | tf_op jit(solution)/shard_map/ppermute | solution.py:321
  40.0 11.0 %collective-permute-start.6 = (bf16[1,16,32,128]{3,2,1,0:T(8,128)(2,1)S(1)}, bf16[1,16,32,128]{3,2,1,0:T(8,128)(2,1)S(1)}, u32[]{:S(2)}, u32[]{:S(2)}) collective-permute-start(bf16[1,16,32,128]{3,2,1,0:T(8,128)(2,1)S(1)} %get-tuple-element.43.refs_3_), channel_id=1, source_target_pairs={{0,7},{1,6},{2,5},{3,4},{4,3},{5,2},{6,1},{7,0},{8,15},{9,14},{10,... | collective-permute-start | bytes 393224 | tf_op jit(solution)/shard_map/ppermute | solution.py:321
  42.8 19.7 %collective-permute-start.19 = (bf16[1,16,32,128]{3,2,1,0:T(8,128)(2,1)S(1)}, bf16[1,16,32,128]{3,2,1,0:T(8,128)(2,1)S(1)}, u32[]{:S(2)}, u32[]{:S(2)}) collective-permute-start(bf16[1,16,32,128]{3,2,1,0:T(8,128)(2,1)S(1)} %get-tuple-element.55), channel_id=1, source_target_pairs={{0,2},{1,3},{2,0},{3,1},{4,6},{5,7},{6,4},{7,5},{8,10},{9,11},{10,... | collective-permute-start | bytes 393224 | tf_op jit(solution)/shard_map/ppermute | solution.py:321
  44.0 26.3 %collective-permute-start.20 = (bf16[1,16,32,128]{3,2,1,0:T(8,128)(2,1)S(1)}, bf16[1,16,32,128]{3,2,1,0:T(8,128)(2,1)S(1)}, u32[]{:S(2)}, u32[]{:S(2)}) collective-permute-start(bf16[1,16,32,128]{3,2,1,0:T(8,128)(2,1)S(1)} %get-tuple-element.56), channel_id=1, source_target_pairs={{0,1},{1,0},{2,3},{3,2},{4,5},{5,4},{6,7},{7,6},{8,9},{9,8},{10,11... | collective-permute-start | bytes 393224 | tf_op jit(solution)/shard_map/ppermute | solution.py:321
  50.2 20.1 %collective-permute-start.21 = (bf16[1,16,32,128]{3,2,1,0:T(8,128)(2,1)S(1)}, bf16[1,16,32,128]{3,2,1,0:T(8,128)(2,1)S(1)}, u32[]{:S(2)}, u32[]{:S(2)}) collective-permute-start(bf16[1,16,32,128]{3,2,1,0:T(8,128)(2,1)S(1)} %get-tuple-element.57), channel_id=1, source_target_pairs={{0,5},{1,4},{2,7},{3,6},{4,1},{5,0},{6,3},{7,2},{8,13},{9,12},{10,... | collective-permute-start | bytes 393224 | tf_op jit(solution)/shard_map/ppermute | solution.py:321
  51.0 20.8 %collective-permute-start.22 = (bf16[1,16,32,128]{3,2,1,0:T(8,128)(2,1)S(1)}, bf16[1,16,32,128]{3,2,1,0:T(8,128)(2,1)S(1)}, u32[]{:S(2)}, u32[]{:S(2)}) collective-permute-start(bf16[1,16,32,128]{3,2,1,0:T(8,128)(2,1)S(1)} %get-tuple-element.58), channel_id=1, source_target_pairs={{0,6},{1,7},{2,4},{3,5},{4,2},{5,3},{6,0},{7,1},{8,14},{9,15},{10,... | collective-permute-start | bytes 393224 | tf_op jit(solution)/shard_map/ppermute | solution.py:321
  55.2 18.1 %collective-permute-start.24 = (bf16[1,16,32,128]{3,2,1,0:T(8,128)(2,1)S(1)}, bf16[1,16,32,128]{3,2,1,0:T(8,128)(2,1)S(1)}, u32[]{:S(2)}, u32[]{:S(2)}) collective-permute-start(bf16[1,16,32,128]{3,2,1,0:T(8,128)(2,1)S(1)} %get-tuple-element.60), channel_id=1, source_target_pairs={{0,7},{1,6},{2,5},{3,4},{4,3},{5,2},{6,1},{7,0},{8,15},{9,14},{10,... | collective-permute-start | bytes 393224 | tf_op jit(solution)/shard_map/ppermute | solution.py:321
  62.5 16.5 %collective-permute-start.23 = (bf16[1,16,32,128]{3,2,1,0:T(8,128)(2,1)S(1)}, bf16[1,16,32,128]{3,2,1,0:T(8,128)(2,1)S(1)}, u32[]{:S(2)}, u32[]{:S(2)}) collective-permute-start(bf16[1,16,32,128]{3,2,1,0:T(8,128)(2,1)S(1)} %get-tuple-element.59), channel_id=1, source_target_pairs={{0,3},{1,2},{2,1},{3,0},{4,7},{5,6},{6,5},{7,4},{8,11},{9,10},{10,... | collective-permute-start | bytes 393224 | tf_op jit(solution)/shard_map/ppermute | solution.py:321
  70.3 15.5 %collective-permute-start.11 = (bf16[2,32,1024]{2,1,0:T(8,128)(2,1)S(1)}, bf16[2,32,1024]{2,1,0:T(8,128)(2,1)S(1)}, u32[]{:S(2)}, u32[]{:S(2)}) collective-permute-start(bf16[2,32,1024]{2,1,0:T(8,128)(2,1)S(1)} %get-tuple-element.47), channel_id=1, source_target_pairs={{0,2},{1,3},{2,0},{3,1},{4,6},{5,7},{6,4},{7,5},{8,10},{9,11},{10,... | collective-permute-start | bytes 393224 | tf_op jit(solution)/shard_map/ppermute | solution.py:321
  70.3 15.5 %collective-permute-start.12 = (bf16[2,32,1024]{2,1,0:T(8,128)(2,1)S(1)}, bf16[2,32,1024]{2,1,0:T(8,128)(2,1)S(1)}, u32[]{:S(2)}, u32[]{:S(2)}) collective-permute-start(bf16[2,32,1024]{2,1,0:T(8,128)(2,1)S(1)} %get-tuple-element.48), channel_id=1, source_target_pairs={{0,4},{1,5},{2,6},{3,7},{4,0},{5,1},{6,2},{7,3},{8,12},{9,13},{10,... | collective-permute-start | bytes 393224 | tf_op jit(solution)/shard_map/ppermute | solution.py:321
  71.7 15.7 %collective-permute-start.13 = (bf16[2,32,1024]{2,1,0:T(8,128)(2,1)S(1)}, bf16[2,32,1024]{2,1,0:T(8,128)(2,1)S(1)}, u32[]{:S(2)}, u32[]{:S(2)}) collective-permute-start(bf16[2,32,1024]{2,1,0:T(8,128)(2,1)S(1)} %get-tuple-element.49), channel_id=1, source_target_pairs={{0,5},{1,4},{2,7},{3,6},{4,1},{5,0},{6,3},{7,2},{8,13},{9,12},{10,... | collective-permute-start | bytes 393224 | tf_op jit(solution)/shard_map/ppermute | solution.py:321
  73.3 16.0 %collective-permute-start.14 = (bf16[2,32,1024]{2,1,0:T(8,128)(2,1)S(1)}, bf16[2,32,1024]{2,1,0:T(8,128)(2,1)S(1)}, u32[]{:S(2)}, u32[]{:S(2)}) collective-permute-start(bf16[2,32,1024]{2,1,0:T(8,128)(2,1)S(1)} %get-tuple-element.50), channel_id=1, source_target_pairs={{0,7},{1,6},{2,5},{3,4},{4,3},{5,2},{6,1},{7,0},{8,15},{9,14},{10,... | collective-permute-start | bytes 393224 | tf_op jit(solution)/shard_map/ppermute | solution.py:321
  79.0 12.7 %collective-permute-start.15 = (bf16[2,32,1024]{2,1,0:T(8,128)(2,1)S(1)}, bf16[2,32,1024]{2,1,0:T(8,128)(2,1)S(1)}, u32[]{:S(2)}, u32[]{:S(2)}) collective-permute-start(bf16[2,32,1024]{2,1,0:T(8,128)(2,1)S(1)} %get-tuple-element.51), channel_id=1, source_target_pairs={{0,6},{1,7},{2,4},{3,5},{4,2},{5,3},{6,0},{7,1},{8,14},{9,15},{10,... | collective-permute-start | bytes 393224 | tf_op jit(solution)/shard_map/ppermute | solution.py:321
  79.0 32.4 %copy-start.3 = (bf16[8,512,512]{2,1,0:T(8,128)(2,1)S(1)}, bf16[8,512,512]{2,1,0:T(8,128)(2,1)}, u32[]{:S(2)}) copy-start(bf16[8,512,512]{2,1,0:T(8,128)(2,1)} %constant.20.clone.refs_17_) | copy-start | bytes 12582916
  85.7 9.0 %collective-permute-start.16 = (bf16[2,32,1024]{2,1,0:T(8,128)(2,1)S(1)}, bf16[2,32,1024]{2,1,0:T(8,128)(2,1)S(1)}, u32[]{:S(2)}, u32[]{:S(2)}) collective-permute-start(bf16[2,32,1024]{2,1,0:T(8,128)(2,1)S(1)} %get-tuple-element.52), channel_id=1, source_target_pairs={{0,3},{1,2},{2,1},{3,0},{4,7},{5,6},{6,5},{7,4},{8,11},{9,10},{10,... | collective-permute-start | bytes 393224 | tf_op jit(solution)/shard_map/ppermute | solution.py:321
  85.8 11.1 %collective-permute-start.17 = (bf16[2,32,1024]{2,1,0:T(8,128)(2,1)S(1)}, bf16[2,32,1024]{2,1,0:T(8,128)(2,1)S(1)}, u32[]{:S(2)}, u32[]{:S(2)}) collective-permute-start(bf16[2,32,1024]{2,1,0:T(8,128)(2,1)S(1)} %get-tuple-element.53), channel_id=1, source_target_pairs={{0,1},{1,0},{2,3},{3,2},{4,5},{5,4},{6,7},{7,6},{8,9},{9,8},{10,11... | collective-permute-start | bytes 393224 | tf_op jit(solution)/shard_map/ppermute | solution.py:321
  87.4 10.2 %collective-permute-start.25 = (bf16[2,32,1024]{2,1,0:T(8,128)(2,1)S(1)}, bf16[2,32,1024]{2,1,0:T(8,128)(2,1)S(1)}, u32[]{:S(2)}, u32[]{:S(2)}) collective-permute-start(bf16[2,32,1024]{2,1,0:T(8,128)(2,1)S(1)} %get-tuple-element.62), channel_id=1, source_target_pairs={{0,2},{1,3},{2,0},{3,1},{4,6},{5,7},{6,4},{7,5},{8,10},{9,11},{10,... | collective-permute-start | bytes 393224 | tf_op jit(solution)/shard_map/ppermute | solution.py:321
  89.3 17.2 %collective-permute-start.26 = (bf16[2,32,1024]{2,1,0:T(8,128)(2,1)S(1)}, bf16[2,32,1024]{2,1,0:T(8,128)(2,1)S(1)}, u32[]{:S(2)}, u32[]{:S(2)}) collective-permute-start(bf16[2,32,1024]{2,1,0:T(8,128)(2,1)S(1)} %get-tuple-element.63), channel_id=1, source_target_pairs={{0,4},{1,5},{2,6},{3,7},{4,0},{5,1},{6,2},{7,3},{8,12},{9,13},{10,... | collective-permute-start | bytes 393224 | tf_op jit(solution)/shard_map/ppermute | solution.py:321
  91.7 17.7 %collective-permute-start.27 = (bf16[2,32,1024]{2,1,0:T(8,128)(2,1)S(1)}, bf16[2,32,1024]{2,1,0:T(8,128)(2,1)S(1)}, u32[]{:S(2)}, u32[]{:S(2)}) collective-permute-start(bf16[2,32,1024]{2,1,0:T(8,128)(2,1)S(1)} %get-tuple-element.64), channel_id=1, source_target_pairs={{0,5},{1,4},{2,7},{3,6},{4,1},{5,0},{6,3},{7,2},{8,13},{9,12},{10,... | collective-permute-start | bytes 393224 | tf_op jit(solution)/shard_map/ppermute | solution.py:321
  94.8 14.7 %collective-permute-start.28 = (bf16[2,32,1024]{2,1,0:T(8,128)(2,1)S(1)}, bf16[2,32,1024]{2,1,0:T(8,128)(2,1)S(1)}, u32[]{:S(2)}, u32[]{:S(2)}) collective-permute-start(bf16[2,32,1024]{2,1,0:T(8,128)(2,1)S(1)} %get-tuple-element.65), channel_id=1, source_target_pairs={{0,7},{1,6},{2,5},{3,4},{4,3},{5,2},{6,1},{7,0},{8,15},{9,14},{10,... | collective-permute-start | bytes 393224 | tf_op jit(solution)/shard_map/ppermute | solution.py:321
  97.0 12.5 %collective-permute-start.29 = (bf16[2,32,1024]{2,1,0:T(8,128)(2,1)S(1)}, bf16[2,32,1024]{2,1,0:T(8,128)(2,1)S(1)}, u32[]{:S(2)}, u32[]{:S(2)}) collective-permute-start(bf16[2,32,1024]{2,1,0:T(8,128)(2,1)S(1)} %get-tuple-element.66), channel_id=1, source_target_pairs={{0,6},{1,7},{2,4},{3,5},{4,2},{5,3},{6,0},{7,1},{8,14},{9,15},{10,... | collective-permute-start | bytes 393224 | tf_op jit(solution)/shard_map/ppermute | solution.py:321
  97.7 12.4 %collective-permute-start.30 = (bf16[2,32,1024]{2,1,0:T(8,128)(2,1)S(1)}, bf16[2,32,1024]{2,1,0:T(8,128)(2,1)S(1)}, u32[]{:S(2)}, u32[]{:S(2)}) collective-permute-start(bf16[2,32,1024]{2,1,0:T(8,128)(2,1)S(1)} %get-tuple-element.67), channel_id=1, source_target_pairs={{0,3},{1,2},{2,1},{3,0},{4,7},{5,6},{6,5},{7,4},{8,11},{9,10},{10,... | collective-permute-start | bytes 393224 | tf_op jit(solution)/shard_map/ppermute | solution.py:321
  106.5 5.0 %collective-permute-start.31 = (bf16[2,32,1024]{2,1,0:T(8,128)(2,1)S(1)}, bf16[2,32,1024]{2,1,0:T(8,128)(2,1)S(1)}, u32[]{:S(2)}, u32[]{:S(2)}) collective-permute-start(bf16[2,32,1024]{2,1,0:T(8,128)(2,1)S(1)} %get-tuple-element.68), channel_id=1, source_target_pairs={{0,1},{1,0},{2,3},{3,2},{4,5},{5,4},{6,7},{7,6},{8,9},{9,8},{10,11... | collective-permute-start | bytes 393224 | tf_op jit(solution)/shard_map/ppermute | solution.py:321
